TPU v7x, 32 devices: a whole 2x2x4 slice. The times are simulated.
32 devices in a mesh: tm: 32 (over z, y, x, core).
Axes of the slice: x: 2, y: 2, z: 4, core: 2. Of those that a mesh axis runs over, the one named last changes fastest.
Arguments:
- inputs: float32 [16, 2048, 512], P(None, 'tm'), may hold values from -39 to 39
- lengths: int32 [16], replicated, may hold values from 1024 to 2048, as said below
- cotangent: float32 [16, 2048, 512], P(None, 'tm'), may hold values from -6 to 6
- bn_gain: float32 [2, 512], replicated, may hold values from 0.5 to 1.5
- bn_bias: float32 [2, 512], replicated, may hold values from -2.5 to 2.5
- running: float32 [2, 2, 512], replicated, may hold values from 0.5 to 1.5
- w_in: bfloat16 [2, 512, 512], replicated, may hold values from -0.25 to 0.25
- nu_log: float32 [2, 256], replicated, as said below
- phase: float32 [2, 256], replicated, may hold values from 0.01 to 3
- w_out: bfloat16 [2, 512, 512], replicated, may hold values from -0.25 to 0.25
- skip: float32 [2, 512], replicated, may hold values from -3 to 3
- w_glu: bfloat16 [2, 512, 1024], replicated, may hold values from -0.25 to 0.25
Outputs:
- output: float32 [16, 2048, 512], P(None, 'tm')
- grad_x: float32 [16, 2048, 512], P(None, 'tm')
- g_bn_gain: float32 [2, 512], replicated
- g_bn_bias: float32 [2, 512], replicated
- g_w_in: float32 [2, 512, 512], replicated
- g_nu_log: float32 [2, 256], replicated
- g_phase: float32 [2, 256], replicated
- g_w_out: float32 [2, 512, 512], replicated
- g_skip: float32 [2, 512], replicated
- g_w_glu: float32 [2, 512, 1024], replicated
- running_out: float32 [2, 2, 512], replicated
Inputs may be any that keep to these rules, and one draw needn't show every extreme that they name: `lengths`: each sequence's valid steps come first; in every draw one sequence has exactly 2048 valid steps. exp(nu_log) lies between 0.1 / 2048 and 1 / 30.
All inputs are finite; a program needn't handle non-finite values.
Results may differ from a plain program's by a relative error of at most 0.015.
Values sent between devices are 32-bit elements; how exact they have to be, the bound alone decides.
No kernel may reach another device: no remote copies, remote signals or barrier semaphores. Data moves between devices by JAX's collectives and lax.ppermute only.
A program may use at most 192 MiB of HBM per device.

v0:
```python
import functools

import jax
import jax.numpy as jnp
from jax import lax
from jax.experimental import pallas as pl
from jax.experimental.pallas import tpu as pltpu
from jax.sharding import PartitionSpec as P

norm_epsilon = 1e-05
momentum = 0.1
inverse_root_two = 0.7071067811865476
density_scale = 0.3989422804014327
F32, BF16 = jnp.float32, jnp.bfloat16
LANES = 128
MIB = 1 << 20


def dot(left, right):
    return jnp.dot(left, right, preferred_element_type=F32)


def dot_nt(left, right):
    return lax.dot_general(left, right, (((1,), (1,)), ((), ())), preferred_element_type=F32)


def run(body, outs, operands, scalars=(), scratch=(), limit=40):
    vmem = pl.BlockSpec(memory_space=pltpu.VMEM)
    smem = pl.BlockSpec(memory_space=pltpu.SMEM)
    return pl.pallas_call(
        body,
        out_shape=[jax.ShapeDtypeStruct(shape, dtype) for shape, dtype in outs],
        in_specs=[smem] * len(scalars) + [vmem] * len(operands),
        out_specs=[vmem] * len(outs),
        scratch_shapes=list(scratch),
        compiler_params=pltpu.CompilerParams(vmem_limit_bytes=limit * MIB),
    )(*scalars, *operands)


def radices(count):
    out = []
    while count > 1:
        radix = 2 if not out or count % 4 else 4
        out.append(radix)
        count //= radix
    return out


def stages(count):
    stride, out = 1, []
    for radix in radices(count):
        out.append((radix, stride))
        stride *= radix
    return out


def swap(value, count, stride, mask):
    return lax.ppermute(value, "tm", [(i, i ^ (stride * mask)) for i in range(count)])


def rows_to_tile(first, second):
    pieces = [
        row[:, j : j + LANES] for row in (first, second) for j in range(0, row.shape[1], LANES)
    ]
    return jnp.concatenate(pieces, axis=0)


def tile_to_rows(tile):
    half = tile.shape[0] // 2
    return [
        jnp.concatenate([tile[base + j : base + j + 1, :] for j in range(half)], axis=1)
        for base in (0, half)
    ]


def spread(ref, first, second):
    ref[...] = jnp.broadcast_to(rows_to_tile(first, second)[None], ref.shape)


def gathered(ref):
    return tile_to_rows(jnp.sum(ref[...], axis=0))


def everywhere(tiles):
    return lax.all_to_all(tiles, "tm", 0, 0)


def mul(ar, ai, br, bi):
    return ar * br - ai * bi, ar * bi + ai * br


def members(refs, place, buffer):
    for offset, ref in enumerate(refs):
        buffer[jnp.bitwise_xor(place, offset)] = ref[...]


def pass_through(buffer, factor, place, state, backward, conj):
    radix, _, width = buffer.shape
    states = width // 2
    if state is None:
        zero = jnp.zeros(buffer.shape[1:-1] + (states,), F32)
        state = (zero, zero)
    entering = state
    for member in range(radix - 1, -1, -1) if backward else range(radix):
        entering = tuple(jnp.where(place == member, s, e) for s, e in zip(state, entering))
        fr, fi = factor[member, :, :states], factor[member, :, states:]
        moved = mul(fr, -fi if conj else fi, *state)
        state = (moved[0] + buffer[member, :, :states], moved[1] + buffer[member, :, states:])
    return entering, state


def total_body(backward, conj, place_ref, *refs):
    radix = len(refs) - 3
    factor, out, buffer = refs[radix], refs[radix + 1], refs[radix + 2]
    place = place_ref[0]
    members(refs[:radix], place, buffer)
    _, (re, im) = pass_through(buffer, factor, place, None, backward, conj)
    states = re.shape[1]
    out[:, :states] = re
    out[:, states:] = im


def exchange(summary, plan, factors, places, backward, conj):
    count = lax.axis_size("tm")
    held = []
    value = summary
    for level, (radix, stride) in enumerate(plan):
        group = [value] + [swap(value, count, stride, mask) for mask in range(1, radix)]
        held.append(group)
        if level + 1 < len(plan):
            (value,) = run(
                functools.partial(total_body, backward, conj),
                [(summary.shape, F32)],
                group + [factors[level]],
                [places[level]],
                [pltpu.VMEM((radix,) + summary.shape, F32)],
                limit=8,
            )
    return held


def entry_operands(held, factors):
    return [value for group in held for value in group] + list(factors)


def entry_scratch(plan, shape):
    return [pltpu.VMEM((radix,) + shape, F32) for radix, _ in plan]


def entering_state(plan, places, refs, buffers, backward, conj):
    total = sum(radix for radix, _ in plan)
    values, factors = refs[:total], refs[total : total + len(plan)]
    start, groups = 0, []
    for radix, _ in plan:
        groups.append(values[start : start + radix])
        start += radix
    state = None
    for level in range(len(plan) - 1, -1, -1):
        members(groups[level], places[level][0], buffers[level])
        state, _ = pass_through(
            buffers[level], factors[level], places[level][0], state, backward, conj
        )
    return state


def steps(span, backward, body, start, unroll=8):
    def one(k, carry):
        return body(span - 1 - k if backward else k, carry)

    return lax.fori_loop(0, span, one, start, unroll=unroll)


def at(t, seqs):
    return pl.ds(pl.multiple_of(t * seqs, seqs), seqs)


def state_scan(v_ref, rel, lr, li, start, span, backward, keep=None):
    seqs, states = lr.shape

    def body(t, carry):
        re, im = carry
        vr, vi = v_ref[at(t, seqs), :states], v_ref[at(t, seqs), states:]
        next_re, next_im = mul(lr, li, re, im)
        live = rel > t
        re, im = jnp.where(live, next_re + vr, re), jnp.where(live, next_im + vi, im)
        if keep is not None:
            keep(t, re, im)
        return re, im

    return steps(span, backward, body, start)


def adjoint_scan(g_ref, rel, lr, li, start, span, backward, use=None, extra=()):
    seqs, states = lr.shape

    def body(t, carry):
        (re, im), kept = carry
        ar, ai = g_ref[at(t, seqs), :states] + re, g_ref[at(t, seqs), states:] + im
        live = rel > t
        if use is not None:
            kept = use(t, ar, ai, live, kept)
        next_re, next_im = mul(lr, -li, ar, ai)
        return (jnp.where(live, next_re, ar), jnp.where(live, next_im, ai)), kept

    return steps(span, backward, body, (start, extra))


def wide(ref, row, shape):
    return jnp.broadcast_to(ref[row : row + 1, :], shape)


def to_time_major(piece):
    seqs, span, width = piece.shape
    return jnp.swapaxes(piece, 0, 1).reshape(span * seqs, width)


def from_time_major(rows, seqs):
    return jnp.swapaxes(rows.reshape(-1, seqs, rows.shape[-1]), 0, 1)


def lane_tiled(column, width):
    return jnp.concatenate([column] * (width // LANES), axis=1)


def gelu_parts(y):
    cdf = 0.5 * (1.0 + lax.erf(y * inverse_root_two))
    pdf = jnp.exp(-0.5 * y * y) * density_scale
    return y * cdf, cdf + y * pdf


def sigmoid(x):
    return 1.0 / (1.0 + jnp.exp(-x))


CHUNK = 16


def prepare_body(plan, span, rel_ref, counts_ref, x_ref, decay_ref, *outs):
    sums_ref, tm_ref, mask_ref = outs[:3]
    factor_refs = outs[3:]
    seqs, _, width = x_ref.shape
    states = decay_ref.shape[-1]
    rel = jnp.broadcast_to(rel_ref[...], (seqs, LANES))
    first = jnp.zeros((seqs, width), F32)
    second = jnp.zeros((seqs, width), F32)
    for t0 in range(0, span, 8):
        piece = jnp.swapaxes(x_ref[:, t0 : t0 + 8, :], 0, 1)
        for j in range(8):
            rows = piece[j]
            mask = jnp.where(rel > t0 + j, 1.0, 0.0)
            place = slice((t0 + j) * seqs, (t0 + j + 1) * seqs)
            mask_ref[place, :] = mask
            tm_ref[place, :] = rows
            live = rows * lane_tiled(mask, width)
            first += live
            second += live * rows
    spread(sums_ref, jnp.sum(first, 0, keepdims=True), jnp.sum(second, 0, keepdims=True))
    for k in range(2):
        row = 0
        for level, (radix, stride) in enumerate(plan):
            for member in range(radix):
                count = jnp.broadcast_to(counts_ref[row], (seqs, states))
                row += 1
                power = (decay_ref[k, 0:1, :], decay_ref[k, 1:2, :])
                re, im = jnp.ones((seqs, states), F32), jnp.zeros((seqs, states), F32)
                for bit in range((span * stride).bit_length()):
                    taken = jnp.bitwise_and(count, 1 << bit) != 0
                    next_re, next_im = mul(re, im, *power)
                    re, im = jnp.where(taken, next_re, re), jnp.where(taken, next_im, im)
                    power = mul(*power, *power)
                ref = factor_refs[k * len(plan) + level]
                ref[member, :, :states] = re
                ref[member, :, states:] = im


def project_body(
    k, span, backward, tokens, rel_ref, sums_ref, x_ref, gain_ref, bias_ref, w_ref, decay_ref,
    u_ref, v_ref, stats_ref, summary_ref,
):
    seqs = rel_ref.shape[0]
    states = decay_ref.shape[-1]
    total, squares = gathered(sums_ref)
    scale = tokens[0]
    mean = total * scale
    var = squares * scale - mean * mean
    rstd = lax.rsqrt(var + norm_epsilon)
    stats_ref[0:1, :] = mean
    stats_ref[1:2, :] = var
    stats_ref[2:3, :] = rstd
    stats_ref[3:4, :] = rstd * gain_ref[k : k + 1, :]
    slope = rstd * gain_ref[k : k + 1, :]
    bias = bias_ref[k : k + 1, :]
    step = CHUNK * seqs
    for r in range(0, span * seqs, step):
        u = ((x_ref[r : r + step, :] - mean) * slope + bias).astype(BF16)
        u_ref[r : r + step, :] = u
        v_ref[r : r + step, :] = dot(u, w_ref[k])
    shape = (seqs, states)
    rel = jnp.broadcast_to(rel_ref[...], shape)
    lr, li = wide(decay_ref.at[k], 0, shape), wide(decay_ref.at[k], 1, shape)
    zero = jnp.zeros(shape, F32)
    re, im = state_scan(v_ref, rel, lr, li, (zero, zero), span, backward)
    summary_ref[:, :states] = re
    summary_ref[:, states:] = im


def rebuild_states(k, plan, span, backward, places, refs, buffers, rel, v_ref, decay_ref, h_ref):
    seqs, states = rel.shape
    lr, li, gamma = (wide(decay_ref.at[k], row, rel.shape) for row in range(3))
    start = entering_state(plan, places, refs, buffers, backward, False)

    lead = 0 if backward else 1

    def keep(t, re, im):
        h_ref[at(t + lead, seqs), :states] = (re * gamma).astype(BF16)
        h_ref[at(t + lead, seqs), states:] = (im * gamma).astype(BF16)

    keep(span if backward else -1, *start)
    state_scan(v_ref, rel, lr, li, start, span, backward, keep)


def forward_body(
    k, plan, span, place_refs, exch, rel_ref, v_ref, x_ref, u_ref, mask_ref, stats_ref, bias_ref,
    decay_ref, w_out_ref, skip_ref, w_glu_ref,
    out_ref, h_ref, act_ref, slope_ref, gate_ref, value_ref, sums_ref, buffers,
):
    seqs = rel_ref.shape[0]
    width = x_ref.shape[1]
    states = decay_ref.shape[-1]
    rel = jnp.broadcast_to(rel_ref[...], (seqs, states))
    rebuild_states(k, plan, span, False, place_refs, exch, buffers, rel, v_ref, decay_ref, h_ref)
    mean, scale = stats_ref[0:1, :], stats_ref[3:4, :]
    bias, skip = bias_ref[k : k + 1, :], skip_ref[k : k + 1, :]
    step = CHUNK * seqs
    first = jnp.zeros((8, width), F32)
    second = jnp.zeros((8, width), F32)
    for r in range(0, span * seqs, step):
        x = x_ref[r : r + step, :]
        u = (x - mean) * scale + bias
        y = dot(h_ref[r + seqs : r + seqs + step, :], w_out_ref[k]) + skip * u
        act, slope = gelu_parts(y)
        act = act.astype(BF16)
        act_ref[r : r + step, :] = act
        slope_ref[r : r + step, :] = slope.astype(BF16)
        z = dot(act, w_glu_ref[k])
        value, gate = z[:, :width], sigmoid(z[:, width:])
        gated = value * gate
        out = x + gated
        out_ref[r : r + step, :] = out
        gate_ref[r : r + step, :] = gate.astype(BF16)
        value_ref[r : r + step, :] = (gated * (1.0 - gate)).astype(BF16)
        live = out * lane_tiled(mask_ref[r : r + step, :], width)
        first += jnp.sum(live.reshape(-1, 8, width), 0)
        second += jnp.sum((live * out).reshape(-1, 8, width), 0)
    spread(sums_ref, jnp.sum(first, 0, keepdims=True), jnp.sum(second, 0, keepdims=True))


def back_rows(k, r, step, dza, dzb, slope, width, w_glu_ref, w_out_ref, dz_ref, dy_ref, g_ref):
    dza, dzb = dza.astype(BF16), dzb.astype(BF16)
    dz_ref[r : r + step, :width] = dza
    dz_ref[r : r + step, width:] = dzb
    w = w_glu_ref[k]
    dact = dot_nt(dza, w[:, :width]) + dot_nt(dzb, w[:, width:])
    dy = (dact * slope).astype(BF16)
    dy_ref[r : r + step, :] = dy
    g_ref[r : r + step, :] = dot_nt(dy, w_out_ref[k])


def local_adjoint(k, span, backward, rel, g_ref, decay_ref, summary_ref):
    seqs, states = rel.shape
    lr, li = wide(decay_ref.at[k], 0, rel.shape), wide(decay_ref.at[k], 1, rel.shape)
    zero = jnp.zeros(rel.shape, F32)
    (re, im), _ = adjoint_scan(g_ref, rel, lr, li, (zero, zero), span, backward)
    summary_ref[:, :states] = re
    summary_ref[:, states:] = im


def turn_body(
    k, plan, span, place_refs, exch, rel_ref, v_ref, x_ref, u_ref, cot_ref, stats_ref, bias_ref,
    decay_ref, w_out_ref, skip_ref, w_glu_ref,
    out_ref, h_ref, act_ref, dz_ref, dy_ref, g_ref, summary_ref, buffers,
):
    seqs = rel_ref.shape[0]
    width = x_ref.shape[1]
    states = decay_ref.shape[-1]
    rel = jnp.broadcast_to(rel_ref[...], (seqs, states))
    rebuild_states(k, plan, span, True, place_refs, exch, buffers, rel, v_ref, decay_ref, h_ref)
    mean, scale = stats_ref[0:1, :], stats_ref[3:4, :]
    bias, skip = bias_ref[k : k + 1, :], skip_ref[k : k + 1, :]
    step = CHUNK * seqs
    for r in range(0, span * seqs, step):
        t0 = r // seqs
        x = x_ref[r : r + step, :]
        u = (x - mean) * scale + bias
        y = dot(h_ref[r : r + step, :], w_out_ref[k]) + skip * u
        act, slope = gelu_parts(y)
        act = act.astype(BF16)
        act_ref[r : r + step, :] = act
        z = dot(act, w_glu_ref[k])
        value, gate = z[:, :width], sigmoid(z[:, width:])
        gated = value * gate
        out_ref[:, t0 : t0 + CHUNK, :] = from_time_major(x + gated, seqs)
        d = to_time_major(cot_ref[:, t0 : t0 + CHUNK, :])
        back_rows(
            k, r, step, d * gate, d * (gated * (1.0 - gate)), slope, width,
            w_glu_ref, w_out_ref, dz_ref, dy_ref, g_ref,
        )
    local_adjoint(k, span, False, rel, g_ref, decay_ref, summary_ref)


def back_body(
    k, span, backward, tokens, rel_ref, sums_ref, part_ref, x_ref, mask_ref, stats_ref, slope_ref,
    gate_ref, value_ref, gain_ref, decay_ref, w_out_ref, w_glu_ref,
    d_ref, dz_ref, dy_ref, g_ref, grads_ref, summary_ref,
):
    seqs = rel_ref.shape[0]
    width = x_ref.shape[1]
    states = decay_ref.shape[-1]
    rel = jnp.broadcast_to(rel_ref[...], (seqs, states))
    shift, tilt = input_terms(k + 1, tokens, sums_ref, stats_ref, gain_ref, grads_ref)
    mean = stats_ref[0:1, :]
    step = CHUNK * seqs
    for r in range(0, span * seqs, step):
        live = lane_tiled(mask_ref[r : r + step, :], width)
        d = part_ref[r : r + step, :] + live * (shift + tilt * (x_ref[r : r + step, :] - mean))
        d_ref[r : r + step, :] = d
        back_rows(
            k, r, step, d * gate_ref[r : r + step, :].astype(F32),
            d * value_ref[r : r + step, :].astype(F32), slope_ref[r : r + step, :].astype(F32), width,
            w_glu_ref, w_out_ref, dz_ref, dy_ref, g_ref,
        )
    local_adjoint(k, span, backward, rel, g_ref, decay_ref, summary_ref)


def input_terms(k, tokens, sums_ref, stats_ref, gain_ref, grads_ref):
    bias_grad, gain_grad = gathered(sums_ref)
    grads_ref[0:1, :] = gain_grad
    grads_ref[1:2, :] = bias_grad
    rstd = stats_ref[2:3, :]
    gain = gain_ref[k : k + 1, :]
    scale = tokens[0]
    return -rstd * gain * bias_grad * scale, -rstd * rstd * gain * gain_grad * scale


def adjoint_body(
    k, plan, span, backward, seq_major, place_refs, exch, rel_ref, g_ref, h_ref, v_ref, dy_ref, x_ref,
    d_ref, stats_ref, gain_ref, bias_ref, decay_ref, w_in_ref, skip_ref,
    dv_ref, part_ref, small_ref, sums_ref, buffers,
):
    seqs = rel_ref.shape[0]
    width = x_ref.shape[1]
    states = decay_ref.shape[-1]
    rel = jnp.broadcast_to(rel_ref[...], (seqs, states))
    lr, li, gamma = (wide(decay_ref.at[k], row, rel.shape) for row in range(3))
    start = entering_state(plan, place_refs, exch, buffers, backward, True)
    before = 0 if backward else 1

    def use(t, ar, ai, live, kept):
        ar, ai = jnp.where(live, ar, 0.0), jnp.where(live, ai, 0.0)
        dv_ref[at(t, seqs), :states] = (ar * gamma).astype(BF16)
        dv_ref[at(t, seqs), states:] = (ai * gamma).astype(BF16)
        pr = h_ref[at(t + before, seqs), :states].astype(F32)
        pi = h_ref[at(t + before, seqs), states:].astype(F32)
        vr, vi = v_ref[at(t, seqs), :states], v_ref[at(t, seqs), states:]
        return (
            kept[0] + (ar * pr + ai * pi),
            kept[1] + (ai * pr - ar * pi),
            kept[2] + (ar * vr + ai * vi),
        )

    zero = jnp.zeros(rel.shape, F32)
    _, kept = adjoint_scan(g_ref, rel, lr, li, start, span, backward, use, (zero, zero, zero))
    mean, scale, rstd = stats_ref[0:1, :], stats_ref[3:4, :], stats_ref[2:3, :]
    gain, bias, skip = (ref[k : k + 1, :] for ref in (gain_ref, bias_ref, skip_ref))
    step = CHUNK * seqs
    first = jnp.zeros((8, width), F32)
    second = jnp.zeros((8, width), F32)
    third = jnp.zeros((8, width), F32)
    for r in range(0, span * seqs, step):
        xhat = (x_ref[r : r + step, :] - mean) * rstd
        dy = dy_ref[r : r + step, :].astype(F32)
        du = dot_nt(dv_ref[r : r + step, :], w_in_ref[k]) + dy * skip
        first += jnp.sum(du.reshape(-1, 8, width), 0)
        second += jnp.sum((du * xhat).reshape(-1, 8, width), 0)
        third += jnp.sum((dy * (xhat * gain + bias)).reshape(-1, 8, width), 0)
        if seq_major:
            d = to_time_major(d_ref[:, r // seqs : r // seqs + CHUNK, :])
        else:
            d = d_ref[r : r + step, :]
        part_ref[r : r + step, :] = d + du * scale
    spread(sums_ref, jnp.sum(first, 0, keepdims=True), jnp.sum(second, 0, keepdims=True))
    small_ref[...] = jnp.zeros_like(small_ref)
    for j in range(2):
        small_ref[0:1, j * states : (j + 1) * states] = jnp.sum(kept[j], 0, keepdims=True)
    small_ref[1:2, :states] = jnp.sum(kept[2], 0, keepdims=True)
    small_ref[2:3, :] = jnp.sum(third, 0, keepdims=True)


def finish_body(
    k, span, tokens, sums_ref, part_ref, x_ref, mask_ref, stats_ref, gain_ref, out_ref, grads_ref
):
    seqs = out_ref.shape[0]
    width = x_ref.shape[1]
    shift, tilt = input_terms(k, tokens, sums_ref, stats_ref, gain_ref, grads_ref)
    mean = stats_ref[0:1, :]
    step = CHUNK * seqs
    for r in range(0, span * seqs, step):
        live = lane_tiled(mask_ref[r : r + step, :], width)
        d = part_ref[r : r + step, :] + live * (shift + tilt * (x_ref[r : r + step, :] - mean))
        out_ref[:, r // seqs : r // seqs + CHUNK, :] = from_time_major(d, seqs)


def with_entry(body, plan, n_out):
    def wrapped(*refs):
        n_exch = sum(radix for radix, _ in plan) + len(plan)
        places, rest = refs[: len(plan)], refs[len(plan) :]
        exch, rest = rest[:n_exch], rest[n_exch:]
        body(places, exch, *rest[: -len(plan)], rest[-len(plan) :])

    return wrapped


def shards(
    inputs, lengths, cotangent, bn_gain, bn_bias, running, w_in, nu_log, phase, w_out, skip, w_glu
):
    seqs, span, width = inputs.shape
    states = nu_log.shape[1]
    count = lax.axis_size("tm")
    here = lax.axis_index("tm")
    rows = span * seqs
    plan = stages(count)
    token_count = jnp.sum(lengths).astype(F32)
    tokens = (1.0 / token_count).reshape(1)
    rel = (lengths - here * span).astype(jnp.int32)[:, None]
    starts, extents = [], []
    places = []
    for radix, stride in plan:
        base = here // (radix * stride) * (radix * stride)
        places.append(((here // stride) % radix).astype(jnp.int32).reshape(1))
        for member in range(radix):
            starts.append((base + member * stride) * span)
            extents.append(stride * span)
    counts = jnp.clip(
        lengths[None, :] - jnp.stack(starts)[:, None], 0, jnp.array(extents, jnp.int32)[:, None]
    )[:, :, None]
    rate = jnp.exp(nu_log)
    radius = jnp.exp(-rate)
    gamma = jnp.sqrt(-jnp.expm1(-2.0 * rate))
    cosine, sine = jnp.cos(phase), jnp.sin(phase)
    decay = jnp.stack([radius * cosine, radius * sine, gamma], axis=1)

    tile = ((count, 2 * width // LANES, LANES), F32)
    whole, whole_low = ((rows, width), F32), ((rows, width), BF16)
    pair, pair_low = ((rows, 2 * states), F32), ((rows, 2 * states), BF16)
    held_low = ((rows + seqs, 2 * states), BF16)
    summary = ((seqs, 2 * states), F32)
    eight = ((8, width), F32)
    buffers = entry_scratch(plan, summary[0])

    prepared = run(
        functools.partial(prepare_body, plan, span),
        [tile, whole, ((rows, LANES), F32)]
        + [((radix,) + summary[0], F32) for _ in range(2) for radix, _ in plan],
        [rel, counts, inputs, decay],
    )
    sums, x0, mask = prepared[:3]
    factors = [prepared[3 : 3 + len(plan)], prepared[3 + len(plan) :]]

    def project(k, sums, x):
        return run(
            functools.partial(project_body, k, span, k == 1),
            [whole_low, pair, eight, summary],
            [rel, everywhere(sums), x, bn_gain, bn_bias, w_in, decay],
            [tokens],
        )

    def entered(body, outs, held, k, operands, limit=48):
        return run(
            with_entry(body, plan, len(outs)),
            outs,
            entry_operands(held, factors[k]) + operands,
            places,
            buffers,
            limit=limit,
        )

    u0, v0, stats0, part = project(0, sums, x0)
    held = exchange(part, plan, factors[0], places, False, False)
    x1, h0, act0, slope0, gate0, value0, sums = entered(
        functools.partial(forward_body, 0, plan, span),
        [whole, held_low, whole_low, whole_low, whole_low, whole_low, tile],
        held,
        0,
        [rel, v0, x0, u0, mask, stats0, bn_bias, decay, w_out, skip, w_glu],
    )
    u1, v1, stats1, part = project(1, sums, x1)
    held = exchange(part, plan, factors[1], places, True, False)
    output, h1, act1, dz1, dy1, g1, part = entered(
        functools.partial(turn_body, 1, plan, span),
        [((seqs, span, width), F32), held_low, whole_low, ((rows, 2 * width), BF16), whole_low, pair, summary],
        held,
        1,
        [rel, v1, x1, u1, cotangent, stats1, bn_bias, decay, w_out, skip, w_glu],
    )
    held = exchange(part, plan, factors[1], places, False, True)
    dv1, part1, small1, sums = entered(
        functools.partial(adjoint_body, 1, plan, span, False, True),
        [pair_low, whole, eight, tile],
        held,
        1,
        [rel, g1, h1, v1, dy1, x1, cotangent, stats1, bn_gain, bn_bias, decay, w_in, skip],
    )
    d0, dz0, dy0, g0, grads1, part = run(
        functools.partial(back_body, 0, span, True),
        [whole, ((rows, 2 * width), BF16), whole_low, pair, eight, summary],
        [rel, everywhere(sums), part1, x1, mask, stats1, slope0, gate0, value0, bn_gain, decay, w_out, w_glu],
        [tokens],
    )
    held = exchange(part, plan, factors[0], places, True, True)
    dv0, part0, small0, sums = entered(
        functools.partial(adjoint_body, 0, plan, span, True, False),
        [pair_low, whole, eight, tile],
        held,
        0,
        [rel, g0, h0, v0, dy0, x0, d0, stats0, bn_gain, bn_bias, decay, w_in, skip],
    )
    grad_x, grads0 = run(
        functools.partial(finish_body, 0, span),
        [((seqs, span, width), F32), eight],
        [everywhere(sums), part0, x0, mask, stats0, bn_gain],
        [tokens],
    )

    def outer(left, right):
        return lax.dot_general(left, right, (((0,), (0,)), ((), ())), preferred_element_type=F32)

    h0, h1 = h0[seqs:], h1[:rows]
    g_glu, g_out, g_in, small = lax.psum(
        (
            jnp.stack([outer(act0, dz0), outer(act1, dz1)]),
            jnp.stack([outer(h0, dy0), outer(h1, dy1)]),
            jnp.stack([outer(u0, dv0), outer(u1, dv1)]),
            jnp.stack([small0, small1]),
        ),
        "tm",
    )
    sum_re, sum_im, g_gamma = small[:, 0, :states], small[:, 0, states:], small[:, 1, :states]
    g_nu = (sum_re * cosine + sum_im * sine) * (-radius * rate) + g_gamma * rate * radius * radius / gamma
    g_phase = radius * (sum_im * cosine - sum_re * sine)
    stats = jnp.stack([stats0, stats1])
    running_out = (1.0 - momentum) * running + momentum * stats[:, :2] * jnp.stack(
        [jnp.ones_like(token_count), token_count / (token_count - 1.0)]
    )[None, :, None]
    grads = jnp.stack([grads0, grads1])
    return (
        output, grad_x, grads[:, 0], grads[:, 1], g_in, g_nu, g_phase, g_out, small[:, 2], g_glu, running_out,
    )


def solution(mesh):
    placed = (P(None, "tm", None), P(), P(None, "tm", None)) + (P(),) * 9
    return jax.shard_map(
        shards,
        mesh=mesh,
        in_specs=placed,
        out_specs=(P(None, "tm", None),) * 2 + (P(),) * 9,
        check_vma=False,
    )
```

profile of v0, /device:TPU:0, one launch (start us, length us, event | category | flops | bytes accessed | tf_op | source)
XLA Modules:
  0.0 387.6 jit_solution(6933042055464796218)
XLA Ops:
  17.0 7.4 %all-to-all-start = ((f32[32,8,128]{2,1,0:T(8,128)}), f32[32,8,128]{2,1,0:T(8,128)}, u32[]{:S(2)}, u32[]{:S(2)}) async-start(f32[32,8,128]{2,1,0:T(8,128)} %copy-done.53), calls=%async_computation | async-start | bytes 262144 | tf_op jit(solution)/shard_map/all_to_all | solution.py:85
  25.2 7.5 %all-to-all-done.sums_ref = f32[32,8,128]{2,1,0:T(8,128)} async-done(((f32[32,8,128]{2,1,0:T(8,128)}), f32[32,8,128]{2,1,0:T(8,128)}, u32[]{:S(2)}, u32[]{:S(2)}) %all-to-all-start) | async-done | bytes 131104 | tf_op jit(solution)/shard_map/all_to_all | solution.py:85
  34.1 2.6 shard_map.213
  46.0 1.9 collective-permute-done.3.refs_3_.refs_8_
  52.0 2.5 collective-permute-start.4
  54.5 1.6 collective-permute-done.6.refs_12_
  61.1 9.2 %shard_map.216 = (f32[1024,512]{1,0:T(8,128)}, bf16[1040,512]{1,0:T(8,128)(2,1)}, bf16[1024,512]{1,0:T(8,128)(2,1)S(1)}, bf16[1024,512]{1,0:T(8,128)(2,1)S(1)}, ...) custom-call(s32[1]{0:T(128)} %bitcast.place_ref.refs_0_, ...), custom_call_target="tpu_custom_call" | custom-call | tf_op jit(solution)/shard_map/pallas_call | solution.py:30
  72.4 11.5 %all_to_all.20.sums_ref = f32[32,8,128]{2,1,0:T(8,128)S(1)} all-to-all(f32[32,8,128]{2,1,0:T(8,128)S(1)} %get-tuple-element.68), channel_id=1, replica_groups=mesh['tm'=32] {'tm'}, dimensions={0} | all-to-all | bytes 262144 | tf_op jit(solution)/shard_map/all_to_all | solution.py:85
  92.7 1.6 collective-permute-done.10.refs_3_.refs_8_
  97.0 2.5 collective-permute-start.11
  103.2 13.0 %shard_map.220 = (f32[16,64,512]{2,1,0:T(8,128)}, bf16[1040,512]{1,0:T(8,128)(2,1)S(1)}, bf16[1024,512]{1,0:T(8,128)(2,1)S(1)}, bf16[1024,1024]{1,0:T(8,128)(2,1...) custom-call(s32[1]{0:T(128)} %bitcast.place_ref.refs_0_, ...), custom_call_target="tpu_custom_call" | custom-call | tf_op jit(solution)/shard_map/pallas_call | solution.py:30
  117.4 1.8 collective-permute-start.17
  124.5 2.1 collective-permute-start.20
  129.0 4.2 %convolution_bitcast_fusion = f32[1,512,1024]{2,1,0:T(8,128)} fusion(bf16[1024,512]{1,0:T(8,128)(2,1)S(1)} %get-tuple-element.103, bf16[1024,1024]{1,0:T(8,128)(2,1)} %get-tuple-element.104), kind=kOutput, calls=%fused_computation.3 | convolution fusion | flops 1073741824 | bytes 5242880 | tf_op jit(solution)/shard_map/dot_general | solution.py:635
  133.1 7.7 %shard_map.223 = (bf16[1024,512]{1,0:T(8,128)(2,1)S(1)}, f32[1024,512]{1,0:T(8,128)}, f32[8,512]{1,0:T(8,128)S(1)}, f32[32,8,128]{2,1,0:T(8,128)S(1)}) custom-call(s32[1]{0:T(128)} %bitcast.place_ref.refs_0_, s32[1]{0:T(128)} %bitcast.1.place_ref.refs_1_, s32[1]{0:T(128)} %bitcast.2.refs_2_, f32[16,512]{1,0:T(8,128)S(1)} %get-tuple-element.78.refs_0_.refs_3_, ...), custom_call_target="tpu_custom_call" | custom-call | tf_op jit(solution)/shard_map/pallas_call | solution.py:30
  143.1 3.3 all-to-all-start.2
  146.6 1.7 convolution_bitcast_fusion.2
  148.4 1.7 convolution_bitcast_fusion.4
  150.1 4.4 %all-to-all-done.2.sums_ref = f32[32,8,128]{2,1,0:T(8,128)} async-done(((f32[32,8,128]{2,1,0:T(8,128)}), f32[32,8,128]{2,1,0:T(8,128)}, u32[]{:S(2)}, u32[]{:S(2)}) %all-to-all-start.2) | async-done | bytes 131104 | tf_op jit(solution)/shard_map/all_to_all | solution.py:85
  159.9 5.1 %shard_map.224 = (f32[1024,512]{1,0:T(8,128)S(1)}, bf16[1024,1024]{1,0:T(8,128)(2,1)S(1)}, bf16[1024,512]{1,0:T(8,128)(2,1)S(1)}, f32[1024,512]{1,0:T(8,128)S(1)...) custom-call(f32[1]{0:T(128)} %bitcast.3.tokens, s32[16,1]{1,0:T(8,128)S(1)} %copy-done.32, ...), custom_call_target="tpu_custom_call" | custom-call | tf_op jit(solution)/shard_map/pallas_call | solution.py:30
  169.9 1.7 collective-permute-start.22
  171.6 2.3 pad_maximum_fusion
  176.1 2.4 collective-permute-start.25
  180.7 7.5 %shard_map.227 = (bf16[1024,512]{1,0:T(8,128)(2,1)S(1)}, f32[1024,512]{1,0:T(8,128)}, f32[8,512]{1,0:T(8,128)S(1)}, f32[32,8,128]{2,1,0:T(8,128)}) custom-call(s32[1]{0:T(128)} %bitcast.place_ref.refs_0_, s32[1]{0:T(128)} %bitcast.1.place_ref.refs_1_, s32[1]{0:T(128)} %bitcast.2.refs_2_, f32[16,512]{1,0:T(8,128)S(1)} %get-tuple-element.87.refs_0_.refs_3_, ...), custom_call_target="tpu_custom_call" | custom-call | tf_op jit(solution)/shard_map/pallas_call | solution.py:30
  192.4 3.4 all-to-all-start.3
  195.9 42.6 %psum.29 = f32[2,8,512]{2,0,1:T(2,128)S(1)} all-reduce(f32[2,8,512]{2,0,1:T(2,128)S(1)} %pad_maximum_fusion.3), channel_id=1, replica_groups=mesh['tm'=32] {'tm'}, use_global_device_ids=true, to_apply=%region_2.3 | all-reduce | flops 8192 | bytes 65536 | tf_op jit(solution)/shard_map/psum | solution.py:638
  239.7 1.6 copy-done.13
  241.4 2.1 shard_map.228
  244.1 128.4 %all-reduce.3.cloned.1.call-done = (f32[2,512,512]{2,1,0:T(8,128)}, f32[2,512,512]{2,1,0:T(8,128)}, f32[2,512,1024]{2,1,0:T(8,128)}) async-done(((f32[2,512,512]{2,1,0:T(8,128)}, f32[2,512,512]{2,1,0:T(8,128)}, f32[2,512,1024]{2,1,0:T(8,128)}), (f32[2,512,512]{2,1,0:T(8,128)}, f32[2,512,512]{2,1,0:T(8,128)}, f32[2,512,1024]{2,1,0:T(8,128)})) %all-reduce.3.cloned.1.call-update) | async-done | bytes 8388624 | tf_op jit(solution)/shard_map/psum | solution.py:638
  372.5 3.2 copy.41
  377.1 1.6 copy-done.61
  378.7 2.0 copy.43
  (225 shorter events, 79.8 us)
Async XLA Ops:
  17.0 15.6 %all-to-all-start = ((f32[32,8,128]{2,1,0:T(8,128)}), f32[32,8,128]{2,1,0:T(8,128)}, u32[]{:S(2)}, u32[]{:S(2)}) async-start(f32[32,8,128]{2,1,0:T(8,128)} %copy-done.53), calls=%async_computation | async-start | bytes 262144 | tf_op jit(solution)/shard_map/all_to_all | solution.py:85
  39.6 1.6 collective-permute-start
  42.5 5.4 %collective-permute-start.3 = (f32[16,512]{1,0:T(8,128)}, f32[16,512]{1,0:T(8,128)}, u32[]{:S(2)}, u32[]{:S(2)}) collective-permute-start(f32[16,512]{1,0:T(8,128)} %shard_map.214.refs_0_.refs_5_), channel_id=1, source_target_pairs={{0,6},{1,7},{2,4},{3,5},{4,2},{5,3},{6,0},{7,1},{8,14},{9,15},{10,... | collective-permute-start | bytes 98312 | tf_op jit(solution)/shard_map/ppermute | solution.py:58
  43.4 4.6 %collective-permute-start.2 = (f32[16,512]{1,0:T(8,128)}, f32[16,512]{1,0:T(8,128)}, u32[]{:S(2)}, u32[]{:S(2)}) collective-permute-start(f32[16,512]{1,0:T(8,128)} %shard_map.214.refs_0_.refs_5_), channel_id=1, source_target_pairs={{0,4},{1,5},{2,6},{3,7},{4,0},{5,1},{6,2},{7,3},{8,12},{9,13},{10,... | collective-permute-start | bytes 98312 | tf_op jit(solution)/shard_map/ppermute | solution.py:58
  44.4 4.2 %collective-permute-start.1 = (f32[16,512]{1,0:T(8,128)}, f32[16,512]{1,0:T(8,128)}, u32[]{:S(2)}, u32[]{:S(2)}) collective-permute-start(f32[16,512]{1,0:T(8,128)} %shard_map.214.refs_0_.refs_5_), channel_id=1, source_target_pairs={{0,2},{1,3},{2,0},{3,1},{4,6},{5,7},{6,4},{7,5},{8,10},{9,11},{10,... | collective-permute-start | bytes 98312 | tf_op jit(solution)/shard_map/ppermute | solution.py:58
  50.1 6.0 %collective-permute-start.6 = (f32[16,512]{1,0:T(8,128)}, f32[16,512]{1,0:T(8,128)}, u32[]{:S(2)}, u32[]{:S(2)}) collective-permute-start(f32[16,512]{1,0:T(8,128)} %shard_map.215.refs_9_), channel_id=1, source_target_pairs={{0,24},{1,25},{2,26},{3,27},{4,28},{5,29},{6,30},{7,31},{8,16},{9,... | collective-permute-start | bytes 98312 | tf_op jit(solution)/shard_map/ppermute | solution.py:58
  51.4 5.6 %collective-permute-start.5 = (f32[16,512]{1,0:T(8,128)}, f32[16,512]{1,0:T(8,128)}, u32[]{:S(2)}, u32[]{:S(2)}) collective-permute-start(f32[16,512]{1,0:T(8,128)} %shard_map.215.refs_9_), channel_id=1, source_target_pairs={{0,16},{1,17},{2,18},{3,19},{4,20},{5,21},{6,22},{7,23},{8,24},{9,... | collective-permute-start | bytes 98312 | tf_op jit(solution)/shard_map/ppermute | solution.py:58
  52.0 5.1 %collective-permute-start.4 = (f32[16,512]{1,0:T(8,128)}, f32[16,512]{1,0:T(8,128)}, u32[]{:S(2)}, u32[]{:S(2)}) collective-permute-start(f32[16,512]{1,0:T(8,128)} %shard_map.215.refs_9_), channel_id=1, source_target_pairs={{0,8},{1,9},{2,10},{3,11},{4,12},{5,13},{6,14},{7,15},{8,0},{9,1},... | collective-permute-start | bytes 98312 | tf_op jit(solution)/shard_map/ppermute | solution.py:58
  88.0 1.2 collective-permute-start.7
  89.2 5.2 %collective-permute-start.10 = (f32[16,512]{1,0:T(8,128)S(1)}, f32[16,512]{1,0:T(8,128)S(1)}, u32[]{:S(2)}, u32[]{:S(2)}) collective-permute-start(f32[16,512]{1,0:T(8,128)S(1)} %shard_map.218.refs_0_.refs_5_), channel_id=1, source_target_pairs={{0,6},{1,7},{2,4},{3,5},{4,2},{5,3},{6,0},{7,1},{8,14},{9,15},{10,... | collective-permute-start | bytes 98312 | tf_op jit(solution)/shard_map/ppermute | solution.py:58
  90.1 4.3 %collective-permute-start.9 = (f32[16,512]{1,0:T(8,128)S(1)}, f32[16,512]{1,0:T(8,128)S(1)}, u32[]{:S(2)}, u32[]{:S(2)}) collective-permute-start(f32[16,512]{1,0:T(8,128)S(1)} %shard_map.218.refs_0_.refs_5_), channel_id=1, source_target_pairs={{0,4},{1,5},{2,6},{3,7},{4,0},{5,1},{6,2},{7,3},{8,12},{9,13},{10,... | collective-permute-start | bytes 98312 | tf_op jit(solution)/shard_map/ppermute | solution.py:58
  91.1 3.9 %collective-permute-start.8 = (f32[16,512]{1,0:T(8,128)S(1)}, f32[16,512]{1,0:T(8,128)S(1)}, u32[]{:S(2)}, u32[]{:S(2)}) collective-permute-start(f32[16,512]{1,0:T(8,128)S(1)} %shard_map.218.refs_0_.refs_5_), channel_id=1, source_target_pairs={{0,2},{1,3},{2,0},{3,1},{4,6},{5,7},{6,4},{7,5},{8,10},{9,11},{10,... | collective-permute-start | bytes 98312 | tf_op jit(solution)/shard_map/ppermute | solution.py:58
  95.1 5.8 %collective-permute-start.13 = (f32[16,512]{1,0:T(8,128)S(1)}, f32[16,512]{1,0:T(8,128)S(1)}, u32[]{:S(2)}, u32[]{:S(2)}) collective-permute-start(f32[16,512]{1,0:T(8,128)S(1)} %shard_map.219.refs_9_), channel_id=1, source_target_pairs={{0,24},{1,25},{2,26},{3,27},{4,28},{5,29},{6,30},{7,31},{8,16},{9,... | collective-permute-start | bytes 98312 | tf_op jit(solution)/shard_map/ppermute | solution.py:58
  96.4 5.2 %collective-permute-start.12 = (f32[16,512]{1,0:T(8,128)S(1)}, f32[16,512]{1,0:T(8,128)S(1)}, u32[]{:S(2)}, u32[]{:S(2)}) collective-permute-start(f32[16,512]{1,0:T(8,128)S(1)} %shard_map.219.refs_9_), channel_id=1, source_target_pairs={{0,16},{1,17},{2,18},{3,19},{4,20},{5,21},{6,22},{7,23},{8,24},{9,... | collective-permute-start | bytes 98312 | tf_op jit(solution)/shard_map/ppermute | solution.py:58
  97.0 4.7 %collective-permute-start.11 = (f32[16,512]{1,0:T(8,128)S(1)}, f32[16,512]{1,0:T(8,128)S(1)}, u32[]{:S(2)}, u32[]{:S(2)}) collective-permute-start(f32[16,512]{1,0:T(8,128)S(1)} %shard_map.219.refs_9_), channel_id=1, source_target_pairs={{0,8},{1,9},{2,10},{3,11},{4,12},{5,13},{6,14},{7,15},{8,0},{9,1},... | collective-permute-start | bytes 98312 | tf_op jit(solution)/shard_map/ppermute | solution.py:58
  116.2 1.2 collective-permute-start.14
  117.4 4.9 %collective-permute-start.17 = (f32[16,512]{1,0:T(8,128)S(1)}, f32[16,512]{1,0:T(8,128)S(1)}, u32[]{:S(2)}, u32[]{:S(2)}) collective-permute-start(f32[16,512]{1,0:T(8,128)S(1)} %shard_map.221.refs_0_.refs_5_), channel_id=1, source_target_pairs={{0,6},{1,7},{2,4},{3,5},{4,2},{5,3},{6,0},{7,1},{8,14},{9,15},{10,... | collective-permute-start | bytes 98312 | tf_op jit(solution)/shard_map/ppermute | solution.py:58
  119.2 3.9 %collective-permute-start.16 = (f32[16,512]{1,0:T(8,128)S(1)}, f32[16,512]{1,0:T(8,128)S(1)}, u32[]{:S(2)}, u32[]{:S(2)}) collective-permute-start(f32[16,512]{1,0:T(8,128)S(1)} %shard_map.221.refs_0_.refs_5_), channel_id=1, source_target_pairs={{0,4},{1,5},{2,6},{3,7},{4,0},{5,1},{6,2},{7,3},{8,12},{9,13},{10,... | collective-permute-start | bytes 98312 | tf_op jit(solution)/shard_map/ppermute | solution.py:58
  120.6 3.9 %collective-permute-start.15 = (f32[16,512]{1,0:T(8,128)S(1)}, f32[16,512]{1,0:T(8,128)S(1)}, u32[]{:S(2)}, u32[]{:S(2)}) collective-permute-start(f32[16,512]{1,0:T(8,128)S(1)} %shard_map.221.refs_0_.refs_5_), channel_id=1, source_target_pairs={{0,2},{1,3},{2,0},{3,1},{4,6},{5,7},{6,4},{7,5},{8,10},{9,11},{10,... | collective-permute-start | bytes 98312 | tf_op jit(solution)/shard_map/ppermute | solution.py:58
  124.5 8.6 %collective-permute-start.20 = (f32[16,512]{1,0:T(8,128)S(1)}, f32[16,512]{1,0:T(8,128)S(1)}, u32[]{:S(2)}, u32[]{:S(2)}) collective-permute-start(f32[16,512]{1,0:T(8,128)S(1)} %shard_map.222.refs_9_), channel_id=1, source_target_pairs={{0,24},{1,25},{2,26},{3,27},{4,28},{5,29},{6,30},{7,31},{8,16},{9,... | collective-permute-start | bytes 98312 | tf_op jit(solution)/shard_map/ppermute | solution.py:58
  126.6 6.5 %collective-permute-start.19 = (f32[16,512]{1,0:T(8,128)S(1)}, f32[16,512]{1,0:T(8,128)S(1)}, u32[]{:S(2)}, u32[]{:S(2)}) collective-permute-start(f32[16,512]{1,0:T(8,128)S(1)} %shard_map.222.refs_9_), channel_id=1, source_target_pairs={{0,16},{1,17},{2,18},{3,19},{4,20},{5,21},{6,22},{7,23},{8,24},{9,... | collective-permute-start | bytes 98312 | tf_op jit(solution)/shard_map/ppermute | solution.py:58
  127.7 5.4 %collective-permute-start.18 = (f32[16,512]{1,0:T(8,128)S(1)}, f32[16,512]{1,0:T(8,128)S(1)}, u32[]{:S(2)}, u32[]{:S(2)}) collective-permute-start(f32[16,512]{1,0:T(8,128)S(1)} %shard_map.222.refs_9_), channel_id=1, source_target_pairs={{0,8},{1,9},{2,10},{3,11},{4,12},{5,13},{6,14},{7,15},{8,0},{9,1},... | collective-permute-start | bytes 98312 | tf_op jit(solution)/shard_map/ppermute | solution.py:58
  143.1 11.5 %all-to-all-start.2 = ((f32[32,8,128]{2,1,0:T(8,128)}), f32[32,8,128]{2,1,0:T(8,128)}, u32[]{:S(2)}, u32[]{:S(2)}) async-start(f32[32,8,128]{2,1,0:T(8,128)} %copy-done.52), calls=%async_computation.2 | async-start | bytes 262144 | tf_op jit(solution)/shard_map/all_to_all | solution.py:85
  146.3 226.2 %all-reduce.3.cloned.1.call-start = ((), (), s32[]{:S(2)}) async-start(), calls=%async_computation.4 | async-start | bytes 16777216 | tf_op jit(solution)/shard_map/psum | solution.py:638
  165.0 3.0 collective-permute-start.21
  168.0 5.9 %collective-permute-start.24 = (f32[16,512]{1,0:T(8,128)S(1)}, f32[16,512]{1,0:T(8,128)S(1)}, u32[]{:S(2)}, u32[]{:S(2)}) collective-permute-start(f32[16,512]{1,0:T(8,128)S(1)} %shard_map.225.refs_0_.refs_5_), channel_id=1, source_target_pairs={{0,6},{1,7},{2,4},{3,5},{4,2},{5,3},{6,0},{7,1},{8,14},{9,15},{10,... | collective-permute-start | bytes 98312 | tf_op jit(solution)/shard_map/ppermute | solution.py:58
  168.8 5.1 %collective-permute-start.23 = (f32[16,512]{1,0:T(8,128)S(1)}, f32[16,512]{1,0:T(8,128)S(1)}, u32[]{:S(2)}, u32[]{:S(2)}) collective-permute-start(f32[16,512]{1,0:T(8,128)S(1)} %shard_map.225.refs_0_.refs_5_), channel_id=1, source_target_pairs={{0,4},{1,5},{2,6},{3,7},{4,0},{5,1},{6,2},{7,3},{8,12},{9,13},{10,... | collective-permute-start | bytes 98312 | tf_op jit(solution)/shard_map/ppermute | solution.py:58
  169.9 4.0 %collective-permute-start.22 = (f32[16,512]{1,0:T(8,128)S(1)}, f32[16,512]{1,0:T(8,128)S(1)}, u32[]{:S(2)}, u32[]{:S(2)}) collective-permute-start(f32[16,512]{1,0:T(8,128)S(1)} %shard_map.225.refs_0_.refs_5_), channel_id=1, source_target_pairs={{0,2},{1,3},{2,0},{3,1},{4,6},{5,7},{6,4},{7,5},{8,10},{9,11},{10,... | collective-permute-start | bytes 98312 | tf_op jit(solution)/shard_map/ppermute | solution.py:58
  174.0 6.0 %collective-permute-start.27 = (f32[16,512]{1,0:T(8,128)S(1)}, f32[16,512]{1,0:T(8,128)S(1)}, u32[]{:S(2)}, u32[]{:S(2)}) collective-permute-start(f32[16,512]{1,0:T(8,128)S(1)} %shard_map.226.refs_9_), channel_id=1, source_target_pairs={{0,24},{1,25},{2,26},{3,27},{4,28},{5,29},{6,30},{7,31},{8,16},{9,... | collective-permute-start | bytes 98312 | tf_op jit(solution)/shard_map/ppermute | solution.py:58
  175.2 5.4 %collective-permute-start.26 = (f32[16,512]{1,0:T(8,128)S(1)}, f32[16,512]{1,0:T(8,128)S(1)}, u32[]{:S(2)}, u32[]{:S(2)}) collective-permute-start(f32[16,512]{1,0:T(8,128)S(1)} %shard_map.226.refs_9_), channel_id=1, source_target_pairs={{0,16},{1,17},{2,18},{3,19},{4,20},{5,21},{6,22},{7,23},{8,24},{9,... | collective-permute-start | bytes 98312 | tf_op jit(solution)/shard_map/ppermute | solution.py:58
  176.1 4.6 %collective-permute-start.25 = (f32[16,512]{1,0:T(8,128)S(1)}, f32[16,512]{1,0:T(8,128)S(1)}, u32[]{:S(2)}, u32[]{:S(2)}) collective-permute-start(f32[16,512]{1,0:T(8,128)S(1)} %shard_map.226.refs_9_), channel_id=1, source_target_pairs={{0,8},{1,9},{2,10},{3,11},{4,12},{5,13},{6,14},{7,15},{8,0},{9,1},... | collective-permute-start | bytes 98312 | tf_op jit(solution)/shard_map/ppermute | solution.py:58
  192.4 47.3 %all-to-all-start.3 = ((f32[32,8,128]{2,1,0:T(8,128)}), f32[32,8,128]{2,1,0:T(8,128)S(1)}, u32[]{:S(2)}, u32[]{:S(2)}) async-start(f32[32,8,128]{2,1,0:T(8,128)} %get-tuple-element.92), calls=%async_computation.3 | async-start | bytes 262144 | tf_op jit(solution)/shard_map/all_to_all | solution.py:85
  (71 other events, 819.7 us)
Sparse Core Ops, SparseCore 0:
  191.2 181.2 all-reduce.2
where the time goes:
time: 389 us; the launch traced here: 388 us
  waiting for transfers between devices  158 us (41%)
  blocking collectives  54.1 us (14%)
  Pallas kernels  53 us (14%)
  starting transfers between devices  47 us (12%)
  local copies, waits for them, and re-layouts  40.3 us (10%)
  between operations  15.4 us (4%)
  matrix products  10.3 us (3%)
  other arithmetic  9.57 us (2%)
    psum x1, waiting for transfers between devices, shards(): lax.psum((jnp.stack([outer(act0, dz0), outer(act1, dz1)]), jnp.stack([out...  128 us
    pallas_call x17, Pallas kernels, run(): pl.pallas_call(body, out_shape=[jax.ShapeDtypeStruct(shape, dtype) for sh...  53 us
    psum x1, blocking collectives, shards(): lax.psum((jnp.stack([outer(act0, dz0), outer(act1, dz1)]), jnp.stack([out...  42.6 us
    unnamed x146, local copies, waits for them, and re-layouts  38.7 us
    ppermute x28, starting transfers between devices, swap(): lax.ppermute(value, 'tm', [(i, i ^ stride * mask) for i in range(count)])  32.6 us
    ppermute x28, waiting for transfers between devices, swap(): lax.ppermute(value, 'tm', [(i, i ^ stride * mask) for i in range(count)])  17.5 us
    all_to_all x3, starting transfers between devices, everywhere(): return lax.all_to_all(tiles, 'tm', 0, 0)  14.1 us
    all_to_all x3, waiting for transfers between devices, everywhere(): return lax.all_to_all(tiles, 'tm', 0, 0)  11.9 us
  transfers between devices with their start and end apart: 32, of which 21 were waited for; matrix products, arithmetic and copies ran while one was open for 4% of the time, Pallas kernels for 1%

commit v1 on v0

v1 whole, which is shorter than its diff:
```python
import functools
import math

import jax
import jax.numpy as jnp
from jax import lax
from jax.experimental import pallas as pl
from jax.experimental.pallas import tpu as pltpu
from jax.sharding import PartitionSpec as P

norm_epsilon = 1e-05
momentum = 0.1
inverse_root_two = 0.7071067811865476
density_scale = 0.3989422804014327
F32, BF16 = jnp.float32, jnp.bfloat16
LANES = 128
MIB = 1 << 20


def dot(left, right):
    return jnp.dot(left, right, preferred_element_type=F32)


def dot_tn(left, right):
    return lax.dot_general(left, right, (((0,), (0,)), ((), ())), preferred_element_type=F32)


def dot_nt(left, right):
    return lax.dot_general(left, right, (((1,), (1,)), ((), ())), preferred_element_type=F32)


def run(body, outs, operands, after=(), scratch=(), limit=12, macs=0):
    vmem = pl.BlockSpec(memory_space=pltpu.VMEM)
    anywhere = pl.BlockSpec(memory_space=pl.ANY)
    first, second = len(operands), len(operands) + len(after)

    def kernel(*refs):
        body(*refs[:first], *refs[second:])

    return pl.pallas_call(
        kernel,
        out_shape=[jax.ShapeDtypeStruct(shape, dtype) for shape, dtype in outs],
        in_specs=[vmem] * len(operands) + [anywhere] * len(after),
        out_specs=[vmem] * len(outs),
        scratch_shapes=list(scratch),
        compiler_params=pltpu.CompilerParams(vmem_limit_bytes=limit * MIB),
        cost_estimate=pl.CostEstimate(
            flops=2 * macs,
            bytes_accessed=sum(a.size * a.dtype.itemsize for a in operands)
            + sum(math.prod(shape) * jnp.dtype(dtype).itemsize for shape, dtype in outs),
            transcendentals=0,
        ),
    )(*operands, *after)


def radices(count):
    out = []
    while count > 1:
        radix = 2 if not out or count % 4 else 4
        out.append(radix)
        count //= radix
    return out


def stages(count):
    stride, out = 1, []
    for radix in radices(count):
        out.append((radix, stride))
        stride *= radix
    return out


def swap(value, stride, mask):
    count = lax.axis_size("tm")
    return lax.ppermute(value, "tm", [(i, i ^ (stride * mask)) for i in range(count)])


def group_of(value, radix, stride):
    return [value] + [swap(value, stride, mask) for mask in range(1, radix)]


def place_in(radix, stride):
    return lax.rem(lax.div(lax.axis_index("tm"), stride), radix)


def rows_to_tile(first, second):
    pieces = [
        row[:, j : j + LANES] for row in (first, second) for j in range(0, row.shape[1], LANES)
    ]
    return jnp.concatenate(pieces, axis=0)


def tile_to_rows(tile):
    half = tile.shape[0] // 2
    return [
        jnp.concatenate([tile[base + j : base + j + 1, :] for j in range(half)], axis=1)
        for base in (0, half)
    ]


def spread(ref, first, second):
    ref[...] = jnp.broadcast_to(rows_to_tile(first, second)[None], ref.shape)


def gathered(ref):
    return tile_to_rows(jnp.sum(ref[...], axis=0))


def everywhere(tiles):
    return lax.all_to_all(tiles, "tm", 0, 0)


def mul(ar, ai, br, bi):
    return ar * br - ai * bi, ar * bi + ai * br


def members(refs, place, buffer):
    for offset, ref in enumerate(refs):
        buffer[jnp.bitwise_xor(place, offset)] = ref[...]


def pass_through(k, buffer, factor, place, state, backward, conj):
    radix, _, width = buffer.shape
    states = width // 2
    if state is None:
        zero = jnp.zeros(buffer.shape[1:-1] + (states,), F32)
        state = (zero, zero)
    entering = state
    for member in range(radix - 1, -1, -1) if backward else range(radix):
        entering = tuple(jnp.where(place == member, s, e) for s, e in zip(state, entering))
        fr, fi = factor[k, member, :, :states], factor[k, member, :, states:]
        moved = mul(fr, -fi if conj else fi, *state)
        state = (moved[0] + buffer[member, :, :states], moved[1] + buffer[member, :, states:])
    return entering, state


def total_body(k, radix, stride, backward, conj, *refs):
    factor, out, buffer = refs[radix:]
    place = place_in(radix, stride)
    members(refs[:radix], place, buffer)
    _, (re, im) = pass_through(k, buffer, factor, place, None, backward, conj)
    states = re.shape[1]
    out[:, :states] = re
    out[:, states:] = im


def group_total(k, group, level, plan, factors, backward, conj, after=()):
    radix, stride = plan[level]
    shape = group[0].shape
    (total,) = run(
        functools.partial(total_body, k, radix, stride, backward, conj),
        [(shape, F32)],
        list(group) + [factors[level]],
        after,
        [pltpu.VMEM((radix,) + shape, F32)],
        limit=4,
    )
    return total


def exchange(k, summary, plan, factors, backward, conj, between=None):
    held = []
    value = summary
    for level, (radix, stride) in enumerate(plan):
        group = group_of(value, radix, stride)
        held.append(group)
        if level + 1 < len(plan):
            after = between(level, value) if between else ()
            value = group_total(k, group, level, plan, factors, backward, conj, after)
            if between and level + 2 == len(plan):
                between(level + 1, value)
    return held


def entry_operands(held, factors):
    return [value for group in held for value in group] + list(factors)


def entry_scratch(plan, shape):
    return [pltpu.VMEM((radix,) + shape, F32) for radix, _ in plan]


def entering_state(k, plan, refs, buffers, backward, conj):
    total = sum(radix for radix, _ in plan)
    values, factors = refs[:total], refs[total:]
    start, groups = 0, []
    for radix, _ in plan:
        groups.append(values[start : start + radix])
        start += radix
    state = None
    for level in range(len(plan) - 1, -1, -1):
        place = place_in(*plan[level])
        members(groups[level], place, buffers[level])
        state, _ = pass_through(k, buffers[level], factors[level], place, state, backward, conj)
    return state


CHUNKS = 32
LEVELS = CHUNKS.bit_length() - 1


def partners(count):
    order = [(1 << b, 1 << b) for b in range(count.bit_length() - 1)]
    if len(order) > 2:
        order[1], order[2] = (2, 4), (4, 2)
    return order


def with_partner(value, bits):
    even, odd = bits
    count = lax.axis_size("tm")
    return lax.ppermute(value, "tm", [(i, i ^ (odd if i & 1 else even)) for i in range(count)])


def own_chunk(count, other_core=False):
    here = lax.axis_index("tm")
    if other_core:
        here = jnp.bitwise_xor(here, 1)
    own = 0
    for even, odd in partners(count)[:LEVELS]:
        taken = jnp.where(jnp.bitwise_and(here, 1) == 1, here & odd, here & even)
        own = own * 2 + jnp.where(taken != 0, 1, 0)
    return own


def slots(level):
    return (CHUNKS >> (level + 1), CHUNKS >> level) if level < LEVELS else (0, 1)


def outer_body(count, pairs, n_left, n_right, *refs):
    lefts, rights = refs[:n_left], refs[n_left : n_left + n_right]
    outs, products = refs[n_left + n_right : -len(pairs)], refs[-len(pairs) :]
    owns = own_chunk(count), own_chunk(count, True)
    half = CHUNKS // 2
    for q, (left, row, right, column) in enumerate(pairs):
        product = products[q]
        span = rights[right].shape[0]
        wide_left = lefts[left].shape[1]
        part = wide_left // CHUNKS
        width = product.shape[1]
        product[...] = dot_tn(
            lefts[left][row : row + span, :], rights[right][:, column : column + width]
        )
        for level in range(LEVELS + 1):
            low, high = slots(level)
            for slot in range(low, high):
                chunk = jnp.bitwise_xor(owns[slot // half], slot % half)
                chunk = pl.multiple_of(chunk * part, part)
                place = ((slot - low) * len(pairs) + q) * part
                outs[level][place : place + part, :] = product[pl.ds(chunk, part), :]


def add_body(low, *refs):
    out = refs[-1]
    total = refs[0][...]
    for ref in refs[1:-1]:
        total += ref[low : low + out.shape[0], :]
    out[...] = total


def join_body(first, second, out):
    out[: first.shape[0], :] = first[...]
    out[first.shape[0] :, :] = second[...]


class Bulk:
    def __init__(self, count, lefts, rights, pairs, after=()):
        self.bits = partners(count)
        width = 512
        part = lefts[0].shape[1] // CHUNKS
        self.rows = part * len(pairs)
        outs = [((self.rows * (hi - lo), width), F32) for lo, hi in map(slots, range(LEVELS + 1))]
        self.parts = run(
            functools.partial(outer_body, count, pairs, len(lefts), len(rights)),
            outs,
            list(lefts) + list(rights),
            after,
            [pltpu.VMEM((lefts[pair[0]].shape[1], width), F32) for pair in pairs],
            limit=16,
            macs=len(pairs) * rights[0].shape[0] * lefts[0].shape[1] * width,
        )
        self.received = []
        self.value = None

    def reduced(self, level, after=()):
        low, high = slots(level)
        if not self.received:
            return self.parts[level]
        (total,) = run(
            functools.partial(add_body, low * self.rows),
            [((self.rows * (high - low), self.parts[level].shape[1]), F32)],
            [self.parts[level]] + self.received,
            after,
            limit=8,
        )
        return total

    def send(self, after=()):
        level = len(self.received)
        total = self.reduced(level, after)
        self.received.append(with_partner(total, self.bits[level]))
        return total

    def settle(self, after=()):
        value = self.reduced(LEVELS, after)
        for even, odd in self.bits[LEVELS:]:
            other = with_partner(value, (even, odd))
            (value,) = run(
                functools.partial(add_body, 0), [(value.shape, F32)], [value, other], limit=4
            )
        self.value, self.level = value, LEVELS - 1
        return value

    def fetch(self, after=()):
        if self.level < LEVELS - 1:
            (self.value,) = run(
                join_body,
                [((2 * self.value.shape[0], self.value.shape[1]), F32)],
                [self.value, self.other],
                after,
                limit=8,
            )
        self.other = with_partner(self.value, self.bits[self.level])
        self.level -= 1
        return self.value


def unpack_body(count, width, layout, *refs):
    n_in = 2 * len(layout)
    outs, sem = refs[n_in:-1], refs[-1]
    owns = own_chunk(count), own_chunk(count, True)
    copies = []
    for piece, places in enumerate(layout):
        near, far = refs[2 * piece], refs[2 * piece + 1]
        for source, own in zip((near, far), owns):
            for j in range(CHUNKS // 2):
                chunk = jnp.bitwise_xor(own, j)
                part = source.shape[0] // (CHUNKS // 2) // len(places)
                for q, (out, k, column) in enumerate(places):
                    place = (j * len(places) + q) * part
                    rows = pl.ds(pl.multiple_of(chunk * part, part), part)
                    copies.append(
                        pltpu.make_async_copy(
                            source.at[pl.ds(place, part), :],
                            outs[out].at[k, rows, pl.ds(column, width)],
                            sem,
                        )
                    )
    for copy in copies:
        copy.start()
    for copy in copies:
        copy.wait()


def unpack(count, bulks, layout, shapes):
    operands = [value for bulk in bulks for value in (bulk.value, bulk.other)]
    anywhere = pl.BlockSpec(memory_space=pl.ANY)
    return pl.pallas_call(
        functools.partial(unpack_body, count, operands[0].shape[1], layout),
        out_shape=[jax.ShapeDtypeStruct(shape, F32) for shape in shapes],
        in_specs=[anywhere] * len(operands),
        out_specs=[anywhere] * len(shapes),
        scratch_shapes=[pltpu.SemaphoreType.DMA],
        compiler_params=pltpu.CompilerParams(vmem_limit_bytes=4 * MIB),
    )(*operands)


def steps(span, backward, body, start, unroll=8):
    def one(k, carry):
        return body(span - 1 - k if backward else k, carry)

    return lax.fori_loop(0, span, one, start, unroll=unroll)


def at(t, seqs):
    return pl.ds(pl.multiple_of(t * seqs, seqs), seqs)


def state_scan(v_ref, rel, lr, li, start, span, backward, keep=None):
    seqs, states = lr.shape

    def body(t, carry):
        re, im = carry
        vr, vi = v_ref[at(t, seqs), :states], v_ref[at(t, seqs), states:]
        next_re, next_im = mul(lr, li, re, im)
        live = rel > t
        re, im = jnp.where(live, next_re + vr, re), jnp.where(live, next_im + vi, im)
        if keep is not None:
            keep(t, re, im)
        return re, im

    return steps(span, backward, body, start)


def adjoint_scan(g_ref, rel, lr, li, start, span, backward, use=None, extra=()):
    seqs, states = lr.shape

    def body(t, carry):
        (re, im), kept = carry
        ar, ai = g_ref[at(t, seqs), :states] + re, g_ref[at(t, seqs), states:] + im
        live = rel > t
        if use is not None:
            kept = use(t, ar, ai, live, kept)
        next_re, next_im = mul(lr, -li, ar, ai)
        return (jnp.where(live, next_re, ar), jnp.where(live, next_im, ai)), kept

    return steps(span, backward, body, (start, extra))


def wide(ref, row, shape):
    return jnp.broadcast_to(ref[row : row + 1, :], shape)


def to_time_major(piece):
    seqs, span, width = piece.shape
    return jnp.swapaxes(piece, 0, 1).reshape(span * seqs, width)


def from_time_major(rows, seqs):
    return jnp.swapaxes(rows.reshape(-1, seqs, rows.shape[-1]), 0, 1)


def lane_tiled(column, width):
    return jnp.concatenate([column] * (width // LANES), axis=1)


def gelu_parts(y):
    cdf = 0.5 * (1.0 + lax.erf(y * inverse_root_two))
    pdf = jnp.exp(-0.5 * y * y) * density_scale
    return y * cdf, cdf + y * pdf


def sigmoid(x):
    return 1.0 / (1.0 + jnp.exp(-x))


CHUNK = 16


def prepare_body(plan, span, lens_ref, x_ref, nu_ref, phase_ref, gamma_ref, *outs):
    sums_ref, tm_ref, mask_ref, decay_ref = outs[:4]
    factor_refs = outs[4:]
    seqs, _, width = x_ref.shape
    states = nu_ref.shape[-1]
    here = lax.axis_index("tm")
    rel = jnp.broadcast_to(lens_ref[...] - here * span, (seqs, LANES))
    first = jnp.zeros((seqs, width), F32)
    second = jnp.zeros((seqs, width), F32)
    for t0 in range(0, span, 8):
        piece = jnp.swapaxes(x_ref[:, t0 : t0 + 8, :], 0, 1)
        for j in range(8):
            rows = piece[j]
            mask = jnp.where(rel > t0 + j, 1.0, 0.0)
            place = slice((t0 + j) * seqs, (t0 + j + 1) * seqs)
            mask_ref[place, :] = mask
            tm_ref[place, :] = rows
            live = rows * lane_tiled(mask, width)
            first += live
            second += live * rows
    spread(sums_ref, jnp.sum(first, 0, keepdims=True), jnp.sum(second, 0, keepdims=True))
    rate = jnp.exp(nu_ref[...])
    radius = jnp.exp(-rate)
    angle = phase_ref[...]
    cosine, sine = jnp.cos(angle), jnp.sin(angle)
    gamma = gamma_ref[...]
    for row, value in enumerate((radius * cosine, radius * sine, gamma, rate, radius, cosine, sine)):
        for k in range(2):
            decay_ref[k, row : row + 1, :] = value[k : k + 1, :]
    for k in range(2):
        for level, (radix, stride) in enumerate(plan):
            base = lax.div(here, radix * stride) * (radix * stride)
            for member in range(radix):
                start = (base + member * stride) * span
                count = jnp.clip(lens_ref[...] - start, 0, stride * span)
                count = jnp.broadcast_to(count, (seqs, states))
                power = (decay_ref[k, 0:1, :], decay_ref[k, 1:2, :])
                re, im = jnp.ones((seqs, states), F32), jnp.zeros((seqs, states), F32)
                for bit in range((span * stride).bit_length()):
                    taken = jnp.bitwise_and(count, 1 << bit) != 0
                    next_re, next_im = mul(re, im, *power)
                    re, im = jnp.where(taken, next_re, re), jnp.where(taken, next_im, im)
                    power = mul(*power, *power)
                factor_refs[level][k, member, :, :states] = re
                factor_refs[level][k, member, :, states:] = im


def relative(lens_ref, span, states):
    return jnp.broadcast_to(
        lens_ref[...] - lax.axis_index("tm") * span, (lens_ref.shape[0], states)
    )


def token_scale(lens_ref):
    return 1.0 / jnp.sum(lens_ref[...].astype(F32), axis=0, keepdims=True)


def project_body(
    k, span, backward, lens_ref, sums_ref, x_ref, gain_ref, bias_ref, w_ref, decay_ref,
    u_ref, v_ref, stats_ref, summary_ref,
):
    seqs = lens_ref.shape[0]
    states = decay_ref.shape[-1]
    total, squares = gathered(sums_ref)
    scale = token_scale(lens_ref)
    mean = total * scale
    var = squares * scale - mean * mean
    rstd = lax.rsqrt(var + norm_epsilon)
    stats_ref[0:1, :] = mean
    stats_ref[1:2, :] = var
    stats_ref[2:3, :] = rstd
    stats_ref[3:4, :] = rstd * gain_ref[k : k + 1, :]
    slope = rstd * gain_ref[k : k + 1, :]
    bias = bias_ref[k : k + 1, :]
    step = CHUNK * seqs
    for r in range(0, span * seqs, step):
        u = ((x_ref[r : r + step, :] - mean) * slope + bias).astype(BF16)
        u_ref[r : r + step, :] = u
        v_ref[r : r + step, :] = dot(u, w_ref[k])
    shape = (seqs, states)
    rel = relative(lens_ref, span, states)
    lr, li = wide(decay_ref.at[k], 0, shape), wide(decay_ref.at[k], 1, shape)
    zero = jnp.zeros(shape, F32)
    re, im = state_scan(v_ref, rel, lr, li, (zero, zero), span, backward)
    summary_ref[:, :states] = re
    summary_ref[:, states:] = im


def rebuild_states(k, plan, span, backward, refs, buffers, rel, v_ref, decay_ref, h_ref):
    seqs, states = rel.shape
    lr, li, gamma = (wide(decay_ref.at[k], row, rel.shape) for row in range(3))
    start = entering_state(k, plan, refs, buffers, backward, False)

    lead = 0 if backward else 1

    def keep(t, re, im):
        h_ref[at(t + lead, seqs), :states] = (re * gamma).astype(BF16)
        h_ref[at(t + lead, seqs), states:] = (im * gamma).astype(BF16)

    keep(span if backward else -1, *start)
    state_scan(v_ref, rel, lr, li, start, span, backward, keep)


def forward_body(
    k, plan, span, exch, lens_ref, v_ref, x_ref, mask_ref, stats_ref, bias_ref,
    decay_ref, w_out_ref, skip_ref, w_glu_ref,
    out_ref, h_ref, act_ref, slope_ref, gate_ref, value_ref, sums_ref, buffers,
):
    seqs = lens_ref.shape[0]
    width = x_ref.shape[1]
    states = decay_ref.shape[-1]
    rel = relative(lens_ref, span, states)
    rebuild_states(k, plan, span, False, exch, buffers, rel, v_ref, decay_ref, h_ref)
    mean, scale = stats_ref[0:1, :], stats_ref[3:4, :]
    bias, skip = bias_ref[k : k + 1, :], skip_ref[k : k + 1, :]
    step = CHUNK * seqs
    first = jnp.zeros((8, width), F32)
    second = jnp.zeros((8, width), F32)
    for r in range(0, span * seqs, step):
        x = x_ref[r : r + step, :]
        u = (x - mean) * scale + bias
        y = dot(h_ref[r + seqs : r + seqs + step, :], w_out_ref[k]) + skip * u
        act, slope = gelu_parts(y)
        act = act.astype(BF16)
        act_ref[r : r + step, :] = act
        slope_ref[r : r + step, :] = slope.astype(BF16)
        z = dot(act, w_glu_ref[k])
        value, gate = z[:, :width], sigmoid(z[:, width:])
        gated = value * gate
        out = x + gated
        out_ref[r : r + step, :] = out
        gate_ref[r : r + step, :] = gate.astype(BF16)
        value_ref[r : r + step, :] = (gated * (1.0 - gate)).astype(BF16)
        live = out * lane_tiled(mask_ref[r : r + step, :], width)
        first += jnp.sum(live.reshape(-1, 8, width), 0)
        second += jnp.sum((live * out).reshape(-1, 8, width), 0)
    spread(sums_ref, jnp.sum(first, 0, keepdims=True), jnp.sum(second, 0, keepdims=True))


def back_rows(k, r, step, dza, dzb, slope, width, w_glu_ref, w_out_ref, dz_ref, dy_ref, g_ref):
    dza, dzb = dza.astype(BF16), dzb.astype(BF16)
    dz_ref[r : r + step, :width] = dza
    dz_ref[r : r + step, width:] = dzb
    w = w_glu_ref[k]
    dact = dot_nt(dza, w[:, :width]) + dot_nt(dzb, w[:, width:])
    dy = (dact * slope).astype(BF16)
    dy_ref[r : r + step, :] = dy
    g_ref[r : r + step, :] = dot_nt(dy, w_out_ref[k])


def local_adjoint(k, span, backward, rel, g_ref, decay_ref, summary_ref):
    seqs, states = rel.shape
    lr, li = wide(decay_ref.at[k], 0, rel.shape), wide(decay_ref.at[k], 1, rel.shape)
    zero = jnp.zeros(rel.shape, F32)
    (re, im), _ = adjoint_scan(g_ref, rel, lr, li, (zero, zero), span, backward)
    summary_ref[:, :states] = re
    summary_ref[:, states:] = im


def turn_body(
    k, plan, span, exch, lens_ref, v_ref, x_ref, cot_ref, stats_ref, bias_ref,
    decay_ref, w_out_ref, skip_ref, w_glu_ref,
    out_ref, h_ref, act_ref, dz_ref, dy_ref, g_ref, summary_ref, buffers,
):
    seqs = lens_ref.shape[0]
    width = x_ref.shape[1]
    states = decay_ref.shape[-1]
    rel = relative(lens_ref, span, states)
    rebuild_states(k, plan, span, True, exch, buffers, rel, v_ref, decay_ref, h_ref)
    mean, scale = stats_ref[0:1, :], stats_ref[3:4, :]
    bias, skip = bias_ref[k : k + 1, :], skip_ref[k : k + 1, :]
    step = CHUNK * seqs
    for r in range(0, span * seqs, step):
        t0 = r // seqs
        x = x_ref[r : r + step, :]
        u = (x - mean) * scale + bias
        y = dot(h_ref[r : r + step, :], w_out_ref[k]) + skip * u
        act, slope = gelu_parts(y)
        act = act.astype(BF16)
        act_ref[r : r + step, :] = act
        z = dot(act, w_glu_ref[k])
        value, gate = z[:, :width], sigmoid(z[:, width:])
        gated = value * gate
        out_ref[:, t0 : t0 + CHUNK, :] = from_time_major(x + gated, seqs)
        d = to_time_major(cot_ref[:, t0 : t0 + CHUNK, :])
        back_rows(
            k, r, step, d * gate, d * (gated * (1.0 - gate)), slope, width,
            w_glu_ref, w_out_ref, dz_ref, dy_ref, g_ref,
        )
    local_adjoint(k, span, False, rel, g_ref, decay_ref, summary_ref)


def back_body(
    k, span, backward, lens_ref, sums_ref, part_ref, x_ref, mask_ref, stats_ref, slope_ref,
    gate_ref, value_ref, gain_ref, decay_ref, w_out_ref, w_glu_ref,
    d_ref, dz_ref, dy_ref, g_ref, grads_ref, summary_ref,
):
    seqs = lens_ref.shape[0]
    width = x_ref.shape[1]
    states = decay_ref.shape[-1]
    rel = relative(lens_ref, span, states)
    shift, tilt = input_terms(k + 1, token_scale(lens_ref), sums_ref, stats_ref, gain_ref, grads_ref)
    mean = stats_ref[0:1, :]
    step = CHUNK * seqs
    for r in range(0, span * seqs, step):
        live = lane_tiled(mask_ref[r : r + step, :], width)
        d = part_ref[r : r + step, :] + live * (shift + tilt * (x_ref[r : r + step, :] - mean))
        d_ref[r : r + step, :] = d
        back_rows(
            k, r, step, d * gate_ref[r : r + step, :].astype(F32),
            d * value_ref[r : r + step, :].astype(F32), slope_ref[r : r + step, :].astype(F32), width,
            w_glu_ref, w_out_ref, dz_ref, dy_ref, g_ref,
        )
    local_adjoint(k, span, backward, rel, g_ref, decay_ref, summary_ref)


def input_terms(k, scale, sums_ref, stats_ref, gain_ref, grads_ref):
    bias_grad, gain_grad = gathered(sums_ref)
    grads_ref[0:1, :] = gain_grad
    grads_ref[1:2, :] = bias_grad
    rstd = stats_ref[2:3, :]
    gain = gain_ref[k : k + 1, :]
    return -rstd * gain * bias_grad * scale, -rstd * rstd * gain * gain_grad * scale


def adjoint_body(
    k, plan, span, backward, exch, lens_ref, g_ref, h_ref, v_ref, decay_ref, dv_ref, small_ref, buffers
):
    seqs = lens_ref.shape[0]
    states = decay_ref.shape[-1]
    rel = relative(lens_ref, span, states)
    lr, li, gamma = (wide(decay_ref.at[k], row, rel.shape) for row in range(3))
    start = entering_state(k, plan, exch, buffers, backward, True)
    before = 0 if backward else 1

    def use(t, ar, ai, live, kept):
        ar, ai = jnp.where(live, ar, 0.0), jnp.where(live, ai, 0.0)
        dv_ref[at(t, seqs), :states] = (ar * gamma).astype(BF16)
        dv_ref[at(t, seqs), states:] = (ai * gamma).astype(BF16)
        pr = h_ref[at(t + before, seqs), :states].astype(F32)
        pi = h_ref[at(t + before, seqs), states:].astype(F32)
        vr, vi = v_ref[at(t, seqs), :states], v_ref[at(t, seqs), states:]
        return (
            kept[0] + (ar * pr + ai * pi),
            kept[1] + (ai * pr - ar * pi),
            kept[2] + (ar * vr + ai * vi),
        )

    zero = jnp.zeros(rel.shape, F32)
    _, kept = adjoint_scan(g_ref, rel, lr, li, start, span, backward, use, (zero, zero, zero))
    small_ref[...] = jnp.zeros_like(small_ref)
    for j in range(2):
        small_ref[0:1, j * states : (j + 1) * states] = jnp.sum(kept[j], 0, keepdims=True)
    small_ref[1:2, :states] = jnp.sum(kept[2], 0, keepdims=True)


def input_body(
    k, seq_major, dv_ref, dy_ref, x_ref, d_ref, stats_ref, gain_ref, bias_ref, w_in_ref, skip_ref,
    part_ref, skip_grad_ref, sums_ref,
):
    width = x_ref.shape[1]
    seqs = CHUNK
    mean, scale, rstd = stats_ref[0:1, :], stats_ref[3:4, :], stats_ref[2:3, :]
    gain, bias, skip = (ref[k : k + 1, :] for ref in (gain_ref, bias_ref, skip_ref))
    if seq_major:
        seqs = d_ref.shape[0]
    step = CHUNK * seqs
    first = jnp.zeros((8, width), F32)
    second = jnp.zeros((8, width), F32)
    third = jnp.zeros((8, width), F32)
    for r in range(0, x_ref.shape[0], step):
        xhat = (x_ref[r : r + step, :] - mean) * rstd
        dy = dy_ref[r : r + step, :].astype(F32)
        du = dot_nt(dv_ref[r : r + step, :], w_in_ref[k]) + dy * skip
        first += jnp.sum(du.reshape(-1, 8, width), 0)
        second += jnp.sum((du * xhat).reshape(-1, 8, width), 0)
        third += jnp.sum((dy * (xhat * gain + bias)).reshape(-1, 8, width), 0)
        if seq_major:
            d = to_time_major(d_ref[:, r // seqs : r // seqs + CHUNK, :])
        else:
            d = d_ref[r : r + step, :]
        part_ref[r : r + step, :] = d + du * scale
    spread(sums_ref, jnp.sum(first, 0, keepdims=True), jnp.sum(second, 0, keepdims=True))
    skip_grad_ref[...] = third


def finish_body(
    k, span, lens_ref, sums_ref, part_ref, x_ref, mask_ref, stats_ref, gain_ref, out_ref, grads_ref
):
    seqs = out_ref.shape[0]
    width = x_ref.shape[1]
    scale = token_scale(lens_ref)
    shift, tilt = input_terms(k, scale, sums_ref, stats_ref, gain_ref, grads_ref)
    mean = stats_ref[0:1, :]
    step = CHUNK * seqs
    for r in range(0, span * seqs, step):
        live = lane_tiled(mask_ref[r : r + step, :], width)
        d = part_ref[r : r + step, :] + live * (shift + tilt * (x_ref[r : r + step, :] - mean))
        out_ref[:, r // seqs : r // seqs + CHUNK, :] = from_time_major(d, seqs)


def small_body(refs_per_block, *refs):
    out = refs[-1]
    out[...] = jnp.zeros_like(out)
    for k in range(2):
        small, skip_grad = refs[2 * k], refs[2 * k + 1]
        out[8 * k : 8 * k + 2, :] = small[0:2, :]
        out[8 * k + 2 : 8 * k + 3, :] = jnp.sum(skip_grad[...], 0, keepdims=True)


def sum_body(*refs):
    total = refs[0][...]
    for ref in refs[1:-1]:
        total += ref[...]
    refs[-1][...] = total


def results_body(n_parts, *refs):
    parts, rest = refs[:n_parts], refs[n_parts:]
    lens_ref, decay_ref, running_ref = rest[:3]
    stats_refs, grads_refs = rest[3:5], rest[5:7]
    gain_ref, bias_ref, nu_ref, phase_ref, skip_ref, run_ref = rest[7:]
    small = parts[0][...]
    for ref in parts[1:]:
        small += ref[...]
    states = decay_ref.shape[-1]
    count = jnp.sum(lens_ref[...].astype(F32), axis=0, keepdims=True)
    for k in range(2):
        _, _, gamma, rate, radius, cosine, sine = (decay_ref[k, j : j + 1, :] for j in range(7))
        sum_re, sum_im = small[8 * k : 8 * k + 1, :states], small[8 * k : 8 * k + 1, states:]
        g_gamma = small[8 * k + 1 : 8 * k + 2, :states]
        nu_ref[k : k + 1, :] = (sum_re * cosine + sum_im * sine) * (
            -radius * rate
        ) + g_gamma * rate * radius * radius / gamma
        phase_ref[k : k + 1, :] = radius * (sum_im * cosine - sum_re * sine)
        skip_ref[k : k + 1, :] = small[8 * k + 2 : 8 * k + 3, :]
        gain_ref[k : k + 1, :] = grads_refs[k][0:1, :]
        bias_ref[k : k + 1, :] = grads_refs[k][1:2, :]
        mean, var = stats_refs[k][0:1, :], stats_refs[k][1:2, :]
        run_ref[k, 0:1, :] = (1.0 - momentum) * running_ref[k, 0:1, :] + momentum * mean
        run_ref[k, 1:2, :] = (1.0 - momentum) * running_ref[k, 1:2, :] + momentum * var * (
            count / (count - 1.0)
        )


def with_entry(body, plan):
    def wrapped(*refs):
        n_exch = sum(radix for radix, _ in plan) + len(plan)
        body(refs[:n_exch], *refs[n_exch : -len(plan)], refs[-len(plan) :])

    return wrapped


def shards(
    inputs, lengths, cotangent, bn_gain, bn_bias, running, w_in, nu_log, phase, w_out, skip, w_glu
):
    seqs, span, width = inputs.shape
    states = nu_log.shape[1]
    count = lax.axis_size("tm")
    rows = span * seqs
    plan = stages(count)
    lens = lengths[:, None]

    tile = ((count, 2 * width // LANES, LANES), F32)
    whole, whole_low = ((rows, width), F32), ((rows, width), BF16)
    pair, pair_low = ((rows, 2 * states), F32), ((rows, 2 * states), BF16)
    double_low = ((rows, 2 * width), BF16)
    held_low = ((rows + seqs, 2 * states), BF16)
    summary = ((seqs, 2 * states), F32)
    eight = ((8, width), F32)
    seq_major = ((seqs, span, width), F32)
    buffers = entry_scratch(plan, summary[0])

    prepared = run(
        functools.partial(prepare_body, plan, span),
        [tile, whole, ((rows, LANES), F32), ((2, 8, states), F32)]
        + [((2, radix) + summary[0], F32) for radix, _ in plan],
        [lens, inputs, nu_log, phase, jnp.sqrt(-jnp.expm1(-2.0 * jnp.exp(nu_log)))],
    )
    sums, x0, mask, decay = prepared[:4]
    factors = prepared[4:]

    def project(k, sums, x):
        return run(
            functools.partial(project_body, k, span, k == 1),
            [whole_low, pair, eight, summary],
            [lens, everywhere(sums), x, bn_gain, bn_bias, w_in, decay],
        )

    def entered(body, outs, held, operands, after=(), limit=12):
        operands = entry_operands(held, factors) + operands
        return run(with_entry(body, plan), outs, operands, after, buffers, limit)

    u0, v0, stats0, part = project(0, sums, x0)
    held = exchange(0, part, plan, factors, False, False)
    x1, h0, act0, slope0, gate0, value0, sums = entered(
        functools.partial(forward_body, 0, plan, span),
        [whole, held_low, whole_low, whole_low, whole_low, whole_low, tile],
        held,
        [lens, v0, x0, mask, stats0, bn_bias, decay, w_out, skip, w_glu],
    )
    u1, v1, stats1, part = project(1, sums, x1)
    held = exchange(1, part, plan, factors, True, False)
    output, h1, act1, dz1, dy1, g1, part = entered(
        functools.partial(turn_body, 1, plan, span),
        [seq_major, held_low, whole_low, double_low, whole_low, pair, summary],
        held,
        [lens, v1, x1, cotangent, stats1, bn_bias, decay, w_out, skip, w_glu],
    )

    flows = {}

    def beside_top(level, value):
        if level == 1:
            flows["top"] = Bulk(
                count, [act1, h1], [dz1, dy1], [(0, 0, 0, 0), (0, 0, 0, width), (1, 0, 1, 0)], [value]
            )
            flows["top"].send()
            return flows["top"].parts[-1:]
        if level == len(plan) - 1:
            flows["step"] = flows["top"].send([value])
        return ()

    held = exchange(1, part, plan, factors, False, True, beside_top)
    top = flows["top"]
    dv1, small1 = entered(
        functools.partial(adjoint_body, 1, plan, span, False),
        [pair_low, eight],
        held,
        [lens, g1, h1, v1, decay],
        [flows["step"]],
    )
    step = top.send([dv1])
    part1, skip1, sums = run(
        functools.partial(input_body, 1, True),
        [whole, eight, tile],
        [dv1, dy1, x1, cotangent, stats1, bn_gain, bn_bias, w_in, skip],
        [step],
        macs=rows * width * 2 * states,
    )
    sums = everywhere(sums)
    step = top.send([sums])
    d0, dz0, dy0, g0, grads1, part = run(
        functools.partial(back_body, 0, span, True),
        [whole, double_low, whole_low, pair, eight, summary],
        [lens, sums, part1, x1, mask, stats1, slope0, gate0, value0, bn_gain, decay, w_out, w_glu],
        [step],
        macs=rows * width * (2 * width + 2 * states),
    )

    def beside_middle(level, value):
        if level == 1:
            step = top.send([value])
            flows["middle"] = Bulk(
                count,
                [u1, act0, h0],
                [dv1, dz0, dy0],
                [(0, 0, 0, 0), (1, 0, 1, 0), (1, 0, 1, width), (2, seqs, 2, 0)],
                [step],
            )
            flows["middle"].send()
            return flows["middle"].parts[-1:]
        if level == len(plan) - 1:
            flows["step"] = flows["middle"].send([value])
        return ()

    held = exchange(0, part, plan, factors, True, True, beside_middle)
    middle = flows["middle"]
    dv0, small0 = entered(
        functools.partial(adjoint_body, 0, plan, span, True),
        [pair_low, eight],
        held,
        [lens, g0, h0, v0, decay],
        [flows["step"]],
    )
    own = top.settle([dv0])
    top.fetch()
    part0, skip0, sums = run(
        functools.partial(input_body, 0, False),
        [whole, eight, tile],
        [dv0, dy0, x0, d0, stats0, bn_gain, bn_bias, w_in, skip],
        [own],
        macs=rows * width * 2 * states,
    )
    step = middle.send([sums])
    sums = everywhere(sums)
    grad_x, grads0 = run(
        functools.partial(finish_body, 0, span),
        [seq_major, eight],
        [lens, sums, part0, x0, mask, stats0, bn_gain],
    )

    last = Bulk(count, [u0], [dv0], [(0, 0, 0, 0)], [sums])
    last.send()
    step = middle.send([last.parts[-1]])
    step = top.fetch([step])
    (small,) = run(
        functools.partial(small_body, 2), [((16, width), F32)], [small0, skip0, small1, skip1], [step]
    )
    step = last.send([small])
    step = top.fetch([step])
    step = middle.send([step])
    group = group_of(small, *plan[0])
    (small,) = run(sum_body, [((16, width), F32)], group, [step], limit=4)
    step = last.send([small])
    step = top.fetch([step])
    step = middle.settle([step])
    middle.fetch()
    step = last.send([step])
    group = group_of(small, *plan[1])
    (small,) = run(sum_body, [((16, width), F32)], group, [step], limit=4)
    step = middle.fetch([small])
    step = last.send([step])
    for stage in plan[2:]:
        group = group_of(small, *stage)
        if stage != plan[-1]:
            (small,) = run(sum_body, [((16, width), F32)], group, [step], limit=4)
    step = middle.fetch([step])
    step = top.fetch([step])
    step = last.settle([step])
    last.fetch()
    step = last.fetch([step])
    g_gain, g_bias, g_nu, g_phase, g_skip, running_out = run(
        functools.partial(results_body, len(group)),
        [((2, width), F32)] * 2 + [((2, states), F32)] * 2 + [((2, width), F32), ((2, 2, width), F32)],
        list(group) + [lens, decay, running, stats0, stats1, grads0, grads1],
        [step],
    )
    step = middle.fetch([step])
    step = last.fetch([step])
    step = last.fetch([step])
    step = middle.fetch([step])
    step = last.fetch([step])
    g_glu, g_out, g_in = unpack(
        count,
        [top, middle, last],
        [
            [(0, 1, 0), (0, 1, width), (1, 1, 0)],
            [(2, 1, 0), (0, 0, 0), (0, 0, width), (1, 0, 0)],
            [(2, 0, 0)],
        ],
        [(2, width, 2 * width), (2, 2 * states, width), (2, width, 2 * states)],
    )
    return (output, grad_x, g_gain, g_bias, g_in, g_nu, g_phase, g_out, g_skip, g_glu, running_out)


def solution(mesh):
    placed = (P(None, "tm", None), P(), P(None, "tm", None)) + (P(),) * 9
    return jax.shard_map(
        shards,
        mesh=mesh,
        in_specs=placed,
        out_specs=(P(None, "tm", None),) * 2 + (P(),) * 9,
        check_vma=False,
    )
```

time: 389 us -> 256 us (0.66)
  waiting for transfers between devices: 158 us -> 94.1 us
  local copies, waits for them, and re-layouts: 40.3 us -> 11.1 us
  starting transfers between devices: 47 us -> 64.5 us
  blocking collectives: 54.1 us -> 38.1 us
  between operations: 15.4 us -> 1.51 us
  matrix products: 10.3 us -> 0 us
  other arithmetic: 9.57 us -> 0.79 us
  Pallas kernels: 53 us -> 45.8 us
    psum x1 -> x0, waiting for transfers between devices: 128 us -> none  [shards(): lax.psum((jnp.stack([outer(act0, dz0), outer(act1, dz1)]), jnp.stack([out...]
    ppermute x0 -> x30, waiting for transfers between devices: none -> 57.5 us  [with_partner(): lax.ppermute(value, 'tm', [(i, i ^ (odd if i & 1 else even)) for i in ran...]
    psum x1 -> x0, blocking collectives: 42.6 us -> none  [shards(): lax.psum((jnp.stack([outer(act0, dz0), outer(act1, dz1)]), jnp.stack([out...]
    unnamed x146 -> x82, local copies, waits for them, and re-layouts: 38.7 us -> 10.3 us
    all_to_all x1 -> x3, blocking collectives: 11.5 us -> 38.1 us  [everywhere(): return lax.all_to_all(tiles, 'tm', 0, 0)]
    ppermute x0 -> x30, starting transfers between devices: none -> 23.5 us  [with_partner(): lax.ppermute(value, 'tm', [(i, i ^ (odd if i & 1 else even)) for i in ran...]
    ppermute x28 -> x35, waiting for transfers between devices: 17.5 us -> 34.2 us  [swap(): lax.ppermute(value, 'tm', [(i, i ^ stride * mask) for i in range(count)])]
    all_to_all x3 -> x1, starting transfers between devices: 14.1 us -> 2.92 us  [everywhere(): return lax.all_to_all(tiles, 'tm', 0, 0)]
  transfers between devices with their start and end apart: 32 -> 66, of which waited for: 21 -> 47; matrix products, arithmetic and copies ran while one was open for 4% -> 0% of each run, Pallas kernels for 1% -> 8%
where the time goes in v1:
time: 256 us
  waiting for transfers between devices  94.1 us (37%)
  starting transfers between devices  64.5 us (25%)
  Pallas kernels  45.8 us (18%)
  blocking collectives  38.1 us (15%)
  local copies, waits for them, and re-layouts  11.1 us (4%)
    ppermute x30, waiting for transfers between devices, with_partner(): lax.ppermute(value, 'tm', [(i, i ^ (odd if i & 1 else even)) for i in ran...  57.5 us
    pallas_call x53, Pallas kernels, run(): pl.pallas_call(kernel, out_shape=[jax.ShapeDtypeStruct(shape, dtype) for...  42.6 us
    all_to_all x3, blocking collectives, everywhere(): return lax.all_to_all(tiles, 'tm', 0, 0)  38.1 us
    ppermute x35, starting transfers between devices, swap(): lax.ppermute(value, 'tm', [(i, i ^ stride * mask) for i in range(count)])  38.1 us
    ppermute x35, waiting for transfers between devices, swap(): lax.ppermute(value, 'tm', [(i, i ^ stride * mask) for i in range(count)])  34.2 us
    ppermute x30, starting transfers between devices, with_partner(): lax.ppermute(value, 'tm', [(i, i ^ (odd if i & 1 else even)) for i in ran...  23.5 us
    unnamed x82, local copies, waits for them, and re-layouts  10.3 us
  transfers between devices with their start and end apart: 66, of which 47 were waited for; matrix products, arithmetic and copies ran while one was open for 0% of the time, Pallas kernels for 8%

profile of v1, /device:TPU:0, one launch (start us, length us, event | category | flops | bytes accessed | tf_op | source)
XLA Modules:
  0.0 255.9 jit_solution(14770607780703357978)
XLA Ops:
  6.9 15.3 %all_to_all.20.refs_1_ = f32[32,8,128]{2,1,0:T(8,128)S(1)} all-to-all(f32[32,8,128]{2,1,0:T(8,128)S(1)} %get-tuple-element.85), channel_id=1, replica_groups=mesh['tm'=32] {'tm'}, dimensions={0} | all-to-all | bytes 262144 | tf_op jit(solution)/shard_map/all_to_all | solution.py:110
  32.6 2.5 collective-permute-start.4
  37.4 4.4 %shard_map.207 = (f32[1024,512]{1,0:T(8,128)S(1)}, bf16[1040,512]{1,0:T(8,128)(2,1)S(1)}, bf16[1024,512]{1,0:T(8,128)(2,1)S(1)}, bf16[1024,512]{1,0:T(8,128)(2,1...) custom-call(f32[16,512]{1,0:T(8,128)S(1)} %get-tuple-element.88.refs_0_, ...), custom_call_target="tpu_custom_call" | custom-call | bytes 16375872 | tf_op jit(solution)/shard_map/pallas_call | solution.py:40
  41.8 11.6 %all_to_all.21.refs_1_ = f32[32,8,128]{2,1,0:T(8,128)S(1)} all-to-all(f32[32,8,128]{2,1,0:T(8,128)S(1)} %get-tuple-element.95), channel_id=1, replica_groups=mesh['tm'=32] {'tm'}, dimensions={0} | all-to-all | bytes 262144 | tf_op jit(solution)/shard_map/all_to_all | solution.py:110
  63.8 2.5 collective-permute-start.11
  68.5 8.4 %shard_map.211 = (f32[16,64,512]{2,1,0:T(8,128)}, bf16[1040,512]{1,0:T(8,128)(2,1)S(1)}, bf16[1024,512]{1,0:T(8,128)(2,1)S(1)}, bf16[1024,1024]{1,0:T(8,128)(2,1...) custom-call(f32[16,512]{1,0:T(8,128)S(1)} %get-tuple-element.97.refs_0_, ...), custom_call_target="tpu_custom_call" | custom-call | bytes 19947584 | tf_op jit(solution)/shard_map/pallas_call | solution.py:40
  96.4 3.1 %collective-permute-done.22.refs_2_ = f32[384,512]{1,0:T(8,128)S(1)} collective-permute-done((f32[384,512]{1,0:T(8,128)S(1)}, f32[384,512]{1,0:T(8,128)S(1)}, u32[]{:S(2)}, u32[]{:S(2)}) %collective-permute-start.22) | collective-permute-done | bytes 786464 | tf_op jit(solution)/shard_map/ppermute | solution.py:212
  102.2 11.2 %all_to_all.22.refs_4_.refs_1_ = f32[32,8,128]{2,1,0:T(8,128)S(1)} all-to-all(f32[32,8,128]{2,1,0:T(8,128)S(1)} %get-tuple-element.112), channel_id=1, replica_groups=mesh['tm'=32] {'tm'}, dimensions={0} | all-to-all | bytes 262144 | tf_op jit(solution)/shard_map/all_to_all | solution.py:110
  114.2 2.9 %shard_map.220 = (f32[1024,512]{1,0:T(8,128)S(1)}, bf16[1024,1024]{1,0:T(8,128)(2,1)S(1)}, bf16[1024,512]{1,0:T(8,128)(2,1)S(1)}, f32[1024,512]{1,0:T(8,128)S(1)...) custom-call(s32[16,1]{1,0:T(8,128)S(1)} %copy.26.refs_0_.refs_13_.refs_4_, f32[32,8,128]{2,1,0:T(8,128)S(1)} %all_to_all.22.refs_4_.refs_1_, ...), custom_call_target="tpu_custom_call" | custom-call | flops 1610612736 | bytes 18567232 | tf_op jit(solution)/shard_map/pallas_call | solution.py:40
  120.6 2.5 shard_map.223
  132.2 2.4 collective-permute-start.31
  138.1 2.3 collective-permute-done.30.refs_8_
  146.6 2.9 %all-to-all-start.3 = ((f32[32,8,128]{2,1,0:T(8,128)}), f32[32,8,128]{2,1,0:T(8,128)S(1)}, u32[]{:S(2)}, u32[]{:S(2)}) async-start(f32[32,8,128]{2,1,0:T(8,128)} %copy-done.17), calls=%async_computation.3 | async-start | bytes 262144 | tf_op jit(solution)/shard_map/all_to_all | solution.py:110
  151.5 2.2 shard_map.230
  155.2 2.4 all-to-all-done.3.refs_1_.refs_2_
  160.5 2.8 %collective-permute-done.36.refs_3_ = f32[256,512]{1,0:T(8,128)} collective-permute-done((f32[256,512]{1,0:T(8,128)}, f32[256,512]{1,0:T(8,128)}, u32[]{:S(2)}, u32[]{:S(2)}) %collective-permute-start.36) | collective-permute-done | bytes 524320 | tf_op jit(solution)/shard_map/ppermute | solution.py:212
  164.7 3.2 %collective-permute-done.34.refs_1_ = f32[48,512]{1,0:T(8,128)S(1)} collective-permute-done((f32[48,512]{1,0:T(8,128)S(1)}, f32[48,512]{1,0:T(8,128)S(1)}, u32[]{:S(2)}, u32[]{:S(2)}) %collective-permute-start.34) | collective-permute-done | bytes 98336 | tf_op jit(solution)/shard_map/ppermute | solution.py:212
  170.1 5.7 %collective-permute-done.39.refs_1_ = f32[96,512]{1,0:T(8,128)S(1)} collective-permute-done((f32[96,512]{1,0:T(8,128)S(1)}, f32[96,512]{1,0:T(8,128)S(1)}, u32[]{:S(2)}, u32[]{:S(2)}) %collective-permute-start.39) | collective-permute-done | bytes 196640 | tf_op jit(solution)/shard_map/ppermute | solution.py:212
  177.2 3.2 %collective-permute-done.38.refs_4_ = f32[128,512]{1,0:T(8,128)S(1)} collective-permute-done((f32[128,512]{1,0:T(8,128)S(1)}, f32[128,512]{1,0:T(8,128)S(1)}, u32[]{:S(2)}, u32[]{:S(2)}) %collective-permute-start.38) | collective-permute-done | bytes 262176 | tf_op jit(solution)/shard_map/ppermute | solution.py:212
  184.6 5.5 %collective-permute-done.46.refs_5_ = f32[64,512]{1,0:T(8,128)S(1)} collective-permute-done((f32[64,512]{1,0:T(8,128)S(1)}, f32[64,512]{1,0:T(8,128)S(1)}, u32[]{:S(2)}, u32[]{:S(2)}) %collective-permute-start.46) | collective-permute-done | bytes 131104 | tf_op jit(solution)/shard_map/ppermute | solution.py:212
  200.3 7.0 %collective-permute-done.51.refs_4_ = f32[32,512]{1,0:T(8,128)S(1)} collective-permute-done((f32[32,512]{1,0:T(8,128)S(1)}, f32[32,512]{1,0:T(8,128)S(1)}, u32[]{:S(2)}, u32[]{:S(2)}) %collective-permute-start.51) | collective-permute-done | bytes 65568 | tf_op jit(solution)/shard_map/ppermute | solution.py:212
  209.1 3.7 %collective-permute-done.53.refs_5_ = f32[16,512]{1,0:T(8,128)S(1)} collective-permute-done((f32[16,512]{1,0:T(8,128)S(1)}, f32[16,512]{1,0:T(8,128)S(1)}, u32[]{:S(2)}, u32[]{:S(2)}) %collective-permute-start.53) | collective-permute-done | bytes 32800 | tf_op jit(solution)/shard_map/ppermute | solution.py:212
  213.9 4.1 %collective-permute-done.56.refs_1_ = f32[16,512]{1,0:T(8,128)S(1)} collective-permute-done((f32[16,512]{1,0:T(8,128)S(1)}, f32[16,512]{1,0:T(8,128)S(1)}, u32[]{:S(2)}, u32[]{:S(2)}) %collective-permute-start.56) | collective-permute-done | bytes 32800 | tf_op jit(solution)/shard_map/ppermute | solution.py:212
  218.1 2.4 collective-permute-start.59
  220.7 4.1 %collective-permute-done.60.refs_1_ = f32[32,512]{1,0:T(8,128)S(1)} collective-permute-done((f32[32,512]{1,0:T(8,128)S(1)}, f32[32,512]{1,0:T(8,128)S(1)}, u32[]{:S(2)}, u32[]{:S(2)}) %collective-permute-start.60) | collective-permute-done | bytes 65568 | tf_op jit(solution)/shard_map/ppermute | solution.py:212
  226.7 4.5 %collective-permute-done.61.refs_1_ = f32[64,512]{1,0:T(8,128)S(1)} collective-permute-done((f32[64,512]{1,0:T(8,128)S(1)}, f32[64,512]{1,0:T(8,128)S(1)}, u32[]{:S(2)}, u32[]{:S(2)}) %collective-permute-start.61) | collective-permute-done | bytes 131104 | tf_op jit(solution)/shard_map/ppermute | solution.py:212
  231.2 3.4 %collective-permute-done.59.refs_1_ = f32[512,512]{1,0:T(8,128)S(1)} collective-permute-done((f32[512,512]{1,0:T(8,128)S(1)}, f32[512,512]{1,0:T(8,128)S(1)}, u32[]{:S(2)}, u32[]{:S(2)}) %collective-permute-start.59) | collective-permute-done | bytes 1048608 | tf_op jit(solution)/shard_map/ppermute | solution.py:212
  237.4 4.4 %collective-permute-done.63.refs_1_ = f32[128,512]{1,0:T(8,128)S(1)} collective-permute-done((f32[128,512]{1,0:T(8,128)S(1)}, f32[128,512]{1,0:T(8,128)S(1)}, u32[]{:S(2)}, u32[]{:S(2)}) %collective-permute-start.63) | collective-permute-done | bytes 262176 | tf_op jit(solution)/shard_map/ppermute | solution.py:212
  241.9 2.1 collective-permute-start.50
  243.9 3.9 %collective-permute-done.50.refs_3_ = f32[16,512]{1,0:T(8,128)S(1)} collective-permute-done((f32[16,512]{1,0:T(8,128)S(1)}, f32[16,512]{1,0:T(8,128)S(1)}, u32[]{:S(2)}, u32[]{:S(2)}) %collective-permute-start.50) | collective-permute-done | bytes 32800 | tf_op jit(solution)/shard_map/ppermute | solution.py:75
  247.9 2.5 shard_map.229
  252.5 3.2 %shard_map.256 = (f32[2,512,1024]{2,1,0:T(8,128)}, f32[2,512,512]{2,1,0:T(8,128)}, f32[2,512,512]{2,1,0:T(8,128)}) custom-call(f32[768,512]{1,0:T(8,128)S(1)} %shard_map.247.refs_6_.refs_0_, f32[768,512]{1,0:T(8,128)S(1)} %collective-permute-done.57.refs_1_, f32[1024,512]{1,0:T(8,128)S(1)} %shard_map.254.refs_2_, ...), custom_call_target="tpu_custom_call" | custom-call | tf_op jit(solution)/shard_map/pallas_call | solution.py:358
  (241 shorter events, 112.3 us)
Async XLA Ops:
  80.1 7.3 %collective-permute-start.21 = (f32[768,512]{1,0:T(8,128)S(1)}, f32[768,512]{1,0:T(8,128)S(1)}, u32[]{:S(2)}, u32[]{:S(2)}) collective-permute-start(f32[768,512]{1,0:T(8,128)S(1)} %get-tuple-element.109), channel_id=1, source_target_pairs={{0,1},{1,0},{2,3},{3,2},{4,5},{5,4},{6,7},{7,6},{8,9},{9,8},{10,11... | collective-permute-start | bytes 4718600 | tf_op jit(solution)/shard_map/ppermute | solution.py:212
  87.5 12.1 %collective-permute-start.22 = (f32[384,512]{1,0:T(8,128)S(1)}, f32[384,512]{1,0:T(8,128)S(1)}, u32[]{:S(2)}, u32[]{:S(2)}) collective-permute-start(f32[384,512]{1,0:T(8,128)S(1)} %shard_map.215.refs_18_), channel_id=1, source_target_pairs={{0,2},{1,5},{2,0},{3,7},{4,6},{5,1},{6,4},{7,3},{8,10},{9,13},{10,... | collective-permute-start | bytes 2359304 | tf_op jit(solution)/shard_map/ppermute | solution.py:212
  99.6 13.8 %collective-permute-start.23 = (f32[192,512]{1,0:T(8,128)S(1)}, f32[192,512]{1,0:T(8,128)S(1)}, u32[]{:S(2)}, u32[]{:S(2)}) collective-permute-start(f32[192,512]{1,0:T(8,128)S(1)} %shard_map.217.refs_9_), channel_id=1, source_target_pairs={{0,4},{1,3},{2,6},{3,1},{4,0},{5,7},{6,2},{7,5},{8,12},{9,11},{10,... | collective-permute-start | bytes 1179656 | tf_op jit(solution)/shard_map/ppermute | solution.py:212
  113.5 7.1 %collective-permute-start.28 = (f32[96,512]{1,0:T(8,128)S(1)}, f32[96,512]{1,0:T(8,128)S(1)}, u32[]{:S(2)}, u32[]{:S(2)}) collective-permute-start(f32[96,512]{1,0:T(8,128)S(1)} %shard_map.219.refs_13_), channel_id=1, source_target_pairs={{0,8},{1,9},{2,10},{3,11},{4,12},{5,13},{6,14},{7,15},{8,0},{9,1},... | collective-permute-start | bytes 589832 | tf_op jit(solution)/shard_map/ppermute | solution.py:212
  123.2 5.9 %collective-permute-start.32 = (f32[1024,512]{1,0:T(8,128)S(1)}, f32[1024,512]{1,0:T(8,128)S(1)}, u32[]{:S(2)}, u32[]{:S(2)}) collective-permute-start(f32[1024,512]{1,0:T(8,128)S(1)} %get-tuple-element.128), channel_id=1, source_target_pairs={{0,1},{1,0},{2,3},{3,2},{4,5},{5,4},{6,7},{7,6},{8,9},{9,8},{10,11... | collective-permute-start | bytes 6291464 | tf_op jit(solution)/shard_map/ppermute | solution.py:212
  130.2 19.4 %collective-permute-start.35 = (f32[512,512]{1,0:T(8,128)}, f32[512,512]{1,0:T(8,128)}, u32[]{:S(2)}, u32[]{:S(2)}) collective-permute-start(f32[512,512]{1,0:T(8,128)} %shard_map.225.refs_18_), channel_id=1, source_target_pairs={{0,2},{1,5},{2,0},{3,7},{4,6},{5,1},{6,4},{7,3},{8,10},{9,13},{10,... | collective-permute-start | bytes 3145736 | tf_op jit(solution)/shard_map/ppermute | solution.py:212
  131.9 9.7 %collective-permute-start.33 = (f32[48,512]{1,0:T(8,128)S(1)}, f32[48,512]{1,0:T(8,128)S(1)}, u32[]{:S(2)}, u32[]{:S(2)}) collective-permute-start(f32[48,512]{1,0:T(8,128)S(1)} %shard_map.222.refs_6_), channel_id=1, source_target_pairs={{0,16},{1,17},{2,18},{3,19},{4,20},{5,21},{6,22},{7,23},{8,24},{9,... | collective-permute-start | bytes 294920 | tf_op jit(solution)/shard_map/ppermute | solution.py:212
  132.2 5.9 %collective-permute-start.31 = (f32[16,512]{1,0:T(8,128)S(1)}, f32[16,512]{1,0:T(8,128)S(1)}, u32[]{:S(2)}, u32[]{:S(2)}) collective-permute-start(f32[16,512]{1,0:T(8,128)S(1)} %shard_map.224.refs_2_.refs_6_), channel_id=1, source_target_pairs={{0,24},{1,25},{2,26},{3,27},{4,28},{5,29},{6,30},{7,31},{8,16},{9,... | collective-permute-start | bytes 98312 | tf_op jit(solution)/shard_map/ppermute | solution.py:75
  134.6 5.8 %collective-permute-start.30 = (f32[16,512]{1,0:T(8,128)S(1)}, f32[16,512]{1,0:T(8,128)S(1)}, u32[]{:S(2)}, u32[]{:S(2)}) collective-permute-start(f32[16,512]{1,0:T(8,128)S(1)} %shard_map.224.refs_2_.refs_6_), channel_id=1, source_target_pairs={{0,16},{1,17},{2,18},{3,19},{4,20},{5,21},{6,22},{7,23},{8,24},{9,... | collective-permute-start | bytes 98312 | tf_op jit(solution)/shard_map/ppermute | solution.py:75
  146.6 11.0 %all-to-all-start.3 = ((f32[32,8,128]{2,1,0:T(8,128)}), f32[32,8,128]{2,1,0:T(8,128)S(1)}, u32[]{:S(2)}, u32[]{:S(2)}) async-start(f32[32,8,128]{2,1,0:T(8,128)} %copy-done.17), calls=%async_computation.3 | async-start | bytes 262144 | tf_op jit(solution)/shard_map/all_to_all | solution.py:110
  153.7 9.6 %collective-permute-start.36 = (f32[256,512]{1,0:T(8,128)}, f32[256,512]{1,0:T(8,128)}, u32[]{:S(2)}, u32[]{:S(2)}) collective-permute-start(f32[256,512]{1,0:T(8,128)} %shard_map.230), channel_id=1, source_target_pairs={{0,4},{1,3},{2,6},{3,1},{4,0},{5,7},{6,2},{7,5},{8,12},{9,11},{10,... | collective-permute-start | bytes 1572872 | tf_op jit(solution)/shard_map/ppermute | solution.py:212
  159.6 10.4 %collective-permute-start.40 = (f32[256,512]{1,0:T(8,128)S(1)}, f32[256,512]{1,0:T(8,128)S(1)}, u32[]{:S(2)}, u32[]{:S(2)}) collective-permute-start(f32[256,512]{1,0:T(8,128)S(1)} %get-tuple-element.144), channel_id=1, source_target_pairs={{0,1},{1,0},{2,3},{3,2},{4,5},{5,4},{6,7},{7,6},{8,9},{9,8},{10,11... | collective-permute-start | bytes 1572872 | tf_op jit(solution)/shard_map/ppermute | solution.py:212
  159.9 8.0 %collective-permute-start.34 = (f32[48,512]{1,0:T(8,128)S(1)}, f32[48,512]{1,0:T(8,128)S(1)}, u32[]{:S(2)}, u32[]{:S(2)}) collective-permute-start(f32[48,512]{1,0:T(8,128)S(1)} %shard_map.227.refs_9_.refs_0_), channel_id=1, source_target_pairs={{0,16},{1,17},{2,18},{3,19},{4,20},{5,21},{6,22},{7,23},{8,24},{9,... | collective-permute-start | bytes 294920 | tf_op jit(solution)/shard_map/ppermute | solution.py:212
  167.9 7.8 %collective-permute-start.39 = (f32[96,512]{1,0:T(8,128)S(1)}, f32[96,512]{1,0:T(8,128)S(1)}, u32[]{:S(2)}, u32[]{:S(2)}) collective-permute-start(f32[96,512]{1,0:T(8,128)S(1)} %shard_map.233.refs_4_.refs_0_), channel_id=1, source_target_pairs={{0,8},{1,9},{2,10},{3,11},{4,12},{5,13},{6,14},{7,15},{8,0},{9,1},... | collective-permute-start | bytes 589832 | tf_op jit(solution)/shard_map/ppermute | solution.py:212
  168.0 12.4 %collective-permute-start.38 = (f32[128,512]{1,0:T(8,128)S(1)}, f32[128,512]{1,0:T(8,128)S(1)}, u32[]{:S(2)}, u32[]{:S(2)}) collective-permute-start(f32[128,512]{1,0:T(8,128)S(1)} %shard_map.232.refs_2_), channel_id=1, source_target_pairs={{0,8},{1,9},{2,10},{3,11},{4,12},{5,13},{6,14},{7,15},{8,0},{9,1},... | collective-permute-start | bytes 786440 | tf_op jit(solution)/shard_map/ppermute | solution.py:212
  175.8 8.8 %collective-permute-start.47 = (f32[192,512]{1,0:T(8,128)S(1)}, f32[192,512]{1,0:T(8,128)S(1)}, u32[]{:S(2)}, u32[]{:S(2)}) collective-permute-start(f32[192,512]{1,0:T(8,128)S(1)} %shard_map.236.refs_5_.refs_0_), channel_id=1, source_target_pairs={{0,4},{1,3},{2,6},{3,1},{4,0},{5,7},{6,2},{7,5},{8,12},{9,11},{10,... | collective-permute-start | bytes 1179656 | tf_op jit(solution)/shard_map/ppermute | solution.py:212
  176.5 7.2 %collective-permute-start.44 = (f32[128,512]{1,0:T(8,128)S(1)}, f32[128,512]{1,0:T(8,128)S(1)}, u32[]{:S(2)}, u32[]{:S(2)}) collective-permute-start(f32[128,512]{1,0:T(8,128)S(1)} %shard_map.235.refs_2_), channel_id=1, source_target_pairs={{0,2},{1,5},{2,0},{3,7},{4,6},{5,1},{6,4},{7,3},{8,10},{9,13},{10,... | collective-permute-start | bytes 786440 | tf_op jit(solution)/shard_map/ppermute | solution.py:212
  181.8 8.3 %collective-permute-start.46 = (f32[64,512]{1,0:T(8,128)S(1)}, f32[64,512]{1,0:T(8,128)S(1)}, u32[]{:S(2)}, u32[]{:S(2)}) collective-permute-start(f32[64,512]{1,0:T(8,128)S(1)} %shard_map.237.refs_2_), channel_id=1, source_target_pairs={{0,16},{1,17},{2,18},{3,19},{4,20},{5,21},{6,22},{7,23},{8,24},{9,... | collective-permute-start | bytes 393224 | tf_op jit(solution)/shard_map/ppermute | solution.py:212
  183.7 11.5 %collective-permute-start.45 = (f32[64,512]{1,0:T(8,128)S(1)}, f32[64,512]{1,0:T(8,128)S(1)}, u32[]{:S(2)}, u32[]{:S(2)}) collective-permute-start(f32[64,512]{1,0:T(8,128)S(1)} %shard_map.239.refs_2_), channel_id=1, source_target_pairs={{0,4},{1,3},{2,6},{3,1},{4,0},{5,7},{6,2},{7,5},{8,12},{9,11},{10,... | collective-permute-start | bytes 393224 | tf_op jit(solution)/shard_map/ppermute | solution.py:212
  191.6 6.6 %collective-permute-start.52 = (f32[64,512]{1,0:T(8,128)S(1)}, f32[64,512]{1,0:T(8,128)S(1)}, u32[]{:S(2)}, u32[]{:S(2)}) collective-permute-start(f32[64,512]{1,0:T(8,128)S(1)} %shard_map.241.refs_4_.refs_0_), channel_id=1, source_target_pairs={{0,16},{1,17},{2,18},{3,19},{4,20},{5,21},{6,22},{7,23},{8,24},{9,... | collective-permute-start | bytes 393224 | tf_op jit(solution)/shard_map/ppermute | solution.py:212
  195.2 13.8 %collective-permute-start.54 = (f32[384,512]{1,0:T(8,128)S(1)}, f32[384,512]{1,0:T(8,128)S(1)}, u32[]{:S(2)}, u32[]{:S(2)}) collective-permute-start(f32[384,512]{1,0:T(8,128)S(1)} %shard_map.240.refs_6_.refs_0_), channel_id=1, source_target_pairs={{0,2},{1,5},{2,0},{3,7},{4,6},{5,1},{6,4},{7,3},{8,10},{9,13},{10,... | collective-permute-start | bytes 2359304 | tf_op jit(solution)/shard_map/ppermute | solution.py:212
  198.2 9.1 %collective-permute-start.55 = (f32[128,512]{1,0:T(8,128)S(1)}, f32[128,512]{1,0:T(8,128)S(1)}, u32[]{:S(2)}, u32[]{:S(2)}) collective-permute-start(f32[128,512]{1,0:T(8,128)S(1)} %shard_map.244.refs_5_.refs_0_), channel_id=1, source_target_pairs={{0,8},{1,9},{2,10},{3,11},{4,12},{5,13},{6,14},{7,15},{8,0},{9,1},... | collective-permute-start | bytes 786440 | tf_op jit(solution)/shard_map/ppermute | solution.py:212
  200.2 7.1 %collective-permute-start.51 = (f32[32,512]{1,0:T(8,128)S(1)}, f32[32,512]{1,0:T(8,128)S(1)}, u32[]{:S(2)}, u32[]{:S(2)}) collective-permute-start(f32[32,512]{1,0:T(8,128)S(1)} %shard_map.242.refs_4_), channel_id=1, source_target_pairs={{0,8},{1,9},{2,10},{3,11},{4,12},{5,13},{6,14},{7,15},{8,0},{9,1},... | collective-permute-start | bytes 196616 | tf_op jit(solution)/shard_map/ppermute | solution.py:212
  207.3 10.7 %collective-permute-start.58 = (f32[256,512]{1,0:T(8,128)S(1)}, f32[256,512]{1,0:T(8,128)S(1)}, u32[]{:S(2)}, u32[]{:S(2)}) collective-permute-start(f32[256,512]{1,0:T(8,128)S(1)} %shard_map.246.refs_2_.refs_0_), channel_id=1, source_target_pairs={{0,4},{1,3},{2,6},{3,1},{4,0},{5,7},{6,2},{7,5},{8,12},{9,11},{10,... | collective-permute-start | bytes 1572872 | tf_op jit(solution)/shard_map/ppermute | solution.py:212
  218.1 16.5 %collective-permute-start.59 = (f32[512,512]{1,0:T(8,128)S(1)}, f32[512,512]{1,0:T(8,128)S(1)}, u32[]{:S(2)}, u32[]{:S(2)}) collective-permute-start(f32[512,512]{1,0:T(8,128)S(1)} %shard_map.251.refs_2_.refs_0_), channel_id=1, source_target_pairs={{0,2},{1,5},{2,0},{3,7},{4,6},{5,1},{6,4},{7,3},{8,10},{9,13},{10,... | collective-permute-start | bytes 3145736 | tf_op jit(solution)/shard_map/ppermute | solution.py:212
  224.7 6.5 %collective-permute-start.61 = (f32[64,512]{1,0:T(8,128)S(1)}, f32[64,512]{1,0:T(8,128)S(1)}, u32[]{:S(2)}, u32[]{:S(2)}) collective-permute-start(f32[64,512]{1,0:T(8,128)S(1)} %shard_map.252.refs_0_.refs_2_), channel_id=1, source_target_pairs={{0,4},{1,3},{2,6},{3,1},{4,0},{5,7},{6,2},{7,5},{8,12},{9,11},{10,... | collective-permute-start | bytes 393224 | tf_op jit(solution)/shard_map/ppermute | solution.py:212
  234.8 17.7 %collective-permute-start.62 = (f32[1024,512]{1,0:T(8,128)S(1)}, f32[1024,512]{1,0:T(8,128)S(1)}, u32[]{:S(2)}, u32[]{:S(2)}) collective-permute-start(f32[1024,512]{1,0:T(8,128)S(1)} %shard_map.254.refs_2_), channel_id=1, source_target_pairs={{0,1},{1,0},{2,3},{3,2},{4,5},{5,4},{6,7},{7,6},{8,9},{9,8},{10,11... | collective-permute-start | bytes 6291464 | tf_op jit(solution)/shard_map/ppermute | solution.py:212
  234.9 17.6 %collective-permute-start.57 = (f32[768,512]{1,0:T(8,128)S(1)}, f32[768,512]{1,0:T(8,128)S(1)}, u32[]{:S(2)}, u32[]{:S(2)}) collective-permute-start(f32[768,512]{1,0:T(8,128)S(1)} %shard_map.247.refs_6_.refs_0_), channel_id=1, source_target_pairs={{0,1},{1,0},{2,3},{3,2},{4,5},{5,4},{6,7},{7,6},{8,9},{9,8},{10,11... | collective-permute-start | bytes 4718600 | tf_op jit(solution)/shard_map/ppermute | solution.py:212
  235.4 6.4 %collective-permute-start.63 = (f32[128,512]{1,0:T(8,128)S(1)}, f32[128,512]{1,0:T(8,128)S(1)}, u32[]{:S(2)}, u32[]{:S(2)}) collective-permute-start(f32[128,512]{1,0:T(8,128)S(1)} %shard_map.253.refs_2_.refs_0_), channel_id=1, source_target_pairs={{0,2},{1,5},{2,0},{3,7},{4,6},{5,1},{6,4},{7,3},{8,10},{9,13},{10,... | collective-permute-start | bytes 786440 | tf_op jit(solution)/shard_map/ppermute | solution.py:212
  241.8 10.7 %collective-permute-start.64 = (f32[256,512]{1,0:T(8,128)S(1)}, f32[256,512]{1,0:T(8,128)S(1)}, u32[]{:S(2)}, u32[]{:S(2)}) collective-permute-start(f32[256,512]{1,0:T(8,128)S(1)} %shard_map.255.refs_4_), channel_id=1, source_target_pairs={{0,1},{1,0},{2,3},{3,2},{4,5},{5,4},{6,7},{7,6},{8,9},{9,8},{10,11... | collective-permute-start | bytes 1572872 | tf_op jit(solution)/shard_map/ppermute | solution.py:212
  241.9 6.0 %collective-permute-start.50 = (f32[16,512]{1,0:T(8,128)S(1)}, f32[16,512]{1,0:T(8,128)S(1)}, u32[]{:S(2)}, u32[]{:S(2)}) collective-permute-start(f32[16,512]{1,0:T(8,128)S(1)} %shard_map.243.refs_2_.refs_0_), channel_id=1, source_target_pairs={{0,24},{1,25},{2,26},{3,27},{4,28},{5,29},{6,30},{7,31},{8,16},{9,... | collective-permute-start | bytes 98312 | tf_op jit(solution)/shard_map/ppermute | solution.py:75
  243.9 6.5 %collective-permute-start.49 = (f32[16,512]{1,0:T(8,128)S(1)}, f32[16,512]{1,0:T(8,128)S(1)}, u32[]{:S(2)}, u32[]{:S(2)}) collective-permute-start(f32[16,512]{1,0:T(8,128)S(1)} %shard_map.243.refs_2_.refs_0_), channel_id=1, source_target_pairs={{0,16},{1,17},{2,18},{3,19},{4,20},{5,21},{6,22},{7,23},{8,24},{9,... | collective-permute-start | bytes 98312 | tf_op jit(solution)/shard_map/ppermute | solution.py:75
  (75 other events, 789.0 us)

commit v2 on v1

--- a/solution.py
+++ b/solution.py
@@ -29,7 +29,7 @@
     return lax.dot_general(left, right, (((1,), (1,)), ((), ())), preferred_element_type=F32)
 
 
-def run(body, outs, operands, after=(), scratch=(), limit=12, macs=0):
+def run(body, outs, operands, after=(), scratch=(), limit=12, weight=1 << 33):
     vmem = pl.BlockSpec(memory_space=pltpu.VMEM)
     anywhere = pl.BlockSpec(memory_space=pl.ANY)
     first, second = len(operands), len(operands) + len(after)
@@ -44,12 +44,7 @@
         out_specs=[vmem] * len(outs),
         scratch_shapes=list(scratch),
         compiler_params=pltpu.CompilerParams(vmem_limit_bytes=limit * MIB),
-        cost_estimate=pl.CostEstimate(
-            flops=2 * macs,
-            bytes_accessed=sum(a.size * a.dtype.itemsize for a in operands)
-            + sum(math.prod(shape) * jnp.dtype(dtype).itemsize for shape, dtype in outs),
-            transcendentals=0,
-        ),
+        cost_estimate=pl.CostEstimate(flops=weight, bytes_accessed=0, transcendentals=0),
     )(*operands, *after)
 
 
@@ -165,10 +160,10 @@
         group = group_of(value, radix, stride)
         held.append(group)
         if level + 1 < len(plan):
-            after = between(level, value) if between else ()
+            after = between(level, group) if between else ()
             value = group_total(k, group, level, plan, factors, backward, conj, after)
             if between and level + 2 == len(plan):
-                between(level + 1, value)
+                between(level + 1, [value])
     return held
 
 
@@ -227,9 +222,12 @@
     return (CHUNKS >> (level + 1), CHUNKS >> level) if level < LEVELS else (0, 1)
 
 
-def outer_body(count, pairs, n_left, n_right, *refs):
+def outer_body(count, pairs, n_left, n_right, n_extra, *refs):
     lefts, rights = refs[:n_left], refs[n_left : n_left + n_right]
-    outs, products = refs[n_left + n_right : -len(pairs)], refs[-len(pairs) :]
+    extra, outs = refs[n_left + n_right :][:n_extra], refs[n_left + n_right + n_extra : -len(pairs)]
+    products = refs[-len(pairs) :]
+    if extra:
+        outs[0][-extra[0].shape[0] :, :] = extra[0][...]
     owns = own_chunk(count), own_chunk(count, True)
     half = CHUNKS // 2
     for q, (left, row, right, column) in enumerate(pairs):
@@ -250,12 +248,16 @@
                 outs[level][place : place + part, :] = product[pl.ds(chunk, part), :]
 
 
-def add_body(low, *refs):
+def add_body(low, extra, *refs):
     out = refs[-1]
-    total = refs[0][...]
-    for ref in refs[1:-1]:
-        total += ref[low : low + out.shape[0], :]
-    out[...] = total
+    rows = out.shape[0] - extra
+    total = refs[0][:rows, :]
+    for ref in refs[1 : -2 if extra else -1]:
+        total += ref[low : low + rows, :]
+    out[:rows, :] = total
+    if extra:
+        mine, other = refs[-2], refs[-3]
+        out[rows:, :] = mine[-extra:, :] + other[-extra:, :]
 
 
 def join_body(first, second, out):
@@ -264,32 +266,33 @@
 
 
 class Bulk:
-    def __init__(self, count, lefts, rights, pairs, after=()):
+    def __init__(self, count, lefts, rights, pairs, after=(), extra=()):
         self.bits = partners(count)
+        self.extra = extra[0].shape[0] if extra else 0
         width = 512
         part = lefts[0].shape[1] // CHUNKS
         self.rows = part * len(pairs)
         outs = [((self.rows * (hi - lo), width), F32) for lo, hi in map(slots, range(LEVELS + 1))]
+        outs[0] = ((outs[0][0][0] + self.extra, width), F32)
         self.parts = run(
-            functools.partial(outer_body, count, pairs, len(lefts), len(rights)),
+            functools.partial(outer_body, count, pairs, len(lefts), len(rights), len(extra)),
             outs,
-            list(lefts) + list(rights),
+            list(lefts) + list(rights) + list(extra),
             after,
             [pltpu.VMEM((lefts[pair[0]].shape[1], width), F32) for pair in pairs],
             limit=16,
-            macs=len(pairs) * rights[0].shape[0] * lefts[0].shape[1] * width,
         )
         self.received = []
-        self.value = None
+        self.sent = None
 
     def reduced(self, level, after=()):
         low, high = slots(level)
         if not self.received:
             return self.parts[level]
         (total,) = run(
-            functools.partial(add_body, low * self.rows),
-            [((self.rows * (high - low), self.parts[level].shape[1]), F32)],
-            [self.parts[level]] + self.received,
+            functools.partial(add_body, low * self.rows, self.extra),
+            [((self.rows * (high - low) + self.extra, self.parts[level].shape[1]), F32)],
+            [self.parts[level]] + self.received + ([self.sent] if self.extra else []),
             after,
             limit=8,
         )
@@ -297,18 +300,18 @@
 
     def send(self, after=()):
         level = len(self.received)
-        total = self.reduced(level, after)
-        self.received.append(with_partner(total, self.bits[level]))
-        return total
+        self.sent = self.reduced(level, after)
+        self.received.append(with_partner(self.sent, self.bits[level]))
+        return self.sent
 
     def settle(self, after=()):
         value = self.reduced(LEVELS, after)
         for even, odd in self.bits[LEVELS:]:
             other = with_partner(value, (even, odd))
             (value,) = run(
-                functools.partial(add_body, 0), [(value.shape, F32)], [value, other], limit=4
+                functools.partial(add_body, 0, 0), [(value.shape, F32)], [value, other], limit=4
             )
-        self.value, self.level = value, LEVELS - 1
+        self.total, self.value, self.level = value, value[: self.rows], LEVELS - 1
         return value
 
     def fetch(self, after=()):
@@ -638,7 +641,12 @@
     width = x_ref.shape[1]
     states = decay_ref.shape[-1]
     rel = relative(lens_ref, span, states)
-    shift, tilt = input_terms(k + 1, token_scale(lens_ref), sums_ref, stats_ref, gain_ref, grads_ref)
+    bias_grad, gain_grad = gathered(sums_ref)
+    grads_ref[0:1, :] = gain_grad
+    grads_ref[1:2, :] = bias_grad
+    shift, tilt = input_terms(
+        k + 1, token_scale(lens_ref), bias_grad, gain_grad, stats_ref, gain_ref
+    )
     mean = stats_ref[0:1, :]
     step = CHUNK * seqs
     for r in range(0, span * seqs, step):
@@ -653,10 +661,7 @@
     local_adjoint(k, span, backward, rel, g_ref, decay_ref, summary_ref)
 
 
-def input_terms(k, scale, sums_ref, stats_ref, gain_ref, grads_ref):
-    bias_grad, gain_grad = gathered(sums_ref)
-    grads_ref[0:1, :] = gain_grad
-    grads_ref[1:2, :] = bias_grad
+def input_terms(k, scale, bias_grad, gain_grad, stats_ref, gain_ref):
     rstd = stats_ref[2:3, :]
     gain = gain_ref[k : k + 1, :]
     return -rstd * gain * bias_grad * scale, -rstd * rstd * gain * gain_grad * scale
@@ -694,15 +699,12 @@
 
 
 def input_body(
-    k, seq_major, dv_ref, dy_ref, x_ref, d_ref, stats_ref, gain_ref, bias_ref, w_in_ref, skip_ref,
+    k, seqs, seq_major, dv_ref, dy_ref, x_ref, d_ref, stats_ref, gain_ref, bias_ref, w_in_ref, skip_ref,
     part_ref, skip_grad_ref, sums_ref,
 ):
     width = x_ref.shape[1]
-    seqs = CHUNK
     mean, scale, rstd = stats_ref[0:1, :], stats_ref[3:4, :], stats_ref[2:3, :]
     gain, bias, skip = (ref[k : k + 1, :] for ref in (gain_ref, bias_ref, skip_ref))
-    if seq_major:
-        seqs = d_ref.shape[0]
     step = CHUNK * seqs
     first = jnp.zeros((8, width), F32)
     second = jnp.zeros((8, width), F32)
@@ -719,49 +721,29 @@
         else:
             d = d_ref[r : r + step, :]
         part_ref[r : r + step, :] = d + du * scale
-    spread(sums_ref, jnp.sum(first, 0, keepdims=True), jnp.sum(second, 0, keepdims=True))
     skip_grad_ref[...] = third
+    if seq_major:
+        spread(sums_ref, jnp.sum(first, 0, keepdims=True), jnp.sum(second, 0, keepdims=True))
+    else:
+        sums_ref[0] = first
+        sums_ref[1] = second
+
+
+def small_body(small0, skip0, sums0, small1, skip1, out):
+    out[...] = jnp.zeros_like(out)
+    rows = [small0[0:1, :], small0[1:2, :], skip0[...], sums0[0], sums0[1]]
+    for row, value in enumerate(rows):
+        out[row : row + 1, :] = jnp.sum(value, 0, keepdims=True)
+    for row, value in enumerate([small1[0:1, :], small1[1:2, :], skip1[...]]):
+        out[8 + row : 9 + row, :] = jnp.sum(value, 0, keepdims=True)
 
 
 def finish_body(
-    k, span, lens_ref, sums_ref, part_ref, x_ref, mask_ref, stats_ref, gain_ref, out_ref, grads_ref
+    span, total_ref, lens_ref, part_ref, x_ref, mask_ref, gain_ref, decay_ref, running_ref, stats0_ref,
+    stats1_ref, grads_ref, out_ref, g_gain_ref, g_bias_ref, nu_ref, phase_ref, skip_ref, run_ref,
 ):
-    seqs = out_ref.shape[0]
-    width = x_ref.shape[1]
-    scale = token_scale(lens_ref)
-    shift, tilt = input_terms(k, scale, sums_ref, stats_ref, gain_ref, grads_ref)
-    mean = stats_ref[0:1, :]
-    step = CHUNK * seqs
-    for r in range(0, span * seqs, step):
-        live = lane_tiled(mask_ref[r : r + step, :], width)
-        d = part_ref[r : r + step, :] + live * (shift + tilt * (x_ref[r : r + step, :] - mean))
-        out_ref[:, r // seqs : r // seqs + CHUNK, :] = from_time_major(d, seqs)
-
-
-def small_body(refs_per_block, *refs):
-    out = refs[-1]
-    out[...] = jnp.zeros_like(out)
-    for k in range(2):
-        small, skip_grad = refs[2 * k], refs[2 * k + 1]
-        out[8 * k : 8 * k + 2, :] = small[0:2, :]
-        out[8 * k + 2 : 8 * k + 3, :] = jnp.sum(skip_grad[...], 0, keepdims=True)
-
-
-def sum_body(*refs):
-    total = refs[0][...]
-    for ref in refs[1:-1]:
-        total += ref[...]
-    refs[-1][...] = total
-
-
-def results_body(n_parts, *refs):
-    parts, rest = refs[:n_parts], refs[n_parts:]
-    lens_ref, decay_ref, running_ref = rest[:3]
-    stats_refs, grads_refs = rest[3:5], rest[5:7]
-    gain_ref, bias_ref, nu_ref, phase_ref, skip_ref, run_ref = rest[7:]
-    small = parts[0][...]
-    for ref in parts[1:]:
-        small += ref[...]
+    stats_refs = (stats0_ref, stats1_ref)
+    small = total_ref[total_ref.shape[0] - 16 :, :]
     states = decay_ref.shape[-1]
     count = jnp.sum(lens_ref[...].astype(F32), axis=0, keepdims=True)
     for k in range(2):
@@ -773,13 +755,23 @@
         ) + g_gamma * rate * radius * radius / gamma
         phase_ref[k : k + 1, :] = radius * (sum_im * cosine - sum_re * sine)
         skip_ref[k : k + 1, :] = small[8 * k + 2 : 8 * k + 3, :]
-        gain_ref[k : k + 1, :] = grads_refs[k][0:1, :]
-        bias_ref[k : k + 1, :] = grads_refs[k][1:2, :]
         mean, var = stats_refs[k][0:1, :], stats_refs[k][1:2, :]
         run_ref[k, 0:1, :] = (1.0 - momentum) * running_ref[k, 0:1, :] + momentum * mean
         run_ref[k, 1:2, :] = (1.0 - momentum) * running_ref[k, 1:2, :] + momentum * var * (
             count / (count - 1.0)
         )
+    bias_grad, gain_grad = small[3:4, :], small[4:5, :]
+    g_gain_ref[0:1, :], g_gain_ref[1:2, :] = gain_grad, grads_ref[0:1, :]
+    g_bias_ref[0:1, :], g_bias_ref[1:2, :] = bias_grad, grads_ref[1:2, :]
+    seqs = out_ref.shape[0]
+    width = x_ref.shape[1]
+    shift, tilt = input_terms(0, 1.0 / count, bias_grad, gain_grad, stats_refs[0], gain_ref)
+    mean = stats_refs[0][0:1, :]
+    step = CHUNK * seqs
+    for r in range(0, span * seqs, step):
+        live = lane_tiled(mask_ref[r : r + step, :], width)
+        d = part_ref[r : r + step, :] + live * (shift + tilt * (x_ref[r : r + step, :] - mean))
+        out_ref[:, r // seqs : r // seqs + CHUNK, :] = from_time_major(d, seqs)
 
 
 def with_entry(body, plan):
@@ -848,16 +840,14 @@
     )
 
     flows = {}
-
-    def beside_top(level, value):
-        if level == 1:
-            flows["top"] = Bulk(
-                count, [act1, h1], [dz1, dy1], [(0, 0, 0, 0), (0, 0, 0, width), (1, 0, 1, 0)], [value]
-            )
-            flows["top"].send()
+    flows["top"] = Bulk(count, [act1, h1], [dz1, dy1], [(0, 0, 0, 0), (0, 0, 0, width), (1, 0, 1, 0)])
+    flows["top"].send()
+
+    def beside_top(level, group):
+        if level == 0:
             return flows["top"].parts[-1:]
-        if level == len(plan) - 1:
-            flows["step"] = flows["top"].send([value])
+        if level == len(plan) - 2:
+            return [flows["top"].send([group[1]])]
         return ()
 
     held = exchange(1, part, plan, factors, False, True, beside_top)
@@ -867,16 +857,13 @@
         [pair_low, eight],
         held,
         [lens, g1, h1, v1, decay],
-        [flows["step"]],
-    )
-    step = top.send([dv1])
+    )
     part1, skip1, sums = run(
-        functools.partial(input_body, 1, True),
+        functools.partial(input_body, 1, seqs, True),
         [whole, eight, tile],
         [dv1, dy1, x1, cotangent, stats1, bn_gain, bn_bias, w_in, skip],
-        [step],
-        macs=rows * width * 2 * states,
-    )
+    )
+    top.send([sums])
     sums = everywhere(sums)
     step = top.send([sums])
     d0, dz0, dy0, g0, grads1, part = run(
@@ -884,87 +871,67 @@
         [whole, double_low, whole_low, pair, eight, summary],
         [lens, sums, part1, x1, mask, stats1, slope0, gate0, value0, bn_gain, decay, w_out, w_glu],
         [step],
-        macs=rows * width * (2 * width + 2 * states),
-    )
-
-    def beside_middle(level, value):
-        if level == 1:
-            step = top.send([value])
-            flows["middle"] = Bulk(
-                count,
-                [u1, act0, h0],
-                [dv1, dz0, dy0],
-                [(0, 0, 0, 0), (1, 0, 1, 0), (1, 0, 1, width), (2, seqs, 2, 0)],
-                [step],
-            )
-            flows["middle"].send()
-            return flows["middle"].parts[-1:]
-        if level == len(plan) - 1:
-            flows["step"] = flows["middle"].send([value])
+    )
+
+    flows["middle"] = Bulk(
+        count, [act0, h0], [dz0, dy0], [(0, 0, 0, 0), (0, 0, 0, width), (1, seqs, 1, 0)], [part]
+    )
+    flows["middle"].send()
+
+    def beside_middle(level, group):
+        if level == 0:
+            return [flows["middle"].parts[-1], top.send([flows["middle"].parts[-1]])]
+        if level == len(plan) - 2:
+            return [flows["middle"].send([group[1]])]
         return ()
 
     held = exchange(0, part, plan, factors, True, True, beside_middle)
     middle = flows["middle"]
+    own = top.settle([held[-1][1]])
+    top.fetch()
     dv0, small0 = entered(
         functools.partial(adjoint_body, 0, plan, span, True),
         [pair_low, eight],
         held,
         [lens, g0, h0, v0, decay],
-        [flows["step"]],
-    )
-    own = top.settle([dv0])
-    top.fetch()
+        [own],
+    )
     part0, skip0, sums = run(
-        functools.partial(input_body, 0, False),
-        [whole, eight, tile],
+        functools.partial(input_body, 0, seqs, False),
+        [whole, eight, ((2, 8, width), F32)],
         [dv0, dy0, x0, d0, stats0, bn_gain, bn_bias, w_in, skip],
-        [own],
-        macs=rows * width * 2 * states,
-    )
-    step = middle.send([sums])
-    sums = everywhere(sums)
-    grad_x, grads0 = run(
-        functools.partial(finish_body, 0, span),
-        [seq_major, eight],
-        [lens, sums, part0, x0, mask, stats0, bn_gain],
-    )
-
-    last = Bulk(count, [u0], [dv0], [(0, 0, 0, 0)], [sums])
+    )
+
+    (small,) = run(small_body, [((16, width), F32)], [small0, skip0, sums, small1, skip1], limit=4)
+    last = Bulk(
+        count, [u0, u1], [dv0, dv1], [(0, 0, 0, 0), (1, 0, 1, 0)], [part0], [small]
+    )
     last.send()
     step = middle.send([last.parts[-1]])
     step = top.fetch([step])
-    (small,) = run(
-        functools.partial(small_body, 2), [((16, width), F32)], [small0, skip0, small1, skip1], [step]
-    )
-    step = last.send([small])
+    step = last.send([step])
+    step = middle.send([step])
+    step = last.send([step])
     step = top.fetch([step])
     step = middle.send([step])
-    group = group_of(small, *plan[0])
-    (small,) = run(sum_body, [((16, width), F32)], group, [step], limit=4)
-    step = last.send([small])
-    step = top.fetch([step])
+    step = last.send([step])
     step = middle.settle([step])
     middle.fetch()
+    step = top.fetch([step])
     step = last.send([step])
-    group = group_of(small, *plan[1])
-    (small,) = run(sum_body, [((16, width), F32)], group, [step], limit=4)
-    step = middle.fetch([small])
-    step = last.send([step])
-    for stage in plan[2:]:
-        group = group_of(small, *stage)
-        if stage != plan[-1]:
-            (small,) = run(sum_body, [((16, width), F32)], group, [step], limit=4)
     step = middle.fetch([step])
-    step = top.fetch([step])
     step = last.settle([step])
     last.fetch()
-    step = last.fetch([step])
-    g_gain, g_bias, g_nu, g_phase, g_skip, running_out = run(
-        functools.partial(results_body, len(group)),
-        [((2, width), F32)] * 2 + [((2, states), F32)] * 2 + [((2, width), F32), ((2, 2, width), F32)],
-        list(group) + [lens, decay, running, stats0, stats1, grads0, grads1],
+    step = middle.fetch([step])
+    grad_x, g_gain, g_bias, g_nu, g_phase, g_skip, running_out = run(
+        functools.partial(finish_body, span),
+        [seq_major] + [((2, width), F32)] * 2 + [((2, states), F32)] * 2
+        + [((2, width), F32), ((2, 2, width), F32)],
+        [last.total, lens, part0, x0, mask, bn_gain, decay, running, stats0, stats1, grads1],
         [step],
     )
+    step = last.fetch([g_gain])
+    step = top.fetch([step])
     step = middle.fetch([step])
     step = last.fetch([step])
     step = last.fetch([step])
@@ -975,8 +942,8 @@
         [top, middle, last],
         [
             [(0, 1, 0), (0, 1, width), (1, 1, 0)],
-            [(2, 1, 0), (0, 0, 0), (0, 0, width), (1, 0, 0)],
-            [(2, 0, 0)],
+            [(0, 0, 0), (0, 0, width), (1, 0, 0)],
+            [(2, 0, 0), (2, 1, 0)],
         ],
         [(2, width, 2 * width), (2, 2 * states, width), (2, width, 2 * states)],
     )

time: 256 us -> 220 us (0.86)
  waiting for transfers between devices: 94.1 us -> 74.1 us
  Pallas kernels: 45.8 us -> 37.8 us
  local copies, waits for them, and re-layouts: 11.1 us -> 4.82 us
    ppermute x35 -> x28, waiting for transfers between devices: 34.2 us -> 23.2 us  [swap(): lax.ppermute(value, 'tm', [(i, i ^ stride * mask) for i in range(count)])]
    pallas_call x53 -> x50, Pallas kernels: 42.6 us -> 34.6 us  [run(): pl.pallas_call(kernel, out_shape=[jax.ShapeDtypeStruct(shape, dtype) for...]
    ppermute x30, starting transfers between devices: 23.5 us -> 30.3 us  [with_partner(): lax.ppermute(value, 'tm', [(i, i ^ (odd if i & 1 else even)) for i in ran...]
    ppermute x30, waiting for transfers between devices: 57.5 us -> 50.9 us  [with_partner(): lax.ppermute(value, 'tm', [(i, i ^ (odd if i & 1 else even)) for i in ran...]
    unnamed x82 -> x48, local copies, waits for them, and re-layouts: 10.3 us -> 4.07 us
    ppermute x35 -> x28, starting transfers between devices: 38.1 us -> 32.3 us  [swap(): lax.ppermute(value, 'tm', [(i, i ^ stride * mask) for i in range(count)])]
    all_to_all x1 -> x0, starting transfers between devices: 2.92 us -> none  [everywhere(): return lax.all_to_all(tiles, 'tm', 0, 0)]
  transfers between devices with their start and end apart: 66 -> 58, of which waited for: 47 -> 39; matrix products, arithmetic and copies ran while one was open for 0% -> 0% of each run, Pallas kernels for 8% -> 7%
where the time goes in v2:
time: 220 us
  waiting for transfers between devices  74.1 us (34%)
  starting transfers between devices  62.5 us (28%)
  blocking collectives  38.6 us (18%)
  Pallas kernels  37.8 us (17%)
  local copies, waits for them, and re-layouts  4.82 us (2%)
    ppermute x30, waiting for transfers between devices, with_partner(): lax.ppermute(value, 'tm', [(i, i ^ (odd if i & 1 else even)) for i in ran...  50.9 us
    all_to_all x3, blocking collectives, everywhere(): return lax.all_to_all(tiles, 'tm', 0, 0)  38.6 us
    pallas_call x50, Pallas kernels, run(): pl.pallas_call(kernel, out_shape=[jax.ShapeDtypeStruct(shape, dtype) for...  34.6 us
    ppermute x28, starting transfers between devices, swap(): lax.ppermute(value, 'tm', [(i, i ^ stride * mask) for i in range(count)])  32.3 us
    ppermute x30, starting transfers between devices, with_partner(): lax.ppermute(value, 'tm', [(i, i ^ (odd if i & 1 else even)) for i in ran...  30.3 us
    ppermute x28, waiting for transfers between devices, swap(): lax.ppermute(value, 'tm', [(i, i ^ stride * mask) for i in range(count)])  23.2 us
  transfers between devices with their start and end apart: 58, of which 39 were waited for; matrix products, arithmetic and copies ran while one was open for 0% of the time, Pallas kernels for 7%

profile of v2, /device:TPU:0, one launch (start us, length us, event | category | flops | bytes accessed | tf_op | source)
XLA Modules:
  0.0 219.9 jit_solution(3646290140498545659)
XLA Ops:
  6.7 15.3 %all_to_all.15.refs_1_ = f32[32,8,128]{2,1,0:T(8,128)S(1)} all-to-all(f32[32,8,128]{2,1,0:T(8,128)S(1)} %get-tuple-element.84), channel_id=1, replica_groups=mesh['tm'=32] {'tm'}, dimensions={0} | all-to-all | bytes 262144 | tf_op jit(solution)/shard_map/all_to_all | solution.py:105
  32.5 2.5 %collective-permute-start.4 = (f32[16,512]{1,0:T(8,128)S(1)}, f32[16,512]{1,0:T(8,128)S(1)}, u32[]{:S(2)}, u32[]{:S(2)}) collective-permute-start(f32[16,512]{1,0:T(8,128)S(1)} %shard_map.206.refs_6_), channel_id=1, source_target_pairs={{0,8},{1,9},{2,10},{3,11},{4,12},{5,13},{6,14},{7,15},{8,0},{9,1},... | collective-permute-start | bytes 98312 | tf_op jit(solution)/shard_map/ppermute | solution.py:70
  37.3 4.3 %shard_map.207 = (f32[1024,512]{1,0:T(8,128)S(1)}, bf16[1040,512]{1,0:T(8,128)(2,1)S(1)}, bf16[1024,512]{1,0:T(8,128)(2,1)S(1)}, bf16[1024,512]{1,0:T(8,128)(2,1...) custom-call(f32[16,512]{1,0:T(8,128)S(1)} %get-tuple-element.87.refs_0_, ...), custom_call_target="tpu_custom_call" | custom-call | flops 8589934592 | tf_op jit(solution)/shard_map/pallas_call | solution.py:40
  41.6 11.6 %all_to_all.16.refs_1_ = f32[32,8,128]{2,1,0:T(8,128)S(1)} all-to-all(f32[32,8,128]{2,1,0:T(8,128)S(1)} %get-tuple-element.94), channel_id=1, replica_groups=mesh['tm'=32] {'tm'}, dimensions={0} | all-to-all | bytes 262144 | tf_op jit(solution)/shard_map/all_to_all | solution.py:105
  63.6 2.5 %collective-permute-start.11 = (f32[16,512]{1,0:T(8,128)S(1)}, f32[16,512]{1,0:T(8,128)S(1)}, u32[]{:S(2)}, u32[]{:S(2)}) collective-permute-start(f32[16,512]{1,0:T(8,128)S(1)} %shard_map.210.refs_6_), channel_id=1, source_target_pairs={{0,8},{1,9},{2,10},{3,11},{4,12},{5,13},{6,14},{7,15},{8,0},{9,1},... | collective-permute-start | bytes 98312 | tf_op jit(solution)/shard_map/ppermute | solution.py:70
  68.3 8.3 %shard_map.211 = (f32[16,64,512]{2,1,0:T(8,128)}, bf16[1040,512]{1,0:T(8,128)(2,1)S(1)}, bf16[1024,512]{1,0:T(8,128)(2,1)S(1)}, bf16[1024,1024]{1,0:T(8,128)(2,1...) custom-call(f32[16,512]{1,0:T(8,128)S(1)} %get-tuple-element.96.refs_0_, ...), custom_call_target="tpu_custom_call" | custom-call | flops 8589934592 | tf_op jit(solution)/shard_map/pallas_call | solution.py:40
  76.6 2.0 shard_map.212
  79.1 2.9 %collective-permute-done.14.refs_1_ = f32[16,512]{1,0:T(8,128)S(1)} collective-permute-done((f32[16,512]{1,0:T(8,128)S(1)}, f32[16,512]{1,0:T(8,128)S(1)}, u32[]{:S(2)}, u32[]{:S(2)}) %collective-permute-start.14) | collective-permute-done | bytes 32800 | tf_op jit(solution)/shard_map/ppermute | solution.py:70
  86.2 2.5 %collective-permute-done.17.refs_3_.refs_5_ = f32[16,512]{1,0:T(8,128)S(1)} collective-permute-done((f32[16,512]{1,0:T(8,128)S(1)}, f32[16,512]{1,0:T(8,128)S(1)}, u32[]{:S(2)}, u32[]{:S(2)}) %collective-permute-start.17) | collective-permute-done | bytes 32800 | tf_op jit(solution)/shard_map/ppermute | solution.py:70
  88.9 2.1 collective-permute-start.21
  99.3 6.6 %collective-permute-done.22.refs_2_ = f32[384,512]{1,0:T(8,128)S(1)} collective-permute-done((f32[384,512]{1,0:T(8,128)S(1)}, f32[384,512]{1,0:T(8,128)S(1)}, u32[]{:S(2)}, u32[]{:S(2)}) %collective-permute-start.22) | collective-permute-done | bytes 786464 | tf_op jit(solution)/shard_map/ppermute | solution.py:207
  106.3 11.7 %all_to_all.17.refs_4_.refs_1_ = f32[32,8,128]{2,1,0:T(8,128)S(1)} all-to-all(f32[32,8,128]{2,1,0:T(8,128)S(1)} %get-tuple-element.112.refs_3_), channel_id=1, replica_groups=mesh['tm'=32] {'tm'}, dimensions={0} | all-to-all | bytes 262144 | tf_op jit(solution)/shard_map/all_to_all | solution.py:105
  118.8 3.0 %shard_map.220 = (f32[1024,512]{1,0:T(8,128)S(1)}, bf16[1024,1024]{1,0:T(8,128)(2,1)S(1)}, bf16[1024,512]{1,0:T(8,128)(2,1)S(1)}, f32[1024,512]{1,0:T(8,128)S(1)...) custom-call(s32[16,1]{1,0:T(8,128)S(1)} %copy.26.refs_0_.refs_13_.refs_1_, f32[32,8,128]{2,1,0:T(8,128)S(1)} %all_to_all.17.refs_4_.refs_1_, ...), custom_call_target="tpu_custom_call" | custom-call | flops 8589934592 | tf_op jit(solution)/shard_map/pallas_call | solution.py:40
  121.9 2.0 shard_map.221
  137.9 2.2 collective-permute-done.31.refs_8_
  144.6 2.1 collective-permute-done.36.refs_2_
  148.5 1.9 collective-permute-start.41
  150.9 7.8 %collective-permute-done.38.refs_3_ = f32[192,512]{1,0:T(8,128)S(1)} collective-permute-done((f32[192,512]{1,0:T(8,128)S(1)}, f32[192,512]{1,0:T(8,128)S(1)}, u32[]{:S(2)}, u32[]{:S(2)}) %collective-permute-start.38) | collective-permute-done | bytes 393248 | tf_op jit(solution)/shard_map/ppermute | solution.py:207
  162.6 2.0 collective-permute-done.40.refs_4_
  164.7 2.8 %collective-permute-start.44 = (f32[48,512]{1,0:T(8,128)S(1)}, f32[48,512]{1,0:T(8,128)S(1)}, u32[]{:S(2)}, u32[]{:S(2)}) collective-permute-start(f32[48,512]{1,0:T(8,128)S(1)} %shard_map.237.refs_5_), channel_id=1, source_target_pairs={{0,16},{1,17},{2,18},{3,19},{4,20},{5,21},{6,22},{7,23},{8,24},{9,... | collective-permute-start | bytes 294920 | tf_op jit(solution)/shard_map/ppermute | solution.py:207
  167.8 2.7 %collective-permute-done.44.refs_5_ = f32[48,512]{1,0:T(8,128)S(1)} collective-permute-done((f32[48,512]{1,0:T(8,128)S(1)}, f32[48,512]{1,0:T(8,128)S(1)}, u32[]{:S(2)}, u32[]{:S(2)}) %collective-permute-start.44) | collective-permute-done | bytes 98336 | tf_op jit(solution)/shard_map/ppermute | solution.py:207
  170.6 3.5 %collective-permute-start.46 = (f32[48,512]{1,0:T(8,128)S(1)}, f32[48,512]{1,0:T(8,128)S(1)}, u32[]{:S(2)}, u32[]{:S(2)}) collective-permute-start(f32[48,512]{1,0:T(8,128)S(1)} %shard_map.239.refs_2_.refs_0_), channel_id=1, source_target_pairs={{0,16},{1,17},{2,18},{3,19},{4,20},{5,21},{6,22},{7,23},{8,24},{9,... | collective-permute-start | bytes 294920 | tf_op jit(solution)/shard_map/ppermute | solution.py:207
  175.1 2.3 %collective-permute-start.45 = (f32[48,512]{1,0:T(8,128)S(1)}, f32[48,512]{1,0:T(8,128)S(1)}, u32[]{:S(2)}, u32[]{:S(2)}) collective-permute-start(f32[48,512]{1,0:T(8,128)S(1)} %shard_map.241.refs_2_.refs_6_), channel_id=1, source_target_pairs={{0,16},{1,17},{2,18},{3,19},{4,20},{5,21},{6,22},{7,23},{8,24},{9,... | collective-permute-start | bytes 294920 | tf_op jit(solution)/shard_map/ppermute | solution.py:207
  181.1 2.2 collective-permute-start.49
  183.3 2.1 collective-permute-done.47.refs_1_
  186.9 2.5 %shard_map.245 = (f32[16,64,512]{2,1,0:T(8,128)}, f32[2,512]{1,0:T(2,128)}, f32[2,512]{1,0:T(2,128)}, f32[2,256]{1,0:T(2,128)}, f32[2,256]{1,0:T(2,128)}, /*index=5*/f32[2,512]{1,0:T(2,128)}, f32[2,2,512]{2,1,0:T(2,128)}) custom-call(f32[48,512]{1,0:T(8,128)S(1)} %shard_map.243.refs_2_.refs_0_, s32[16,1]{1,0:T(8,128)S(1)} %copy.26.refs_0_.refs_13_.refs_1_, ...), custom_call_target="tpu_custom_call" | custom-call | flops 8589934592 | tf_op jit(solution)/shard_map/pallas_call | solution.py:40
  190.5 2.8 %collective-permute-done.51.refs_1_ = f32[192,512]{1,0:T(8,128)S(1)} collective-permute-done((f32[192,512]{1,0:T(8,128)S(1)}, f32[192,512]{1,0:T(8,128)S(1)}, u32[]{:S(2)}, u32[]{:S(2)}) %collective-permute-start.51) | collective-permute-done | bytes 393248 | tf_op jit(solution)/shard_map/ppermute | solution.py:207
  197.0 7.4 %collective-permute-done.54.refs_1_ = f32[128,512]{1,0:T(8,128)S(1)} collective-permute-done((f32[128,512]{1,0:T(8,128)S(1)}, f32[128,512]{1,0:T(8,128)S(1)}, u32[]{:S(2)}, u32[]{:S(2)}) %collective-permute-start.54) | collective-permute-done | bytes 262176 | tf_op jit(solution)/shard_map/ppermute | solution.py:207
  205.1 2.7 %collective-permute-done.52.refs_1_ = f32[384,512]{1,0:T(8,128)S(1)} collective-permute-done((f32[384,512]{1,0:T(8,128)S(1)}, f32[384,512]{1,0:T(8,128)S(1)}, u32[]{:S(2)}, u32[]{:S(2)}) %collective-permute-start.52) | collective-permute-done | bytes 786464 | tf_op jit(solution)/shard_map/ppermute | solution.py:207
  208.0 5.7 %collective-permute-done.56.refs_1_ = f32[256,512]{1,0:T(8,128)S(1)} collective-permute-done((f32[256,512]{1,0:T(8,128)S(1)}, f32[256,512]{1,0:T(8,128)S(1)}, u32[]{:S(2)}, u32[]{:S(2)}) %collective-permute-start.56) | collective-permute-done | bytes 524320 | tf_op jit(solution)/shard_map/ppermute | solution.py:207
  213.9 2.6 %collective-permute-done.57.refs_5_ = f32[512,512]{1,0:T(8,128)S(1)} collective-permute-done((f32[512,512]{1,0:T(8,128)S(1)}, f32[512,512]{1,0:T(8,128)S(1)}, u32[]{:S(2)}, u32[]{:S(2)}) %collective-permute-start.57) | collective-permute-done | bytes 1048608 | tf_op jit(solution)/shard_map/ppermute | solution.py:207
  216.5 3.2 %shard_map.253 = (f32[2,512,1024]{2,1,0:T(8,128)}, f32[2,512,512]{2,1,0:T(8,128)}, f32[2,512,512]{2,1,0:T(8,128)}) custom-call(f32[768,512]{1,0:T(8,128)S(1)} %shard_map.247.refs_2_.refs_0_, f32[768,512]{1,0:T(8,128)S(1)} %collective-permute-done.50.refs_1_, f32[768,512]{1,0:T(8,128)S(1)} %shard_map.251.refs_2_, ...), custom_call_target="tpu_custom_call" | custom-call | tf_op jit(solution)/shard_map/pallas_call | solution.py:361
  (189 shorter events, 82.9 us)
Async XLA Ops:
  30.5 5.8 %collective-permute-start.6 = (f32[16,512]{1,0:T(8,128)S(1)}, f32[16,512]{1,0:T(8,128)S(1)}, u32[]{:S(2)}, u32[]{:S(2)}) collective-permute-start(f32[16,512]{1,0:T(8,128)S(1)} %shard_map.206.refs_6_), channel_id=1, source_target_pairs={{0,24},{1,25},{2,26},{3,27},{4,28},{5,29},{6,30},{7,31},{8,16},{9,... | collective-permute-start | bytes 98312 | tf_op jit(solution)/shard_map/ppermute | solution.py:70
  61.6 5.8 %collective-permute-start.13 = (f32[16,512]{1,0:T(8,128)S(1)}, f32[16,512]{1,0:T(8,128)S(1)}, u32[]{:S(2)}, u32[]{:S(2)}) collective-permute-start(f32[16,512]{1,0:T(8,128)S(1)} %shard_map.210.refs_6_), channel_id=1, source_target_pairs={{0,24},{1,25},{2,26},{3,27},{4,28},{5,29},{6,30},{7,31},{8,16},{9,... | collective-permute-start | bytes 98312 | tf_op jit(solution)/shard_map/ppermute | solution.py:70
  78.5 7.5 %collective-permute-start.18 = (f32[768,512]{1,0:T(8,128)S(1)}, f32[768,512]{1,0:T(8,128)S(1)}, u32[]{:S(2)}, u32[]{:S(2)}) collective-permute-start(f32[768,512]{1,0:T(8,128)S(1)} %get-tuple-element.109), channel_id=1, source_target_pairs={{0,1},{1,0},{2,3},{3,2},{4,5},{5,4},{6,7},{7,6},{8,9},{9,8},{10,11... | collective-permute-start | bytes 4718600 | tf_op jit(solution)/shard_map/ppermute | solution.py:207
  88.9 5.8 %collective-permute-start.21 = (f32[16,512]{1,0:T(8,128)S(1)}, f32[16,512]{1,0:T(8,128)S(1)}, u32[]{:S(2)}, u32[]{:S(2)}) collective-permute-start(f32[16,512]{1,0:T(8,128)S(1)} %shard_map.215.refs_6_), channel_id=1, source_target_pairs={{0,24},{1,25},{2,26},{3,27},{4,28},{5,29},{6,30},{7,31},{8,16},{9,... | collective-permute-start | bytes 98312 | tf_op jit(solution)/shard_map/ppermute | solution.py:70
  93.4 12.5 %collective-permute-start.22 = (f32[384,512]{1,0:T(8,128)S(1)}, f32[384,512]{1,0:T(8,128)S(1)}, u32[]{:S(2)}, u32[]{:S(2)}) collective-permute-start(f32[384,512]{1,0:T(8,128)S(1)} %shard_map.214.refs_5_), channel_id=1, source_target_pairs={{0,2},{1,5},{2,0},{3,7},{4,6},{5,1},{6,4},{7,3},{8,10},{9,13},{10,... | collective-permute-start | bytes 2359304 | tf_op jit(solution)/shard_map/ppermute | solution.py:207
  105.9 12.2 %collective-permute-start.23 = (f32[192,512]{1,0:T(8,128)S(1)}, f32[192,512]{1,0:T(8,128)S(1)}, u32[]{:S(2)}, u32[]{:S(2)}) collective-permute-start(f32[192,512]{1,0:T(8,128)S(1)} %shard_map.218), channel_id=1, source_target_pairs={{0,4},{1,3},{2,6},{3,1},{4,0},{5,7},{6,2},{7,5},{8,12},{9,11},{10,... | collective-permute-start | bytes 1179656 | tf_op jit(solution)/shard_map/ppermute | solution.py:207
  118.1 7.1 %collective-permute-start.25 = (f32[96,512]{1,0:T(8,128)S(1)}, f32[96,512]{1,0:T(8,128)S(1)}, u32[]{:S(2)}, u32[]{:S(2)}) collective-permute-start(f32[96,512]{1,0:T(8,128)S(1)} %shard_map.219.refs_13_), channel_id=1, source_target_pairs={{0,8},{1,9},{2,10},{3,11},{4,12},{5,13},{6,14},{7,15},{8,0},{9,1},... | collective-permute-start | bytes 589832 | tf_op jit(solution)/shard_map/ppermute | solution.py:207
  128.8 7.9 %collective-permute-start.33 = (f32[48,512]{1,0:T(8,128)S(1)}, f32[48,512]{1,0:T(8,128)S(1)}, u32[]{:S(2)}, u32[]{:S(2)}) collective-permute-start(f32[48,512]{1,0:T(8,128)S(1)} %shard_map.222.refs_4_), channel_id=1, source_target_pairs={{0,16},{1,17},{2,18},{3,19},{4,20},{5,21},{6,22},{7,23},{8,24},{9,... | collective-permute-start | bytes 294920 | tf_op jit(solution)/shard_map/ppermute | solution.py:207
  132.1 5.8 %collective-permute-start.32 = (f32[16,512]{1,0:T(8,128)S(1)}, f32[16,512]{1,0:T(8,128)S(1)}, u32[]{:S(2)}, u32[]{:S(2)}) collective-permute-start(f32[16,512]{1,0:T(8,128)S(1)} %shard_map.225.refs_6_), channel_id=1, source_target_pairs={{0,24},{1,25},{2,26},{3,27},{4,28},{5,29},{6,30},{7,31},{8,16},{9,... | collective-permute-start | bytes 98312 | tf_op jit(solution)/shard_map/ppermute | solution.py:70
  133.4 6.6 %collective-permute-start.31 = (f32[16,512]{1,0:T(8,128)S(1)}, f32[16,512]{1,0:T(8,128)S(1)}, u32[]{:S(2)}, u32[]{:S(2)}) collective-permute-start(f32[16,512]{1,0:T(8,128)S(1)} %shard_map.225.refs_6_), channel_id=1, source_target_pairs={{0,16},{1,17},{2,18},{3,19},{4,20},{5,21},{6,22},{7,23},{8,24},{9,... | collective-permute-start | bytes 98312 | tf_op jit(solution)/shard_map/ppermute | solution.py:70
  134.6 12.0 %collective-permute-start.36 = (f32[384,512]{1,0:T(8,128)S(1)}, f32[384,512]{1,0:T(8,128)S(1)}, u32[]{:S(2)}, u32[]{:S(2)}) collective-permute-start(f32[384,512]{1,0:T(8,128)S(1)} %shard_map.224.refs_5_), channel_id=1, source_target_pairs={{0,2},{1,5},{2,0},{3,7},{4,6},{5,1},{6,4},{7,3},{8,10},{9,13},{10,... | collective-permute-start | bytes 2359304 | tf_op jit(solution)/shard_map/ppermute | solution.py:207
  136.7 11.7 %collective-permute-start.35 = (f32[48,512]{1,0:T(8,128)S(1)}, f32[48,512]{1,0:T(8,128)S(1)}, u32[]{:S(2)}, u32[]{:S(2)}) collective-permute-start(f32[48,512]{1,0:T(8,128)S(1)} %shard_map.226.refs_18_.refs_0_), channel_id=1, source_target_pairs={{0,16},{1,17},{2,18},{3,19},{4,20},{5,21},{6,22},{7,23},{8,24},{9,... | collective-permute-start | bytes 294920 | tf_op jit(solution)/shard_map/ppermute | solution.py:207
  144.5 5.9 %collective-permute-start.34 = (f32[528,512]{1,0:T(8,128)S(1)}, f32[528,512]{1,0:T(8,128)S(1)}, u32[]{:S(2)}, u32[]{:S(2)}) collective-permute-start(f32[528,512]{1,0:T(8,128)S(1)} %get-tuple-element.138.refs_2_), channel_id=1, source_target_pairs={{0,1},{1,0},{2,3},{3,2},{4,5},{5,4},{6,7},{7,6},{8,9},{9,8},{10,11... | collective-permute-start | bytes 3244040 | tf_op jit(solution)/shard_map/ppermute | solution.py:207
  146.7 12.1 %collective-permute-start.38 = (f32[192,512]{1,0:T(8,128)S(1)}, f32[192,512]{1,0:T(8,128)S(1)}, u32[]{:S(2)}, u32[]{:S(2)}) collective-permute-start(f32[192,512]{1,0:T(8,128)S(1)} %shard_map.231.refs_2_), channel_id=1, source_target_pairs={{0,4},{1,3},{2,6},{3,1},{4,0},{5,7},{6,2},{7,5},{8,12},{9,11},{10,... | collective-permute-start | bytes 1179656 | tf_op jit(solution)/shard_map/ppermute | solution.py:207
  148.5 13.1 %collective-permute-start.41 = (f32[96,512]{1,0:T(8,128)S(1)}, f32[96,512]{1,0:T(8,128)S(1)}, u32[]{:S(2)}, u32[]{:S(2)}) collective-permute-start(f32[96,512]{1,0:T(8,128)S(1)} %shard_map.232.refs_3_.refs_0_), channel_id=1, source_target_pairs={{0,8},{1,9},{2,10},{3,11},{4,12},{5,13},{6,14},{7,15},{8,0},{9,1},... | collective-permute-start | bytes 589832 | tf_op jit(solution)/shard_map/ppermute | solution.py:207
  150.4 10.0 %collective-permute-start.37 = (f32[272,512]{1,0:T(8,128)S(1)}, f32[272,512]{1,0:T(8,128)S(1)}, u32[]{:S(2)}, u32[]{:S(2)}) collective-permute-start(f32[272,512]{1,0:T(8,128)S(1)} %shard_map.233.refs_4_.refs_3_), channel_id=1, source_target_pairs={{0,2},{1,5},{2,0},{3,7},{4,6},{5,1},{6,4},{7,3},{8,10},{9,13},{10,... | collective-permute-start | bytes 1671176 | tf_op jit(solution)/shard_map/ppermute | solution.py:207
  158.8 5.8 %collective-permute-start.40 = (f32[96,512]{1,0:T(8,128)S(1)}, f32[96,512]{1,0:T(8,128)S(1)}, u32[]{:S(2)}, u32[]{:S(2)}) collective-permute-start(f32[96,512]{1,0:T(8,128)S(1)} %shard_map.234.refs_4_), channel_id=1, source_target_pairs={{0,8},{1,9},{2,10},{3,11},{4,12},{5,13},{6,14},{7,15},{8,0},{9,1},... | collective-permute-start | bytes 589832 | tf_op jit(solution)/shard_map/ppermute | solution.py:207
  160.5 7.0 %collective-permute-start.39 = (f32[144,512]{1,0:T(8,128)S(1)}, f32[144,512]{1,0:T(8,128)S(1)}, u32[]{:S(2)}, u32[]{:S(2)}) collective-permute-start(f32[144,512]{1,0:T(8,128)S(1)} %shard_map.235.refs_2_.refs_4_), channel_id=1, source_target_pairs={{0,4},{1,3},{2,6},{3,1},{4,0},{5,7},{6,2},{7,5},{8,12},{9,11},{10,... | collective-permute-start | bytes 884744 | tf_op jit(solution)/shard_map/ppermute | solution.py:207
  161.6 12.5 %collective-permute-start.43 = (f32[192,512]{1,0:T(8,128)S(1)}, f32[192,512]{1,0:T(8,128)S(1)}, u32[]{:S(2)}, u32[]{:S(2)}) collective-permute-start(f32[192,512]{1,0:T(8,128)S(1)} %shard_map.236.refs_5_.refs_0_), channel_id=1, source_target_pairs={{0,4},{1,3},{2,6},{3,1},{4,0},{5,7},{6,2},{7,5},{8,12},{9,11},{10,... | collective-permute-start | bytes 1179656 | tf_op jit(solution)/shard_map/ppermute | solution.py:207
  164.7 5.8 %collective-permute-start.44 = (f32[48,512]{1,0:T(8,128)S(1)}, f32[48,512]{1,0:T(8,128)S(1)}, u32[]{:S(2)}, u32[]{:S(2)}) collective-permute-start(f32[48,512]{1,0:T(8,128)S(1)} %shard_map.237.refs_5_), channel_id=1, source_target_pairs={{0,16},{1,17},{2,18},{3,19},{4,20},{5,21},{6,22},{7,23},{8,24},{9,... | collective-permute-start | bytes 294920 | tf_op jit(solution)/shard_map/ppermute | solution.py:207
  167.5 7.6 %collective-permute-start.42 = (f32[80,512]{1,0:T(8,128)S(1)}, f32[80,512]{1,0:T(8,128)S(1)}, u32[]{:S(2)}, u32[]{:S(2)}) collective-permute-start(f32[80,512]{1,0:T(8,128)S(1)} %shard_map.238.refs_6_.refs_5_), channel_id=1, source_target_pairs={{0,8},{1,9},{2,10},{3,11},{4,12},{5,13},{6,14},{7,15},{8,0},{9,1},... | collective-permute-start | bytes 491528 | tf_op jit(solution)/shard_map/ppermute | solution.py:207
  170.6 8.4 %collective-permute-start.46 = (f32[48,512]{1,0:T(8,128)S(1)}, f32[48,512]{1,0:T(8,128)S(1)}, u32[]{:S(2)}, u32[]{:S(2)}) collective-permute-start(f32[48,512]{1,0:T(8,128)S(1)} %shard_map.239.refs_2_.refs_0_), channel_id=1, source_target_pairs={{0,16},{1,17},{2,18},{3,19},{4,20},{5,21},{6,22},{7,23},{8,24},{9,... | collective-permute-start | bytes 294920 | tf_op jit(solution)/shard_map/ppermute | solution.py:207
  174.1 16.3 %collective-permute-start.48 = (f32[384,512]{1,0:T(8,128)S(1)}, f32[384,512]{1,0:T(8,128)S(1)}, u32[]{:S(2)}, u32[]{:S(2)}) collective-permute-start(f32[384,512]{1,0:T(8,128)S(1)} %shard_map.240.refs_6_.refs_0_), channel_id=1, source_target_pairs={{0,2},{1,5},{2,0},{3,7},{4,6},{5,1},{6,4},{7,3},{8,10},{9,13},{10,... | collective-permute-start | bytes 2359304 | tf_op jit(solution)/shard_map/ppermute | solution.py:207
  175.1 5.9 %collective-permute-start.45 = (f32[48,512]{1,0:T(8,128)S(1)}, f32[48,512]{1,0:T(8,128)S(1)}, u32[]{:S(2)}, u32[]{:S(2)}) collective-permute-start(f32[48,512]{1,0:T(8,128)S(1)} %shard_map.241.refs_2_.refs_6_), channel_id=1, source_target_pairs={{0,16},{1,17},{2,18},{3,19},{4,20},{5,21},{6,22},{7,23},{8,24},{9,... | collective-permute-start | bytes 294920 | tf_op jit(solution)/shard_map/ppermute | solution.py:207
  178.9 6.4 %collective-permute-start.47 = (f32[96,512]{1,0:T(8,128)S(1)}, f32[96,512]{1,0:T(8,128)S(1)}, u32[]{:S(2)}, u32[]{:S(2)}) collective-permute-start(f32[96,512]{1,0:T(8,128)S(1)} %shard_map.242.refs_7_.refs_0_), channel_id=1, source_target_pairs={{0,8},{1,9},{2,10},{3,11},{4,12},{5,13},{6,14},{7,15},{8,0},{9,1},... | collective-permute-start | bytes 589832 | tf_op jit(solution)/shard_map/ppermute | solution.py:207
  181.1 8.3 %collective-permute-start.49 = (f32[32,512]{1,0:T(8,128)S(1)}, f32[32,512]{1,0:T(8,128)S(1)}, u32[]{:S(2)}, u32[]{:S(2)}) collective-permute-start(f32[32,512]{1,0:T(8,128)S(1)} %slice.4.refs_0_), channel_id=1, source_target_pairs={{0,16},{1,17},{2,18},{3,19},{4,20},{5,21},{6,22},{7,23},{8,24},{9,... | collective-permute-start | bytes 196616 | tf_op jit(solution)/shard_map/ppermute | solution.py:207
  185.4 7.8 %collective-permute-start.51 = (f32[192,512]{1,0:T(8,128)S(1)}, f32[192,512]{1,0:T(8,128)S(1)}, u32[]{:S(2)}, u32[]{:S(2)}) collective-permute-start(f32[192,512]{1,0:T(8,128)S(1)} %shard_map.244.refs_11_.refs_0_), channel_id=1, source_target_pairs={{0,4},{1,3},{2,6},{3,1},{4,0},{5,7},{6,2},{7,5},{8,12},{9,11},{10,... | collective-permute-start | bytes 1179656 | tf_op jit(solution)/shard_map/ppermute | solution.py:207
  195.1 9.3 %collective-permute-start.54 = (f32[128,512]{1,0:T(8,128)S(1)}, f32[128,512]{1,0:T(8,128)S(1)}, u32[]{:S(2)}, u32[]{:S(2)}) collective-permute-start(f32[128,512]{1,0:T(8,128)S(1)} %shard_map.249.refs_0_.refs_2_), channel_id=1, source_target_pairs={{0,4},{1,3},{2,6},{3,1},{4,0},{5,7},{6,2},{7,5},{8,12},{9,11},{10,... | collective-permute-start | bytes 786440 | tf_op jit(solution)/shard_map/ppermute | solution.py:207
  195.8 12.0 %collective-permute-start.52 = (f32[384,512]{1,0:T(8,128)S(1)}, f32[384,512]{1,0:T(8,128)S(1)}, u32[]{:S(2)}, u32[]{:S(2)}) collective-permute-start(f32[384,512]{1,0:T(8,128)S(1)} %shard_map.248.refs_2_.refs_0_), channel_id=1, source_target_pairs={{0,2},{1,5},{2,0},{3,7},{4,6},{5,1},{6,4},{7,3},{8,10},{9,13},{10,... | collective-permute-start | bytes 2359304 | tf_op jit(solution)/shard_map/ppermute | solution.py:207
  197.0 16.9 %collective-permute-start.50 = (f32[768,512]{1,0:T(8,128)S(1)}, f32[768,512]{1,0:T(8,128)S(1)}, u32[]{:S(2)}, u32[]{:S(2)}) collective-permute-start(f32[768,512]{1,0:T(8,128)S(1)} %shard_map.247.refs_2_.refs_0_), channel_id=1, source_target_pairs={{0,1},{1,0},{2,3},{3,2},{4,5},{5,4},{6,7},{7,6},{8,9},{9,8},{10,11... | collective-permute-start | bytes 4718600 | tf_op jit(solution)/shard_map/ppermute | solution.py:207
  204.5 9.2 %collective-permute-start.56 = (f32[256,512]{1,0:T(8,128)S(1)}, f32[256,512]{1,0:T(8,128)S(1)}, u32[]{:S(2)}, u32[]{:S(2)}) collective-permute-start(f32[256,512]{1,0:T(8,128)S(1)} %shard_map.250.refs_2_.refs_0_), channel_id=1, source_target_pairs={{0,2},{1,5},{2,0},{3,7},{4,6},{5,1},{6,4},{7,3},{8,10},{9,13},{10,... | collective-permute-start | bytes 1572872 | tf_op jit(solution)/shard_map/ppermute | solution.py:207
  207.9 8.6 %collective-permute-start.55 = (f32[768,512]{1,0:T(8,128)S(1)}, f32[768,512]{1,0:T(8,128)S(1)}, u32[]{:S(2)}, u32[]{:S(2)}) collective-permute-start(f32[768,512]{1,0:T(8,128)S(1)} %shard_map.251.refs_2_), channel_id=1, source_target_pairs={{0,1},{1,0},{2,3},{3,2},{4,5},{5,4},{6,7},{7,6},{8,9},{9,8},{10,11... | collective-permute-start | bytes 4718600 | tf_op jit(solution)/shard_map/ppermute | solution.py:207
  (50 other events, 601.3 us)

commit v3 on v2

--- a/solution.py
+++ b/solution.py
@@ -29,7 +29,7 @@
     return lax.dot_general(left, right, (((1,), (1,)), ((), ())), preferred_element_type=F32)
 
 
-def run(body, outs, operands, after=(), scratch=(), limit=12, weight=1 << 33):
+def run(body, outs, operands, after=(), scratch=(), limit=24, weight=1 << 33):
     vmem = pl.BlockSpec(memory_space=pltpu.VMEM)
     anywhere = pl.BlockSpec(memory_space=pl.ANY)
     first, second = len(operands), len(operands) + len(after)
@@ -260,13 +260,41 @@
         out[rows:, :] = mine[-extra:, :] + other[-extra:, :]
 
 
-def join_body(first, second, out):
-    out[: first.shape[0], :] = first[...]
-    out[first.shape[0] :, :] = second[...]
+def spokes_body(rows, extra, *refs):
+    near, far = refs[:2]
+    received, mine, outs = refs[2:-4], refs[-4], refs[-3:]
+    for slot, out in enumerate(outs, 1):
+        total = near[...] if slot == 1 else far[(slot - 2) * rows : (slot - 1) * rows, :]
+        for ref in received:
+            total += ref[slot * rows : (slot + 1) * rows, :]
+        out[:rows, :] = total
+        if extra:
+            out[rows:, :] = mine[-extra:, :] + received[-1][-extra:, :]
+
+
+def hub_body(rows, extra, *refs):
+    kept, received, mine, spokes, out = refs[0], refs[1:-5], refs[-5], refs[-4:-1], refs[-1]
+    total = kept[...]
+    for ref in received + spokes:
+        total += ref[:rows, :]
+    out[:rows, :] = total
+    if extra:
+        total = mine[-extra:, :]
+        for ref in spokes:
+            total += ref[-extra:, :]
+        out[rows:, :] = total
+
+
+def join_body(*refs):
+    out = refs[-1]
+    rows = refs[0].shape[0]
+    for j, ref in enumerate(refs[:-1]):
+        out[j * rows : (j + 1) * rows] = ref[...]
 
 
 class Bulk:
-    def __init__(self, count, lefts, rights, pairs, after=(), extra=()):
+    def __init__(self, count, lefts, rights, pairs, after=(), extra=(), hub=False, weight=1 << 33):
+        self.hub = hub
         self.bits = partners(count)
         self.extra = extra[0].shape[0] if extra else 0
         width = 512
@@ -281,6 +309,7 @@
             after,
             [pltpu.VMEM((lefts[pair[0]].shape[1], width), F32) for pair in pairs],
             limit=16,
+            weight=weight,
         )
         self.received = []
         self.sent = None
@@ -300,12 +329,37 @@
 
     def send(self, after=()):
         level = len(self.received)
+        if self.hub and level == LEVELS - 2:
+            shape = (self.rows + self.extra, self.parts[LEVELS].shape[1])
+            sent = run(
+                functools.partial(spokes_body, self.rows, self.extra),
+                [(shape, F32)] * 3,
+                [self.parts[LEVELS - 1], self.parts[LEVELS - 2]] + self.received + [self.sent],
+                after,
+                limit=8,
+            )
+            self.sent, self.spokes = sent[0], self.with_partners(sent)
+            return self.sent
         self.sent = self.reduced(level, after)
         self.received.append(with_partner(self.sent, self.bits[level]))
         return self.sent
 
+    def with_partners(self, values):
+        far, near = self.bits[LEVELS - 2][0], self.bits[LEVELS - 1][0]
+        masks = (near, far, near | far)
+        return [swap(value, 1, mask) for value, mask in zip(values, masks)]
+
     def settle(self, after=()):
-        value = self.reduced(LEVELS, after)
+        if self.hub:
+            (value,) = run(
+                functools.partial(hub_body, self.rows, self.extra),
+                [((self.rows + self.extra, self.parts[LEVELS].shape[1]), F32)],
+                [self.parts[LEVELS]] + self.received + [self.sent] + self.spokes,
+                after,
+                limit=8,
+            )
+        else:
+            value = self.reduced(LEVELS, after)
         for even, odd in self.bits[LEVELS:]:
             other = with_partner(value, (even, odd))
             (value,) = run(
@@ -316,21 +370,25 @@
 
     def fetch(self, after=()):
         if self.level < LEVELS - 1:
+            parts = [self.value] + self.others
             (self.value,) = run(
                 join_body,
-                [((2 * self.value.shape[0], self.value.shape[1]), F32)],
-                [self.value, self.other],
+                [((len(parts) * self.value.shape[0], self.value.shape[1]), F32)],
+                parts,
                 after,
                 limit=8,
             )
-        self.other = with_partner(self.value, self.bits[self.level])
-        self.level -= 1
+        if self.hub and self.level == LEVELS - 1:
+            self.others = self.with_partners([self.value] * 3)
+            self.level -= 2
+        else:
+            self.others = [with_partner(self.value, self.bits[self.level])]
+            self.level -= 1
         return self.value
 
 
-def unpack_body(count, width, layout, *refs):
-    n_in = 2 * len(layout)
-    outs, sem = refs[n_in:-1], refs[-1]
+def unpack_body(count, width, layout, n_after, *refs):
+    outs, sem = refs[2 * len(layout) + n_after : -1], refs[-1]
     owns = own_chunk(count), own_chunk(count, True)
     copies = []
     for piece, places in enumerate(layout):
@@ -355,17 +413,17 @@
         copy.wait()
 
 
-def unpack(count, bulks, layout, shapes):
-    operands = [value for bulk in bulks for value in (bulk.value, bulk.other)]
+def unpack(count, bulks, layout, shapes, after=()):
+    operands = [value for bulk in bulks for value in (bulk.value, bulk.others[0])]
     anywhere = pl.BlockSpec(memory_space=pl.ANY)
     return pl.pallas_call(
-        functools.partial(unpack_body, count, operands[0].shape[1], layout),
+        functools.partial(unpack_body, count, operands[0].shape[1], layout, len(after)),
         out_shape=[jax.ShapeDtypeStruct(shape, F32) for shape in shapes],
-        in_specs=[anywhere] * len(operands),
+        in_specs=[anywhere] * (len(operands) + len(after)),
         out_specs=[anywhere] * len(shapes),
         scratch_shapes=[pltpu.SemaphoreType.DMA],
         compiler_params=pltpu.CompilerParams(vmem_limit_bytes=4 * MIB),
-    )(*operands)
+    )(*operands, *after)
 
 
 def steps(span, backward, body, start, unroll=8):
@@ -433,25 +491,72 @@
     return y * cdf, cdf + y * pdf
 
 
-def sigmoid(x):
-    return 1.0 / (1.0 + jnp.exp(-x))
-
-
-CHUNK = 16
-
-
-def prepare_body(plan, span, lens_ref, x_ref, nu_ref, phase_ref, gamma_ref, *outs):
-    sums_ref, tm_ref, mask_ref, decay_ref = outs[:4]
-    factor_refs = outs[4:]
+sigmoid = jax.nn.sigmoid
+
+
+CHUNK = 64
+PIECE = 8
+
+
+def prepare_body(plan, span, lengths_any, x_any, nu_any, phase_any, *outs):
+    lens_ref, sums_ref, tm_ref, mask_ref, decay_ref = outs[:5]
+    factor_refs = outs[5 : 5 + len(plan)]
+    lengths_ref, x_ref, nu_ref, phase_ref, sems = outs[5 + len(plan) :]
     seqs, _, width = x_ref.shape
     states = nu_ref.shape[-1]
+    copies = [
+        pltpu.make_async_copy(
+            x_any.at[:, pl.ds(t0, PIECE), :], x_ref.at[:, pl.ds(t0, PIECE), :], sems.at[t0 // PIECE]
+        )
+        for t0 in range(0, span, PIECE)
+    ]
+    small = [
+        pltpu.make_async_copy(nu_any, nu_ref, sems.at[len(copies)]),
+        pltpu.make_async_copy(phase_any, phase_ref, sems.at[len(copies) + 1]),
+        pltpu.make_async_copy(lengths_any, lengths_ref, sems.at[len(copies) + 2]),
+    ]
+    for copy in small + copies:
+        copy.start()
+    for copy in small:
+        copy.wait()
     here = lax.axis_index("tm")
-    rel = jnp.broadcast_to(lens_ref[...] - here * span, (seqs, LANES))
+    row = lax.broadcasted_iota(jnp.int32, (seqs, LANES), 0)
+    lens = jnp.zeros((seqs, LANES), jnp.int32)
+    for seq in range(seqs):
+        lens = jnp.where(row == seq, lengths_ref[seq], lens)
+    lens_ref[...] = lens
+    rel = lens - here * span
+    rate = jnp.exp(nu_ref[...])
+    radius = jnp.exp(-rate)
+    angle = phase_ref[...]
+    cosine, sine = jnp.cos(angle), jnp.sin(angle)
+    gamma = jnp.sqrt(one_less_exp(2.0 * rate))
+    for row, value in enumerate((radius * cosine, radius * sine, gamma, rate, radius, cosine, sine)):
+        for k in range(2):
+            decay_ref[k, row : row + 1, :] = value[k : k + 1, :]
+    for k in range(2):
+        for level, (radix, stride) in enumerate(plan):
+            base = lax.div(here, radix * stride) * (radix * stride)
+            for member in range(radix):
+                start = (base + member * stride) * span
+                count = jnp.concatenate(
+                    [jnp.clip(lens - start, 0, stride * span)] * (states // LANES), axis=1
+                )
+                power = (decay_ref[k, 0:1, :], decay_ref[k, 1:2, :])
+                re, im = jnp.ones((seqs, states), F32), jnp.zeros((seqs, states), F32)
+                for bit in range((span * stride).bit_length()):
+                    taken = jnp.bitwise_and(count, 1 << bit) != 0
+                    next_re, next_im = mul(re, im, *power)
+                    re, im = jnp.where(taken, next_re, re), jnp.where(taken, next_im, im)
+                    power = mul(*power, *power)
+                factor_refs[level][k, member, :, :states] = re
+                factor_refs[level][k, member, :, states:] = im
     first = jnp.zeros((seqs, width), F32)
     second = jnp.zeros((seqs, width), F32)
-    for t0 in range(0, span, 8):
-        piece = jnp.swapaxes(x_ref[:, t0 : t0 + 8, :], 0, 1)
-        for j in range(8):
+    for t0 in range(0, span, PIECE):
+        copies[t0 // PIECE].wait()
+        piece = jnp.swapaxes(x_ref[:, t0 : t0 + PIECE, :], 0, 1)
+        for j in range(PIECE):
             rows = piece[j]
             mask = jnp.where(rel > t0 + j, 1.0, 0.0)
             place = slice((t0 + j) * seqs, (t0 + j + 1) * seqs)
@@ -461,40 +566,22 @@
             first += live
             second += live * rows
     spread(sums_ref, jnp.sum(first, 0, keepdims=True), jnp.sum(second, 0, keepdims=True))
-    rate = jnp.exp(nu_ref[...])
-    radius = jnp.exp(-rate)
-    angle = phase_ref[...]
-    cosine, sine = jnp.cos(angle), jnp.sin(angle)
-    gamma = gamma_ref[...]
-    for row, value in enumerate((radius * cosine, radius * sine, gamma, rate, radius, cosine, sine)):
-        for k in range(2):
-            decay_ref[k, row : row + 1, :] = value[k : k + 1, :]
-    for k in range(2):
-        for level, (radix, stride) in enumerate(plan):
-            base = lax.div(here, radix * stride) * (radix * stride)
-            for member in range(radix):
-                start = (base + member * stride) * span
-                count = jnp.clip(lens_ref[...] - start, 0, stride * span)
-                count = jnp.broadcast_to(count, (seqs, states))
-                power = (decay_ref[k, 0:1, :], decay_ref[k, 1:2, :])
-                re, im = jnp.ones((seqs, states), F32), jnp.zeros((seqs, states), F32)
-                for bit in range((span * stride).bit_length()):
-                    taken = jnp.bitwise_and(count, 1 << bit) != 0
-                    next_re, next_im = mul(re, im, *power)
-                    re, im = jnp.where(taken, next_re, re), jnp.where(taken, next_im, im)
-                    power = mul(*power, *power)
-                factor_refs[level][k, member, :, :states] = re
-                factor_refs[level][k, member, :, states:] = im
+
+
+def one_less_exp(x):
+    total = 1.0
+    for n in range(8, 1, -1):
+        total = 1.0 - total * x * (1.0 / n)
+    return total * x
 
 
 def relative(lens_ref, span, states):
-    return jnp.broadcast_to(
-        lens_ref[...] - lax.axis_index("tm") * span, (lens_ref.shape[0], states)
-    )
+    rel = lens_ref[...] - lax.axis_index("tm") * span
+    return jnp.concatenate([rel] * (states // LANES), axis=1)
 
 
 def token_scale(lens_ref):
-    return 1.0 / jnp.sum(lens_ref[...].astype(F32), axis=0, keepdims=True)
+    return 1.0 / jnp.sum(lens_ref[:, 0:1].astype(F32), axis=0, keepdims=True)
 
 
 def project_body(
@@ -745,7 +832,7 @@
     stats_refs = (stats0_ref, stats1_ref)
     small = total_ref[total_ref.shape[0] - 16 :, :]
     states = decay_ref.shape[-1]
-    count = jnp.sum(lens_ref[...].astype(F32), axis=0, keepdims=True)
+    count = jnp.sum(lens_ref[:, 0:1].astype(F32), axis=0, keepdims=True)
     for k in range(2):
         _, _, gamma, rate, radius, cosine, sine = (decay_ref[k, j : j + 1, :] for j in range(7))
         sum_re, sum_im = small[8 * k : 8 * k + 1, :states], small[8 * k : 8 * k + 1, states:]
@@ -790,7 +877,6 @@
     count = lax.axis_size("tm")
     rows = span * seqs
     plan = stages(count)
-    lens = lengths[:, None]
 
     tile = ((count, 2 * width // LANES, LANES), F32)
     whole, whole_low = ((rows, width), F32), ((rows, width), BF16)
@@ -802,14 +888,25 @@
     seq_major = ((seqs, span, width), F32)
     buffers = entry_scratch(plan, summary[0])
 
-    prepared = run(
+    in_hbm = pl.BlockSpec(memory_space=pltpu.HBM)
+    outs = [((seqs, LANES), jnp.int32), tile, whole, ((rows, LANES), F32), ((2, 8, states), F32)]
+    outs += [((2, radix) + summary[0], F32) for radix, _ in plan]
+    prepared = pl.pallas_call(
         functools.partial(prepare_body, plan, span),
-        [tile, whole, ((rows, LANES), F32), ((2, 8, states), F32)]
-        + [((2, radix) + summary[0], F32) for radix, _ in plan],
-        [lens, inputs, nu_log, phase, jnp.sqrt(-jnp.expm1(-2.0 * jnp.exp(nu_log)))],
-    )
-    sums, x0, mask, decay = prepared[:4]
-    factors = prepared[4:]
+        out_shape=[jax.ShapeDtypeStruct(shape, dtype) for shape, dtype in outs],
+        in_specs=[in_hbm] * 4,
+        out_specs=[pl.BlockSpec(memory_space=pltpu.VMEM)] * len(outs),
+        scratch_shapes=[
+            pltpu.SMEM(lengths.shape, jnp.int32),
+            pltpu.VMEM(inputs.shape, F32),
+            pltpu.VMEM(nu_log.shape, F32),
+            pltpu.VMEM(phase.shape, F32),
+            pltpu.SemaphoreType.DMA((span // PIECE + 3,)),
+        ],
+        compiler_params=pltpu.CompilerParams(vmem_limit_bytes=24 * MIB),
+    )(*(pltpu.with_memory_space_constraint(a, pltpu.HBM) for a in (lengths, inputs, nu_log, phase)))
+    lens, sums, x0, mask, decay = prepared[:5]
+    factors = prepared[5:]
 
     def project(k, sums, x):
         return run(
@@ -818,9 +915,9 @@
             [lens, everywhere(sums), x, bn_gain, bn_bias, w_in, decay],
         )
 
-    def entered(body, outs, held, operands, after=(), limit=12):
+    def entered(body, outs, held, operands, after=(), limit=24, weight=1 << 33):
         operands = entry_operands(held, factors) + operands
-        return run(with_entry(body, plan), outs, operands, after, buffers, limit)
+        return run(with_entry(body, plan), outs, operands, after, buffers, limit, weight)
 
     u0, v0, stats0, part = project(0, sums, x0)
     held = exchange(0, part, plan, factors, False, False)
@@ -840,14 +937,16 @@
     )
 
     flows = {}
-    flows["top"] = Bulk(count, [act1, h1], [dz1, dy1], [(0, 0, 0, 0), (0, 0, 0, width), (1, 0, 1, 0)])
+    flows["top"] = Bulk(
+        count, [act1, h1], [dz1, dy1], [(0, 0, 0, 0), (0, 0, 0, width), (1, 0, 1, 0)], [part]
+    )
     flows["top"].send()
 
     def beside_top(level, group):
         if level == 0:
             return flows["top"].parts[-1:]
-        if level == len(plan) - 2:
-            return [flows["top"].send([group[1]])]
+        if level == len(plan) - 1:
+            flows["step"] = flows["top"].send(group)
         return ()
 
     held = exchange(1, part, plan, factors, False, True, beside_top)
@@ -857,13 +956,17 @@
         [pair_low, eight],
         held,
         [lens, g1, h1, v1, decay],
+        [flows["step"]],
+        weight=1 << 20,
     )
     part1, skip1, sums = run(
         functools.partial(input_body, 1, seqs, True),
         [whole, eight, tile],
         [dv1, dy1, x1, cotangent, stats1, bn_gain, bn_bias, w_in, skip],
-    )
-    top.send([sums])
+        weight=1 << 20,
+    )
+    step = top.send([sums])
+    (sums,) = run(join_body, [tile], [sums], [step], limit=4)
     sums = everywhere(sums)
     step = top.send([sums])
     d0, dz0, dy0, g0, grads1, part = run(
@@ -874,55 +977,73 @@
     )
 
     flows["middle"] = Bulk(
-        count, [act0, h0], [dz0, dy0], [(0, 0, 0, 0), (0, 0, 0, width), (1, seqs, 1, 0)], [part]
+        count, [act0], [dz0], [(0, 0, 0, 0), (0, 0, 0, width)], [part]
     )
     flows["middle"].send()
 
     def beside_middle(level, group):
         if level == 0:
-            return [flows["middle"].parts[-1], top.send([flows["middle"].parts[-1]])]
+            return flows["middle"].parts[-1:]
         if level == len(plan) - 2:
-            return [flows["middle"].send([group[1]])]
+            return [top.send(group[1:2])]
+        if level == len(plan) - 1:
+            flows["step"] = flows["middle"].send(group)
         return ()
 
     held = exchange(0, part, plan, factors, True, True, beside_middle)
     middle = flows["middle"]
-    own = top.settle([held[-1][1]])
-    top.fetch()
+    other = Bulk(
+        count, [u1, h0], [dv1, dy0], [(0, 0, 0, 0), (1, seqs, 1, 0)], [held[-1][1]], weight=1 << 20
+    )
+    other.send()
     dv0, small0 = entered(
         functools.partial(adjoint_body, 0, plan, span, True),
         [pair_low, eight],
         held,
         [lens, g0, h0, v0, decay],
-        [own],
+        [flows["step"], other.parts[-1]],
+        weight=1 << 20,
     )
     part0, skip0, sums = run(
         functools.partial(input_body, 0, seqs, False),
         [whole, eight, ((2, 8, width), F32)],
         [dv0, dy0, x0, d0, stats0, bn_gain, bn_bias, w_in, skip],
+        weight=1 << 20,
     )
 
     (small,) = run(small_body, [((16, width), F32)], [small0, skip0, sums, small1, skip1], limit=4)
-    last = Bulk(
-        count, [u0, u1], [dv0, dv1], [(0, 0, 0, 0), (1, 0, 1, 0)], [part0], [small]
-    )
+    step = top.settle([part0])
+    top.fetch()
+    step = other.send([step])
+    step = middle.send([step])
+    step = top.fetch([step])
+    last = Bulk(count, [u0], [dv0], [(0, 0, 0, 0)], [step], [small], weight=1 << 20)
     last.send()
-    step = middle.send([last.parts[-1]])
-    step = top.fetch([step])
-    step = last.send([step])
+    step = last.parts[-1]
+    step = other.send([step])
     step = middle.send([step])
     step = last.send([step])
+    step = other.send([step])
     step = top.fetch([step])
     step = middle.send([step])
     step = last.send([step])
+    step = other.send([step])
     step = middle.settle([step])
     middle.fetch()
+    step = last.send([step])
+    step = other.settle([step])
+    other.fetch()
     step = top.fetch([step])
+    step = middle.fetch([step])
     step = last.send([step])
+    step = other.fetch([step])
     step = middle.fetch([step])
     step = last.settle([step])
     last.fetch()
+    step = other.fetch([step])
+    step = last.fetch([step])
     step = middle.fetch([step])
+    step = last.fetch([step])
     grad_x, g_gain, g_bias, g_nu, g_phase, g_skip, running_out = run(
         functools.partial(finish_body, span),
         [seq_major] + [((2, width), F32)] * 2 + [((2, states), F32)] * 2
@@ -930,20 +1051,20 @@
         [last.total, lens, part0, x0, mask, bn_gain, decay, running, stats0, stats1, grads1],
         [step],
     )
-    step = last.fetch([g_gain])
+    step = other.fetch([g_gain])
     step = top.fetch([step])
-    step = middle.fetch([step])
-    step = last.fetch([step])
     step = last.fetch([step])
     step = middle.fetch([step])
+    step = other.fetch([step])
     step = last.fetch([step])
     g_glu, g_out, g_in = unpack(
         count,
-        [top, middle, last],
+        [top, middle, other, last],
         [
             [(0, 1, 0), (0, 1, width), (1, 1, 0)],
-            [(0, 0, 0), (0, 0, width), (1, 0, 0)],
-            [(2, 0, 0), (2, 1, 0)],
+            [(0, 0, 0), (0, 0, width)],
+            [(2, 1, 0), (1, 0, 0)],
+            [(2, 0, 0)],
         ],
         [(2, width, 2 * width), (2, 2 * states, width), (2, width, 2 * states)],
     )

time: 220 us -> 206 us (0.936)
  waiting for transfers between devices: 74.1 us -> 58.9 us
  starting transfers between devices: 62.5 us -> 69.3 us
  local copies, waits for them, and re-layouts: 4.82 us -> 1.13 us
    ppermute x30 -> x40, waiting for transfers between devices: 50.9 us -> 38 us  [with_partner(): lax.ppermute(value, 'tm', [(i, i ^ (odd if i & 1 else even)) for i in ran...]
    ppermute x30 -> x40, starting transfers between devices: 30.3 us -> 37.6 us  [with_partner(): lax.ppermute(value, 'tm', [(i, i ^ (odd if i & 1 else even)) for i in ran...]
    pallas_call x50 -> x60, Pallas kernels: 34.6 us -> 31.3 us  [run(): pl.pallas_call(kernel, out_shape=[jax.ShapeDtypeStruct(shape, dtype) for...]
    unnamed x48 -> x34, local copies, waits for them, and re-layouts: 4.07 us -> 1.13 us
    pallas_call x0 -> x1, Pallas kernels: none -> 2.6 us  [shards(): pl.pallas_call(functools.partial(prepare_body, plan, span), out_shape=[ja...]
    ppermute x28, waiting for transfers between devices: 23.2 us -> 20.9 us  [swap(): lax.ppermute(value, 'tm', [(i, i ^ stride * mask) for i in range(count)])]
  transfers between devices with their start and end apart: 58 -> 68, of which waited for: 39 -> 40; matrix products, arithmetic and copies ran while one was open for 0% -> 0% of each run, Pallas kernels for 7% -> 9%
where the time goes in v3:
time: 206 us
  starting transfers between devices  69.3 us (34%)
  waiting for transfers between devices  58.9 us (29%)
  blocking collectives  38.1 us (18%)
  Pallas kernels  37.1 us (18%)
    all_to_all x3, blocking collectives, everywhere(): return lax.all_to_all(tiles, 'tm', 0, 0)  38.1 us
    ppermute x40, waiting for transfers between devices, with_partner(): lax.ppermute(value, 'tm', [(i, i ^ (odd if i & 1 else even)) for i in ran...  38 us
    ppermute x40, starting transfers between devices, with_partner(): lax.ppermute(value, 'tm', [(i, i ^ (odd if i & 1 else even)) for i in ran...  37.6 us
    ppermute x28, starting transfers between devices, swap(): lax.ppermute(value, 'tm', [(i, i ^ stride * mask) for i in range(count)])  31.6 us
    pallas_call x60, Pallas kernels, run(): pl.pallas_call(kernel, out_shape=[jax.ShapeDtypeStruct(shape, dtype) for...  31.3 us
    ppermute x28, waiting for transfers between devices, swap(): lax.ppermute(value, 'tm', [(i, i ^ stride * mask) for i in range(count)])  20.9 us
  transfers between devices with their start and end apart: 68, of which 40 were waited for; matrix products, arithmetic and copies ran while one was open for 0% of the time, Pallas kernels for 9%

profile of v3, /device:TPU:0, one launch (start us, length us, event | category | flops | bytes accessed | tf_op | source)
XLA Modules:
  0.0 206.0 jit_solution(15498346245676300601)
XLA Ops:
  0.7 2.6 %shard_map.203 = (s32[16,128]{1,0:T(8,128)S(1)}, f32[32,8,128]{2,1,0:T(8,128)S(1)}, f32[1024,512]{1,0:T(8,128)S(1)}, f32[1024,128]{1,0:T(8,128)S(1)}, f32[2,8,25...) custom-call(s32[16]{0:T(128)} %lengths_any.1, ...), custom_call_target="tpu_custom_call" | custom-call | tf_op jit(solution)/shard_map/pallas_call | solution.py:894
  3.3 15.3 %all_to_all.15.refs_1_ = f32[32,8,128]{2,1,0:T(8,128)S(1)} all-to-all(f32[32,8,128]{2,1,0:T(8,128)S(1)} %get-tuple-element.92), channel_id=1, replica_groups=mesh['tm'=32] {'tm'}, dimensions={0} | all-to-all | bytes 262144 | tf_op jit(solution)/shard_map/all_to_all | solution.py:105
  29.0 2.5 %collective-permute-start.4 = (f32[16,512]{1,0:T(8,128)S(1)}, f32[16,512]{1,0:T(8,128)S(1)}, u32[]{:S(2)}, u32[]{:S(2)}) collective-permute-start(f32[16,512]{1,0:T(8,128)S(1)} %shard_map.206.refs_6_), channel_id=1, source_target_pairs={{0,8},{1,9},{2,10},{3,11},{4,12},{5,13},{6,14},{7,15},{8,0},{9,1},... | collective-permute-start | bytes 98312 | tf_op jit(solution)/shard_map/ppermute | solution.py:70
  33.8 3.6 %shard_map.207 = (f32[1024,512]{1,0:T(8,128)S(1)}, bf16[1040,512]{1,0:T(8,128)(2,1)S(1)}, bf16[1024,512]{1,0:T(8,128)(2,1)S(1)}, bf16[1024,512]{1,0:T(8,128)(2,1...) custom-call(f32[16,512]{1,0:T(8,128)S(1)} %get-tuple-element.95.refs_0_, ...), custom_call_target="tpu_custom_call" | custom-call | flops 8589934592 | tf_op jit(solution)/shard_map/pallas_call | solution.py:40
  37.5 11.6 %all_to_all.16.refs_1_ = f32[32,8,128]{2,1,0:T(8,128)S(1)} all-to-all(f32[32,8,128]{2,1,0:T(8,128)S(1)} %get-tuple-element.102), channel_id=1, replica_groups=mesh['tm'=32] {'tm'}, dimensions={0} | all-to-all | bytes 262144 | tf_op jit(solution)/shard_map/all_to_all | solution.py:105
  59.4 2.5 %collective-permute-start.11 = (f32[16,512]{1,0:T(8,128)S(1)}, f32[16,512]{1,0:T(8,128)S(1)}, u32[]{:S(2)}, u32[]{:S(2)}) collective-permute-start(f32[16,512]{1,0:T(8,128)S(1)} %shard_map.210.refs_6_), channel_id=1, source_target_pairs={{0,8},{1,9},{2,10},{3,11},{4,12},{5,13},{6,14},{7,15},{8,0},{9,1},... | collective-permute-start | bytes 98312 | tf_op jit(solution)/shard_map/ppermute | solution.py:70
  64.2 7.3 %shard_map.211 = (f32[16,64,512]{2,1,0:T(8,128)}, bf16[1040,512]{1,0:T(8,128)(2,1)S(1)}, bf16[1024,512]{1,0:T(8,128)(2,1)S(1)}, bf16[1024,1024]{1,0:T(8,128)(2,1...) custom-call(f32[16,512]{1,0:T(8,128)S(1)} %get-tuple-element.104.refs_0_, ...), custom_call_target="tpu_custom_call" | custom-call | flops 8589934592 | tf_op jit(solution)/shard_map/pallas_call | solution.py:40
  71.4 1.9 shard_map.212
  81.7 2.0 collective-permute-start.20
  90.1 2.0 shard_map.217
  94.0 11.2 %all_to_all.17.refs_4_.refs_1_ = f32[32,8,128]{2,1,0:T(8,128)S(1)} all-to-all(f32[32,8,128]{2,1,0:T(8,128)S(1)} %shard_map.219), channel_id=1, replica_groups=mesh['tm'=32] {'tm'}, dimensions={0} | all-to-all | bytes 262144 | tf_op jit(solution)/shard_map/all_to_all | solution.py:105
  106.0 2.4 %shard_map.221 = (f32[1024,512]{1,0:T(8,128)S(1)}, bf16[1024,1024]{1,0:T(8,128)(2,1)S(1)}, bf16[1024,512]{1,0:T(8,128)(2,1)S(1)}, f32[1024,512]{1,0:T(8,128)S(1)...) custom-call(s32[16,128]{1,0:T(8,128)S(1)} %get-tuple-element.91.refs_0_.refs_13_.refs_1_, ...), custom_call_target="tpu_custom_call" | custom-call | flops 8589934592 | tf_op jit(solution)/shard_map/pallas_call | solution.py:40
  119.9 2.1 %collective-permute-start.33 = (f32[48,512]{1,0:T(8,128)S(1)}, f32[48,512]{1,0:T(8,128)S(1)}, u32[]{:S(2)}, u32[]{:S(2)}) collective-permute-start(f32[48,512]{1,0:T(8,128)S(1)} %shard_map.224.refs_5_), channel_id=1, source_target_pairs={{0,16},{1,17},{2,18},{3,19},{4,20},{5,21},{6,22},{7,23},{8,24},{9,... | collective-permute-start | bytes 294920 | tf_op jit(solution)/shard_map/ppermute | solution.py:207
  130.4 2.5 %collective-permute-done.35.refs_2_ = f32[256,512]{1,0:T(8,128)S(1)} collective-permute-done((f32[256,512]{1,0:T(8,128)S(1)}, f32[256,512]{1,0:T(8,128)S(1)}, u32[]{:S(2)}, u32[]{:S(2)}) %collective-permute-start.35) | collective-permute-done | bytes 524320 | tf_op jit(solution)/shard_map/ppermute | solution.py:207
  134.3 2.0 collective-permute-done.34.refs_1_
  137.3 3.9 %collective-permute-done.39.refs_2_ = f32[256,512]{1,0:T(8,128)S(1)} collective-permute-done((f32[256,512]{1,0:T(8,128)S(1)}, f32[256,512]{1,0:T(8,128)S(1)}, u32[]{:S(2)}, u32[]{:S(2)}) %collective-permute-start.39) | collective-permute-done | bytes 524320 | tf_op jit(solution)/shard_map/ppermute | solution.py:207
  142.8 2.3 %collective-permute-start.41 = (f32[64,512]{1,0:T(8,128)S(1)}, f32[64,512]{1,0:T(8,128)S(1)}, u32[]{:S(2)}, u32[]{:S(2)}) collective-permute-start(f32[64,512]{1,0:T(8,128)S(1)} %shard_map.237.refs_3_), channel_id=1, source_target_pairs={{0,8},{1,9},{2,10},{3,11},{4,12},{5,13},{6,14},{7,15},{8,0},{9,1},... | collective-permute-start | bytes 393224 | tf_op jit(solution)/shard_map/ppermute | solution.py:207
  145.8 3.3 %collective-permute-done.43.refs_3_ = f32[128,512]{1,0:T(8,128)S(1)} collective-permute-done((f32[128,512]{1,0:T(8,128)S(1)}, f32[128,512]{1,0:T(8,128)S(1)}, u32[]{:S(2)}, u32[]{:S(2)}) %collective-permute-start.43) | collective-permute-done | bytes 262176 | tf_op jit(solution)/shard_map/ppermute | solution.py:207
  149.1 3.6 %collective-permute-start.46 = (f32[64,512]{1,0:T(8,128)S(1)}, f32[64,512]{1,0:T(8,128)S(1)}, u32[]{:S(2)}, u32[]{:S(2)}) collective-permute-start(f32[64,512]{1,0:T(8,128)S(1)} %shard_map.239.refs_2_), channel_id=1, source_target_pairs={{0,8},{1,9},{2,10},{3,11},{4,12},{5,13},{6,14},{7,15},{8,0},{9,1},... | collective-permute-start | bytes 393224 | tf_op jit(solution)/shard_map/ppermute | solution.py:207
  156.3 2.2 %collective-permute-start.50 = (f32[32,512]{1,0:T(8,128)S(1)}, f32[32,512]{1,0:T(8,128)S(1)}, u32[]{:S(2)}, u32[]{:S(2)}) collective-permute-start(f32[32,512]{1,0:T(8,128)S(1)} %shard_map.243.refs_6_), channel_id=1, source_target_pairs={{0,16},{1,17},{2,18},{3,19},{4,20},{5,21},{6,22},{7,23},{8,24},{9,... | collective-permute-start | bytes 196616 | tf_op jit(solution)/shard_map/ppermute | solution.py:207
  160.4 1.9 collective-permute-done.44.refs_3_
  162.6 1.8 collective-permute-start.53
  165.7 2.3 %collective-permute-start.52 = (f32[64,512]{1,0:T(8,128)S(1)}, f32[64,512]{1,0:T(8,128)S(1)}, u32[]{:S(2)}, u32[]{:S(2)}) collective-permute-start(f32[64,512]{1,0:T(8,128)S(1)} %shard_map.248.refs_6_.refs_0_), channel_id=1, source_target_pairs={{0,8},{1,9},{2,10},{3,11},{4,12},{5,13},{6,14},{7,15},{8,0},{9,1},... | collective-permute-start | bytes 393224 | tf_op jit(solution)/shard_map/ppermute | solution.py:207
  169.6 1.8 collective-permute-start.55
  172.7 2.2 %collective-permute-done.51.refs_5_ = f32[32,512]{1,0:T(8,128)S(1)} collective-permute-done((f32[32,512]{1,0:T(8,128)S(1)}, f32[32,512]{1,0:T(8,128)S(1)}, u32[]{:S(2)}, u32[]{:S(2)}) %collective-permute-start.51) | collective-permute-done | bytes 65568 | tf_op jit(solution)/shard_map/ppermute | solution.py:207
  177.1 2.6 %collective-permute-done.54.refs_1_ = f32[16,512]{1,0:T(8,128)S(1)} collective-permute-done((f32[16,512]{1,0:T(8,128)S(1)}, f32[16,512]{1,0:T(8,128)S(1)}, u32[]{:S(2)}, u32[]{:S(2)}) %collective-permute-start.54) | collective-permute-done | bytes 32800 | tf_op jit(solution)/shard_map/ppermute | solution.py:207
  180.7 1.8 collective-permute-start.61
  185.1 2.7 %shard_map.257 = (f32[16,64,512]{2,1,0:T(8,128)}, f32[2,512]{1,0:T(2,128)}, f32[2,512]{1,0:T(2,128)}, f32[2,256]{1,0:T(2,128)}, f32[2,256]{1,0:T(2,128)}, /*index=5*/f32[2,512]{1,0:T(2,128)}, f32[2,2,512]{2,1,0:T(2,128)}) custom-call(f32[32,512]{1,0:T(8,128)S(1)} %shard_map.252.refs_2_.refs_0_, s32[16,128]{1,0:T(8,128)S(1)} %get-tuple-element.91.refs_0_.refs_13_.refs_1_, ...), custom_call_target="tpu_custom_call" | custom-call | flops 8589934592 | tf_op jit(solution)/shard_map/pallas_call | solution.py:40
  191.5 6.2 %collective-permute-done.64.refs_1_ = f32[256,512]{1,0:T(8,128)S(1)} collective-permute-done((f32[256,512]{1,0:T(8,128)S(1)}, f32[256,512]{1,0:T(8,128)S(1)}, u32[]{:S(2)}, u32[]{:S(2)}) %collective-permute-start.64) | collective-permute-done | bytes 524320 | tf_op jit(solution)/shard_map/ppermute | solution.py:207
  197.9 2.7 %collective-permute-done.66.refs_1_ = f32[128,512]{1,0:T(8,128)S(1)} collective-permute-done((f32[128,512]{1,0:T(8,128)S(1)}, f32[128,512]{1,0:T(8,128)S(1)}, u32[]{:S(2)}, u32[]{:S(2)}) %collective-permute-start.66) | collective-permute-done | bytes 262176 | tf_op jit(solution)/shard_map/ppermute | solution.py:207
  200.7 1.9 collective-permute-done.67.refs_7_
  202.6 3.2 %shard_map.264 = (f32[2,512,1024]{2,1,0:T(8,128)}, f32[2,512,512]{2,1,0:T(8,128)}, f32[2,512,512]{2,1,0:T(8,128)}) custom-call(f32[768,512]{1,0:T(8,128)S(1)} %shard_map.259.refs_2_.refs_0_, f32[768,512]{1,0:T(8,128)S(1)} %collective-permute-done.60.refs_1_, f32[512,512]{1,0:T(8,128)S(1)} %shard_map.261.refs_2_, ...), custom_call_target="tpu_custom_call" | custom-call | tf_op jit(solution)/shard_map/pallas_call | solution.py:419
  (204 shorter events, 86.7 us)
Async XLA Ops:
  73.4 7.7 %collective-permute-start.21 = (f32[768,512]{1,0:T(8,128)S(1)}, f32[768,512]{1,0:T(8,128)S(1)}, u32[]{:S(2)}, u32[]{:S(2)}) collective-permute-start(f32[768,512]{1,0:T(8,128)S(1)} %get-tuple-element.117), channel_id=1, source_target_pairs={{0,1},{1,0},{2,3},{3,2},{4,5},{5,4},{6,7},{7,6},{8,9},{9,8},{10,11... | collective-permute-start | bytes 4718600 | tf_op jit(solution)/shard_map/ppermute | solution.py:207
  81.2 12.1 %collective-permute-start.22 = (f32[384,512]{1,0:T(8,128)S(1)}, f32[384,512]{1,0:T(8,128)S(1)}, u32[]{:S(2)}, u32[]{:S(2)}) collective-permute-start(f32[384,512]{1,0:T(8,128)S(1)} %shard_map.215.refs_18_), channel_id=1, source_target_pairs={{0,2},{1,5},{2,0},{3,7},{4,6},{5,1},{6,4},{7,3},{8,10},{9,13},{10,... | collective-permute-start | bytes 2359304 | tf_op jit(solution)/shard_map/ppermute | solution.py:207
  93.3 12.0 %collective-permute-start.23 = (f32[192,512]{1,0:T(8,128)S(1)}, f32[192,512]{1,0:T(8,128)S(1)}, u32[]{:S(2)}, u32[]{:S(2)}) collective-permute-start(f32[192,512]{1,0:T(8,128)S(1)} %shard_map.218.refs_1_), channel_id=1, source_target_pairs={{0,4},{1,3},{2,6},{3,1},{4,0},{5,7},{6,2},{7,5},{8,12},{9,11},{10,... | collective-permute-start | bytes 1179656 | tf_op jit(solution)/shard_map/ppermute | solution.py:207
  105.3 8.7 %collective-permute-start.28 = (f32[96,512]{1,0:T(8,128)S(1)}, f32[96,512]{1,0:T(8,128)S(1)}, u32[]{:S(2)}, u32[]{:S(2)}) collective-permute-start(f32[96,512]{1,0:T(8,128)S(1)} %shard_map.220.refs_13_), channel_id=1, source_target_pairs={{0,8},{1,9},{2,10},{3,11},{4,12},{5,13},{6,14},{7,15},{8,0},{9,1},... | collective-permute-start | bytes 589832 | tf_op jit(solution)/shard_map/ppermute | solution.py:207
  110.4 13.1 %collective-permute-start.32 = (f32[512,512]{1,0:T(8,128)S(1)}, f32[512,512]{1,0:T(8,128)S(1)}, u32[]{:S(2)}, u32[]{:S(2)}) collective-permute-start(f32[512,512]{1,0:T(8,128)S(1)} %get-tuple-element.134), channel_id=1, source_target_pairs={{0,1},{1,0},{2,3},{3,2},{4,5},{5,4},{6,7},{7,6},{8,9},{9,8},{10,11... | collective-permute-start | bytes 3145736 | tf_op jit(solution)/shard_map/ppermute | solution.py:207
  117.8 6.9 %collective-permute-start.31 = (f32[16,512]{1,0:T(8,128)S(1)}, f32[16,512]{1,0:T(8,128)S(1)}, u32[]{:S(2)}, u32[]{:S(2)}) collective-permute-start(f32[16,512]{1,0:T(8,128)S(1)} %shard_map.225.refs_2_.refs_6_), channel_id=1, source_target_pairs={{0,24},{1,25},{2,26},{3,27},{4,28},{5,29},{6,30},{7,31},{8,16},{9,... | collective-permute-start | bytes 98312 | tf_op jit(solution)/shard_map/ppermute | solution.py:70
  119.1 6.6 %collective-permute-start.30 = (f32[16,512]{1,0:T(8,128)S(1)}, f32[16,512]{1,0:T(8,128)S(1)}, u32[]{:S(2)}, u32[]{:S(2)}) collective-permute-start(f32[16,512]{1,0:T(8,128)S(1)} %shard_map.225.refs_2_.refs_6_), channel_id=1, source_target_pairs={{0,16},{1,17},{2,18},{3,19},{4,20},{5,21},{6,22},{7,23},{8,24},{9,... | collective-permute-start | bytes 98312 | tf_op jit(solution)/shard_map/ppermute | solution.py:70
  119.9 8.9 %collective-permute-start.33 = (f32[48,512]{1,0:T(8,128)S(1)}, f32[48,512]{1,0:T(8,128)S(1)}, u32[]{:S(2)}, u32[]{:S(2)}) collective-permute-start(f32[48,512]{1,0:T(8,128)S(1)} %shard_map.224.refs_5_), channel_id=1, source_target_pairs={{0,16},{1,17},{2,18},{3,19},{4,20},{5,21},{6,22},{7,23},{8,24},{9,... | collective-permute-start | bytes 294920 | tf_op jit(solution)/shard_map/ppermute | solution.py:207
  123.6 9.2 %collective-permute-start.35 = (f32[256,512]{1,0:T(8,128)S(1)}, f32[256,512]{1,0:T(8,128)S(1)}, u32[]{:S(2)}, u32[]{:S(2)}) collective-permute-start(f32[256,512]{1,0:T(8,128)S(1)} %shard_map.226.refs_18_), channel_id=1, source_target_pairs={{0,2},{1,5},{2,0},{3,7},{4,6},{5,1},{6,4},{7,3},{8,10},{9,13},{10,... | collective-permute-start | bytes 1572872 | tf_op jit(solution)/shard_map/ppermute | solution.py:207
  128.9 7.4 %collective-permute-start.34 = (f32[48,512]{1,0:T(8,128)S(1)}, f32[48,512]{1,0:T(8,128)S(1)}, u32[]{:S(2)}, u32[]{:S(2)}) collective-permute-start(f32[48,512]{1,0:T(8,128)S(1)} %shard_map.231.refs_2_.refs_0_), channel_id=1, source_target_pairs={{0,16},{1,17},{2,18},{3,19},{4,20},{5,21},{6,22},{7,23},{8,24},{9,... | collective-permute-start | bytes 294920 | tf_op jit(solution)/shard_map/ppermute | solution.py:207
  129.2 12.1 %collective-permute-start.39 = (f32[256,512]{1,0:T(8,128)S(1)}, f32[256,512]{1,0:T(8,128)S(1)}, u32[]{:S(2)}, u32[]{:S(2)}) collective-permute-start(f32[256,512]{1,0:T(8,128)S(1)} %shard_map.232.refs_3_), channel_id=1, source_target_pairs={{0,2},{1,5},{2,0},{3,7},{4,6},{5,1},{6,4},{7,3},{8,10},{9,13},{10,... | collective-permute-start | bytes 1572872 | tf_op jit(solution)/shard_map/ppermute | solution.py:207
  132.9 9.9 %collective-permute-start.38 = (f32[128,512]{1,0:T(8,128)S(1)}, f32[128,512]{1,0:T(8,128)S(1)}, u32[]{:S(2)}, u32[]{:S(2)}) collective-permute-start(f32[128,512]{1,0:T(8,128)S(1)} %shard_map.233.refs_2_), channel_id=1, source_target_pairs={{0,4},{1,3},{2,6},{3,1},{4,0},{5,7},{6,2},{7,5},{8,12},{9,11},{10,... | collective-permute-start | bytes 786440 | tf_op jit(solution)/shard_map/ppermute | solution.py:207
  136.3 16.4 %collective-permute-start.42 = (f32[96,512]{1,0:T(8,128)S(1)}, f32[96,512]{1,0:T(8,128)S(1)}, u32[]{:S(2)}, u32[]{:S(2)}) collective-permute-start(f32[96,512]{1,0:T(8,128)S(1)} %shard_map.234.refs_3_.refs_0_), channel_id=1, source_target_pairs={{0,8},{1,9},{2,10},{3,11},{4,12},{5,13},{6,14},{7,15},{8,0},{9,1},... | collective-permute-start | bytes 589832 | tf_op jit(solution)/shard_map/ppermute | solution.py:207
  137.2 7.8 %collective-permute-start.37 = (f32[272,512]{1,0:T(8,128)S(1)}, f32[272,512]{1,0:T(8,128)S(1)}, u32[]{:S(2)}, u32[]{:S(2)}) collective-permute-start(f32[272,512]{1,0:T(8,128)S(1)} %get-tuple-element.150.refs_2_), channel_id=1, source_target_pairs={{0,1},{1,0},{2,3},{3,2},{4,5},{5,4},{6,7},{7,6},{8,9},{9,8},{10,11... | collective-permute-start | bytes 1671176 | tf_op jit(solution)/shard_map/ppermute | solution.py:207
  141.3 7.8 %collective-permute-start.43 = (f32[128,512]{1,0:T(8,128)S(1)}, f32[128,512]{1,0:T(8,128)S(1)}, u32[]{:S(2)}, u32[]{:S(2)}) collective-permute-start(f32[128,512]{1,0:T(8,128)S(1)} %shard_map.236.refs_4_), channel_id=1, source_target_pairs={{0,4},{1,3},{2,6},{3,1},{4,0},{5,7},{6,2},{7,5},{8,12},{9,11},{10,... | collective-permute-start | bytes 786440 | tf_op jit(solution)/shard_map/ppermute | solution.py:207
  142.8 10.8 %collective-permute-start.41 = (f32[64,512]{1,0:T(8,128)S(1)}, f32[64,512]{1,0:T(8,128)S(1)}, u32[]{:S(2)}, u32[]{:S(2)}) collective-permute-start(f32[64,512]{1,0:T(8,128)S(1)} %shard_map.237.refs_3_), channel_id=1, source_target_pairs={{0,8},{1,9},{2,10},{3,11},{4,12},{5,13},{6,14},{7,15},{8,0},{9,1},... | collective-permute-start | bytes 393224 | tf_op jit(solution)/shard_map/ppermute | solution.py:207
  145.1 9.8 %collective-permute-start.40 = (f32[144,512]{1,0:T(8,128)S(1)}, f32[144,512]{1,0:T(8,128)S(1)}, u32[]{:S(2)}, u32[]{:S(2)}) collective-permute-start(f32[144,512]{1,0:T(8,128)S(1)} %shard_map.238.refs_4_.refs_3_), channel_id=1, source_target_pairs={{0,2},{1,5},{2,0},{3,7},{4,6},{5,1},{6,4},{7,3},{8,10},{9,13},{10,... | collective-permute-start | bytes 884744 | tf_op jit(solution)/shard_map/ppermute | solution.py:207
  149.1 7.2 %collective-permute-start.46 = (f32[64,512]{1,0:T(8,128)S(1)}, f32[64,512]{1,0:T(8,128)S(1)}, u32[]{:S(2)}, u32[]{:S(2)}) collective-permute-start(f32[64,512]{1,0:T(8,128)S(1)} %shard_map.239.refs_2_), channel_id=1, source_target_pairs={{0,8},{1,9},{2,10},{3,11},{4,12},{5,13},{6,14},{7,15},{8,0},{9,1},... | collective-permute-start | bytes 393224 | tf_op jit(solution)/shard_map/ppermute | solution.py:207
  152.7 11.7 %collective-permute-start.49 = (f32[192,512]{1,0:T(8,128)S(1)}, f32[192,512]{1,0:T(8,128)S(1)}, u32[]{:S(2)}, u32[]{:S(2)}) collective-permute-start(f32[192,512]{1,0:T(8,128)S(1)} %shard_map.240.refs_5_.refs_0_), channel_id=1, source_target_pairs={{0,4},{1,3},{2,6},{3,1},{4,0},{5,7},{6,2},{7,5},{8,12},{9,11},{10,... | collective-permute-start | bytes 1179656 | tf_op jit(solution)/shard_map/ppermute | solution.py:207
  153.6 6.7 %collective-permute-start.45 = (f32[32,512]{1,0:T(8,128)S(1)}, f32[32,512]{1,0:T(8,128)S(1)}, u32[]{:S(2)}, u32[]{:S(2)}) collective-permute-start(f32[32,512]{1,0:T(8,128)S(1)} %shard_map.241.refs_4_), channel_id=1, source_target_pairs={{0,16},{1,17},{2,18},{3,19},{4,20},{5,21},{6,22},{7,23},{8,24},{9,... | collective-permute-start | bytes 196616 | tf_op jit(solution)/shard_map/ppermute | solution.py:207
  154.9 7.4 %collective-permute-start.44 = (f32[80,512]{1,0:T(8,128)S(1)}, f32[80,512]{1,0:T(8,128)S(1)}, u32[]{:S(2)}, u32[]{:S(2)}) collective-permute-start(f32[80,512]{1,0:T(8,128)S(1)} %shard_map.242.refs_5_.refs_4_), channel_id=1, source_target_pairs={{0,4},{1,3},{2,6},{3,1},{4,0},{5,7},{6,2},{7,5},{8,12},{9,11},{10,... | collective-permute-start | bytes 491528 | tf_op jit(solution)/shard_map/ppermute | solution.py:207
  162.4 7.1 %collective-permute-start.47 = (f32[48,512]{1,0:T(8,128)S(1)}, f32[48,512]{1,0:T(8,128)S(1)}, u32[]{:S(2)}, u32[]{:S(2)}) collective-permute-start(f32[48,512]{1,0:T(8,128)S(1)} %shard_map.245.refs_6_.refs_5_), channel_id=1, source_target_pairs={{0,8},{1,9},{2,10},{3,11},{4,12},{5,13},{6,14},{7,15},{8,0},{9,1},... | collective-permute-start | bytes 294920 | tf_op jit(solution)/shard_map/ppermute | solution.py:207
  162.6 7.0 %collective-permute-start.53 = (f32[32,512]{1,0:T(8,128)S(1)}, f32[32,512]{1,0:T(8,128)S(1)}, u32[]{:S(2)}, u32[]{:S(2)}) collective-permute-start(f32[32,512]{1,0:T(8,128)S(1)} %shard_map.246.refs_2_.refs_0_), channel_id=1, source_target_pairs={{0,16},{1,17},{2,18},{3,19},{4,20},{5,21},{6,22},{7,23},{8,24},{9,... | collective-permute-start | bytes 196616 | tf_op jit(solution)/shard_map/ppermute | solution.py:207
  164.5 25.1 %collective-permute-start.58 = (f32[384,512]{1,0:T(8,128)S(1)}, f32[384,512]{1,0:T(8,128)S(1)}, u32[]{:S(2)}, u32[]{:S(2)}) collective-permute-start(f32[384,512]{1,0:T(8,128)S(1)} %shard_map.247.refs_2_.refs_0_), channel_id=1, source_target_pairs={{0,2},{1,5},{2,0},{3,7},{4,6},{5,1},{6,4},{7,3},{8,10},{9,13},{10,... | collective-permute-start | bytes 2359304 | tf_op jit(solution)/shard_map/ppermute | solution.py:207
  171.4 9.2 %collective-permute-start.57 = (f32[128,512]{1,0:T(8,128)S(1)}, f32[128,512]{1,0:T(8,128)S(1)}, u32[]{:S(2)}, u32[]{:S(2)}) collective-permute-start(f32[128,512]{1,0:T(8,128)S(1)} %shard_map.251.refs_7_.refs_0_), channel_id=1, source_target_pairs={{0,4},{1,3},{2,6},{3,1},{4,0},{5,7},{6,2},{7,5},{8,12},{9,11},{10,... | collective-permute-start | bytes 786440 | tf_op jit(solution)/shard_map/ppermute | solution.py:207
  175.9 11.9 %collective-permute-start.59 = (f32[128,512]{1,0:T(8,128)S(1)}, f32[128,512]{1,0:T(8,128)S(1)}, u32[]{:S(2)}, u32[]{:S(2)}) collective-permute-start(f32[128,512]{1,0:T(8,128)S(1)} %shard_map.253.refs_2_.refs_0_), channel_id=1, source_target_pairs={{0,4},{1,3},{2,6},{3,1},{4,0},{5,7},{6,2},{7,5},{8,12},{9,11},{10,... | collective-permute-start | bytes 786440 | tf_op jit(solution)/shard_map/ppermute | solution.py:207
  180.7 10.6 %collective-permute-start.61 = (f32[256,512]{1,0:T(8,128)S(1)}, f32[256,512]{1,0:T(8,128)S(1)}, u32[]{:S(2)}, u32[]{:S(2)}) collective-permute-start(f32[256,512]{1,0:T(8,128)S(1)} %shard_map.255.refs_2_.refs_0_), channel_id=1, source_target_pairs={{0,2},{1,5},{2,0},{3,7},{4,6},{5,1},{6,4},{7,3},{8,10},{9,13},{10,... | collective-permute-start | bytes 1572872 | tf_op jit(solution)/shard_map/ppermute | solution.py:207
  184.0 6.5 %collective-permute-start.62 = (f32[64,512]{1,0:T(8,128)S(1)}, f32[64,512]{1,0:T(8,128)S(1)}, u32[]{:S(2)}, u32[]{:S(2)}) collective-permute-start(f32[64,512]{1,0:T(8,128)S(1)} %shard_map.256.refs_11_.refs_0_), channel_id=1, source_target_pairs={{0,4},{1,3},{2,6},{3,1},{4,0},{5,7},{6,2},{7,5},{8,12},{9,11},{10,... | collective-permute-start | bytes 393224 | tf_op jit(solution)/shard_map/ppermute | solution.py:207
  188.5 9.2 %collective-permute-start.64 = (f32[256,512]{1,0:T(8,128)S(1)}, f32[256,512]{1,0:T(8,128)S(1)}, u32[]{:S(2)}, u32[]{:S(2)}) collective-permute-start(f32[256,512]{1,0:T(8,128)S(1)} %shard_map.258.refs_2_.refs_0_), channel_id=1, source_target_pairs={{0,2},{1,5},{2,0},{3,7},{4,6},{5,1},{6,4},{7,3},{8,10},{9,13},{10,... | collective-permute-start | bytes 1572872 | tf_op jit(solution)/shard_map/ppermute | solution.py:207
  189.7 12.9 %collective-permute-start.60 = (f32[768,512]{1,0:T(8,128)S(1)}, f32[768,512]{1,0:T(8,128)S(1)}, u32[]{:S(2)}, u32[]{:S(2)}) collective-permute-start(f32[768,512]{1,0:T(8,128)S(1)} %shard_map.259.refs_2_.refs_0_), channel_id=1, source_target_pairs={{0,1},{1,0},{2,3},{3,2},{4,5},{5,4},{6,7},{7,6},{8,9},{9,8},{10,11... | collective-permute-start | bytes 4718600 | tf_op jit(solution)/shard_map/ppermute | solution.py:207
  190.6 10.0 %collective-permute-start.66 = (f32[128,512]{1,0:T(8,128)S(1)}, f32[128,512]{1,0:T(8,128)S(1)}, u32[]{:S(2)}, u32[]{:S(2)}) collective-permute-start(f32[128,512]{1,0:T(8,128)S(1)} %shard_map.260.refs_2_.refs_0_), channel_id=1, source_target_pairs={{0,2},{1,5},{2,0},{3,7},{4,6},{5,1},{6,4},{7,3},{8,10},{9,13},{10,... | collective-permute-start | bytes 786440 | tf_op jit(solution)/shard_map/ppermute | solution.py:207
  191.4 11.1 %collective-permute-start.63 = (f32[512,512]{1,0:T(8,128)S(1)}, f32[512,512]{1,0:T(8,128)S(1)}, u32[]{:S(2)}, u32[]{:S(2)}) collective-permute-start(f32[512,512]{1,0:T(8,128)S(1)} %shard_map.261.refs_2_), channel_id=1, source_target_pairs={{0,1},{1,0},{2,3},{3,2},{4,5},{5,4},{6,7},{7,6},{8,9},{9,8},{10,11... | collective-permute-start | bytes 3145736 | tf_op jit(solution)/shard_map/ppermute | solution.py:207
  (53 other events, 376.9 us)

commit v4 on v3

--- a/solution.py
+++ b/solution.py
@@ -387,8 +387,8 @@
         return self.value
 
 
-def unpack_body(count, width, layout, n_after, *refs):
-    outs, sem = refs[2 * len(layout) + n_after : -1], refs[-1]
+def unpack_body(count, width, layout, n_into, *refs):
+    outs, sem = refs[2 * len(layout) + n_into : -1], refs[-1]
     owns = own_chunk(count), own_chunk(count, True)
     copies = []
     for piece, places in enumerate(layout):
@@ -413,17 +413,18 @@
         copy.wait()
 
 
-def unpack(count, bulks, layout, shapes, after=()):
+def unpack(count, bulks, layout, shapes, into=()):
     operands = [value for bulk in bulks for value in (bulk.value, bulk.others[0])]
     anywhere = pl.BlockSpec(memory_space=pl.ANY)
     return pl.pallas_call(
-        functools.partial(unpack_body, count, operands[0].shape[1], layout, len(after)),
+        functools.partial(unpack_body, count, operands[0].shape[1], layout, len(into)),
         out_shape=[jax.ShapeDtypeStruct(shape, F32) for shape in shapes],
-        in_specs=[anywhere] * (len(operands) + len(after)),
+        in_specs=[anywhere] * (len(operands) + len(into)),
         out_specs=[anywhere] * len(shapes),
         scratch_shapes=[pltpu.SemaphoreType.DMA],
+        input_output_aliases={len(operands) + j: j for j in range(len(into))},
         compiler_params=pltpu.CompilerParams(vmem_limit_bytes=4 * MIB),
-    )(*operands, *after)
+    )(*operands, *into)
 
 
 def steps(span, backward, body, start, unroll=8):
@@ -985,23 +986,24 @@
         if level == 0:
             return flows["middle"].parts[-1:]
         if level == len(plan) - 2:
-            return [top.send(group[1:2])]
+            flows["other"] = Bulk(
+                count, [u1, h0], [dv1, dy0], [(0, 0, 0, 0), (1, seqs, 1, 0)], group[1:2], weight=1 << 20
+            )
+            flows["other"].send()
+            return [top.send(group[1:2]), flows["other"].parts[-1]]
         if level == len(plan) - 1:
             flows["step"] = flows["middle"].send(group)
         return ()
 
     held = exchange(0, part, plan, factors, True, True, beside_middle)
     middle = flows["middle"]
-    other = Bulk(
-        count, [u1, h0], [dv1, dy0], [(0, 0, 0, 0), (1, seqs, 1, 0)], [held[-1][1]], weight=1 << 20
-    )
-    other.send()
+    other = flows["other"]
     dv0, small0 = entered(
         functools.partial(adjoint_body, 0, plan, span, True),
         [pair_low, eight],
         held,
         [lens, g0, h0, v0, decay],
-        [flows["step"], other.parts[-1]],
+        [flows["step"]],
         weight=1 << 20,
     )
     part0, skip0, sums = run(
@@ -1012,17 +1014,17 @@
     )
 
     (small,) = run(small_body, [((16, width), F32)], [small0, skip0, sums, small1, skip1], limit=4)
-    step = top.settle([part0])
+    step = middle.send([part0])
+    step = other.send([step])
+    step = top.settle([step])
     top.fetch()
-    step = other.send([step])
-    step = middle.send([step])
-    step = top.fetch([step])
     last = Bulk(count, [u0], [dv0], [(0, 0, 0, 0)], [step], [small], weight=1 << 20)
     last.send()
     step = last.parts[-1]
+    step = top.fetch([step])
+    step = last.send([step])
     step = other.send([step])
     step = middle.send([step])
-    step = last.send([step])
     step = other.send([step])
     step = top.fetch([step])
     step = middle.send([step])
@@ -1044,6 +1046,9 @@
     step = last.fetch([step])
     step = middle.fetch([step])
     step = last.fetch([step])
+    step = other.fetch([step])
+    step = top.fetch([step])
+    step = last.fetch([step])
     grad_x, g_gain, g_bias, g_nu, g_phase, g_skip, running_out = run(
         functools.partial(finish_body, span),
         [seq_major] + [((2, width), F32)] * 2 + [((2, states), F32)] * 2
@@ -1051,22 +1056,25 @@
         [last.total, lens, part0, x0, mask, bn_gain, decay, running, stats0, stats1, grads1],
         [step],
     )
-    step = other.fetch([g_gain])
-    step = top.fetch([step])
-    step = last.fetch([step])
-    step = middle.fetch([step])
+    step = middle.fetch([g_gain])
     step = other.fetch([step])
     step = last.fetch([step])
+    g_glu, g_out = unpack(
+        count,
+        [top],
+        [[(0, 1, 0), (0, 1, width), (1, 1, 0)]],
+        [(2, width, 2 * width), (2, 2 * states, width)],
+    )
     g_glu, g_out, g_in = unpack(
         count,
-        [top, middle, other, last],
+        [middle, other, last],
         [
-            [(0, 1, 0), (0, 1, width), (1, 1, 0)],
             [(0, 0, 0), (0, 0, width)],
             [(2, 1, 0), (1, 0, 0)],
             [(2, 0, 0)],
         ],
         [(2, width, 2 * width), (2, 2 * states, width), (2, width, 2 * states)],
+        [g_glu, g_out],
     )
     return (output, grad_x, g_gain, g_bias, g_in, g_nu, g_phase, g_out, g_skip, g_glu, running_out)
 

time: 206 us -> 201 us (0.976)
  starting transfers between devices: 69.3 us -> 65.8 us
  waiting for transfers between devices: 58.9 us -> 56.1 us
    ppermute x40, starting transfers between devices: 37.6 us -> 33.3 us  [with_partner(): lax.ppermute(value, 'tm', [(i, i ^ (odd if i & 1 else even)) for i in ran...]
    ppermute x40, waiting for transfers between devices: 38 us -> 34.7 us  [with_partner(): lax.ppermute(value, 'tm', [(i, i ^ (odd if i & 1 else even)) for i in ran...]
  transfers between devices with their start and end apart: 68 -> 68, of which waited for: 40 -> 43; matrix products, arithmetic and copies ran while one was open for 0% -> 0% of each run, Pallas kernels for 9% -> 10%
where the time goes in v4:
time: 201 us
  starting transfers between devices  65.8 us (33%)
  waiting for transfers between devices  56.1 us (28%)
  blocking collectives  38.1 us (19%)
  Pallas kernels  38 us (19%)
    all_to_all x3, blocking collectives, everywhere(): return lax.all_to_all(tiles, 'tm', 0, 0)  38.1 us
    ppermute x40, waiting for transfers between devices, with_partner(): lax.ppermute(value, 'tm', [(i, i ^ (odd if i & 1 else even)) for i in ran...  34.7 us
    ppermute x40, starting transfers between devices, with_partner(): lax.ppermute(value, 'tm', [(i, i ^ (odd if i & 1 else even)) for i in ran...  33.3 us
    ppermute x28, starting transfers between devices, swap(): lax.ppermute(value, 'tm', [(i, i ^ stride * mask) for i in range(count)])  32.5 us
    pallas_call x60, Pallas kernels, run(): pl.pallas_call(kernel, out_shape=[jax.ShapeDtypeStruct(shape, dtype) for...  31.5 us
    ppermute x28, waiting for transfers between devices, swap(): lax.ppermute(value, 'tm', [(i, i ^ stride * mask) for i in range(count)])  21.4 us
  transfers between devices with their start and end apart: 68, of which 43 were waited for; matrix products, arithmetic and copies ran while one was open for 0% of the time, Pallas kernels for 10%

profile of v4, /device:TPU:0, one launch (start us, length us, event | category | flops | bytes accessed | tf_op | source)
XLA Modules:
  0.0 200.6 jit_solution(5571851438062612570)
XLA Ops:
  0.7 2.6 %shard_map.203 = (s32[16,128]{1,0:T(8,128)S(1)}, f32[32,8,128]{2,1,0:T(8,128)S(1)}, f32[1024,512]{1,0:T(8,128)S(1)}, f32[1024,128]{1,0:T(8,128)S(1)}, f32[2,8,25...) custom-call(s32[16]{0:T(128)} %lengths_any.1, ...), custom_call_target="tpu_custom_call" | custom-call | tf_op jit(solution)/shard_map/pallas_call | solution.py:895
  3.3 15.3 %all_to_all.15.refs_1_ = f32[32,8,128]{2,1,0:T(8,128)S(1)} all-to-all(f32[32,8,128]{2,1,0:T(8,128)S(1)} %get-tuple-element.94), channel_id=1, replica_groups=mesh['tm'=32] {'tm'}, dimensions={0} | all-to-all | bytes 262144 | tf_op jit(solution)/shard_map/all_to_all | solution.py:105
  29.1 2.5 %collective-permute-start.4 = (f32[16,512]{1,0:T(8,128)S(1)}, f32[16,512]{1,0:T(8,128)S(1)}, u32[]{:S(2)}, u32[]{:S(2)}) collective-permute-start(f32[16,512]{1,0:T(8,128)S(1)} %shard_map.206.refs_6_), channel_id=1, source_target_pairs={{0,8},{1,9},{2,10},{3,11},{4,12},{5,13},{6,14},{7,15},{8,0},{9,1},... | collective-permute-start | bytes 98312 | tf_op jit(solution)/shard_map/ppermute | solution.py:70
  33.8 3.7 %shard_map.207 = (f32[1024,512]{1,0:T(8,128)S(1)}, bf16[1040,512]{1,0:T(8,128)(2,1)S(1)}, bf16[1024,512]{1,0:T(8,128)(2,1)S(1)}, bf16[1024,512]{1,0:T(8,128)(2,1...) custom-call(f32[16,512]{1,0:T(8,128)S(1)} %get-tuple-element.97.refs_0_, ...), custom_call_target="tpu_custom_call" | custom-call | flops 8589934592 | tf_op jit(solution)/shard_map/pallas_call | solution.py:40
  37.6 11.6 %all_to_all.16.refs_1_ = f32[32,8,128]{2,1,0:T(8,128)S(1)} all-to-all(f32[32,8,128]{2,1,0:T(8,128)S(1)} %get-tuple-element.104), channel_id=1, replica_groups=mesh['tm'=32] {'tm'}, dimensions={0} | all-to-all | bytes 262144 | tf_op jit(solution)/shard_map/all_to_all | solution.py:105
  59.5 2.5 %collective-permute-start.11 = (f32[16,512]{1,0:T(8,128)S(1)}, f32[16,512]{1,0:T(8,128)S(1)}, u32[]{:S(2)}, u32[]{:S(2)}) collective-permute-start(f32[16,512]{1,0:T(8,128)S(1)} %shard_map.210.refs_6_), channel_id=1, source_target_pairs={{0,8},{1,9},{2,10},{3,11},{4,12},{5,13},{6,14},{7,15},{8,0},{9,1},... | collective-permute-start | bytes 98312 | tf_op jit(solution)/shard_map/ppermute | solution.py:70
  64.2 7.3 %shard_map.211 = (f32[16,64,512]{2,1,0:T(8,128)}, bf16[1040,512]{1,0:T(8,128)(2,1)S(1)}, bf16[1024,512]{1,0:T(8,128)(2,1)S(1)}, bf16[1024,1024]{1,0:T(8,128)(2,1...) custom-call(f32[16,512]{1,0:T(8,128)S(1)} %get-tuple-element.106.refs_0_, ...), custom_call_target="tpu_custom_call" | custom-call | flops 8589934592 | tf_op jit(solution)/shard_map/pallas_call | solution.py:40
  71.5 1.9 shard_map.212
  74.0 1.8 collective-permute-start.17
  81.8 2.0 %collective-permute-start.20 = (f32[16,512]{1,0:T(8,128)S(1)}, f32[16,512]{1,0:T(8,128)S(1)}, u32[]{:S(2)}, u32[]{:S(2)}) collective-permute-start(f32[16,512]{1,0:T(8,128)S(1)} %shard_map.214.refs_2_.refs_6_), channel_id=1, source_target_pairs={{0,24},{1,25},{2,26},{3,27},{4,28},{5,29},{6,30},{7,31},{8,16},{9,... | collective-permute-start | bytes 98312 | tf_op jit(solution)/shard_map/ppermute | solution.py:70
  90.2 1.9 shard_map.217
  94.1 11.2 %all_to_all.17.refs_4_.refs_1_ = f32[32,8,128]{2,1,0:T(8,128)S(1)} all-to-all(f32[32,8,128]{2,1,0:T(8,128)S(1)} %shard_map.219), channel_id=1, replica_groups=mesh['tm'=32] {'tm'}, dimensions={0} | all-to-all | bytes 262144 | tf_op jit(solution)/shard_map/all_to_all | solution.py:105
  106.1 2.4 %shard_map.221 = (f32[1024,512]{1,0:T(8,128)S(1)}, bf16[1024,1024]{1,0:T(8,128)(2,1)S(1)}, bf16[1024,512]{1,0:T(8,128)(2,1)S(1)}, f32[1024,512]{1,0:T(8,128)S(1)...) custom-call(s32[16,128]{1,0:T(8,128)S(1)} %get-tuple-element.93.refs_0_.refs_13_.refs_1_, ...), custom_call_target="tpu_custom_call" | custom-call | flops 8589934592 | tf_op jit(solution)/shard_map/pallas_call | solution.py:40
  110.7 1.8 collective-permute-start.27
  133.3 3.2 %collective-permute-done.37.refs_1_ = f32[48,512]{1,0:T(8,128)S(1)} collective-permute-done((f32[48,512]{1,0:T(8,128)S(1)}, f32[48,512]{1,0:T(8,128)S(1)}, u32[]{:S(2)}, u32[]{:S(2)}) %collective-permute-start.37) | collective-permute-done | bytes 98336 | tf_op jit(solution)/shard_map/ppermute | solution.py:207
  137.8 2.7 %collective-permute-done.40.refs_2_ = f32[256,512]{1,0:T(8,128)S(1)} collective-permute-done((f32[256,512]{1,0:T(8,128)S(1)}, f32[256,512]{1,0:T(8,128)S(1)}, u32[]{:S(2)}, u32[]{:S(2)}) %collective-permute-start.40) | collective-permute-done | bytes 524320 | tf_op jit(solution)/shard_map/ppermute | solution.py:207
  141.6 2.5 %collective-permute-start.41 = (f32[64,512]{1,0:T(8,128)S(1)}, f32[64,512]{1,0:T(8,128)S(1)}, u32[]{:S(2)}, u32[]{:S(2)}) collective-permute-start(f32[64,512]{1,0:T(8,128)S(1)} %shard_map.238.refs_4_), channel_id=1, source_target_pairs={{0,8},{1,9},{2,10},{3,11},{4,12},{5,13},{6,14},{7,15},{8,0},{9,1},... | collective-permute-start | bytes 393224 | tf_op jit(solution)/shard_map/ppermute | solution.py:207
  144.0 3.2 %collective-permute-done.43.refs_3_ = f32[128,512]{1,0:T(8,128)S(1)} collective-permute-done((f32[128,512]{1,0:T(8,128)S(1)}, f32[128,512]{1,0:T(8,128)S(1)}, u32[]{:S(2)}, u32[]{:S(2)}) %collective-permute-start.43) | collective-permute-done | bytes 262176 | tf_op jit(solution)/shard_map/ppermute | solution.py:207
  147.3 2.5 %collective-permute-start.46 = (f32[64,512]{1,0:T(8,128)S(1)}, f32[64,512]{1,0:T(8,128)S(1)}, u32[]{:S(2)}, u32[]{:S(2)}) collective-permute-start(f32[64,512]{1,0:T(8,128)S(1)} %shard_map.239.refs_2_), channel_id=1, source_target_pairs={{0,8},{1,9},{2,10},{3,11},{4,12},{5,13},{6,14},{7,15},{8,0},{9,1},... | collective-permute-start | bytes 393224 | tf_op jit(solution)/shard_map/ppermute | solution.py:207
  153.2 2.7 %collective-permute-start.50 = (f32[32,512]{1,0:T(8,128)S(1)}, f32[32,512]{1,0:T(8,128)S(1)}, u32[]{:S(2)}, u32[]{:S(2)}) collective-permute-start(f32[32,512]{1,0:T(8,128)S(1)} %shard_map.243.refs_6_), channel_id=1, source_target_pairs={{0,16},{1,17},{2,18},{3,19},{4,20},{5,21},{6,22},{7,23},{8,24},{9,... | collective-permute-start | bytes 196616 | tf_op jit(solution)/shard_map/ppermute | solution.py:207
  155.9 2.1 %collective-permute-done.45.refs_5_ = f32[32,512]{1,0:T(8,128)S(1)} collective-permute-done((f32[32,512]{1,0:T(8,128)S(1)}, f32[32,512]{1,0:T(8,128)S(1)}, u32[]{:S(2)}, u32[]{:S(2)}) %collective-permute-start.45) | collective-permute-done | bytes 65568 | tf_op jit(solution)/shard_map/ppermute | solution.py:207
  163.0 1.7 collective-permute-done.48.refs_1_
  165.6 1.8 collective-permute-start.51
  168.5 2.9 %collective-permute-done.52.refs_1_ = f32[64,512]{1,0:T(8,128)S(1)} collective-permute-done((f32[64,512]{1,0:T(8,128)S(1)}, f32[64,512]{1,0:T(8,128)S(1)}, u32[]{:S(2)}, u32[]{:S(2)}) %collective-permute-start.52) | collective-permute-done | bytes 131104 | tf_op jit(solution)/shard_map/ppermute | solution.py:207
  173.9 2.9 %collective-permute-done.54.refs_1_ = f32[16,512]{1,0:T(8,128)S(1)} collective-permute-done((f32[16,512]{1,0:T(8,128)S(1)}, f32[16,512]{1,0:T(8,128)S(1)}, u32[]{:S(2)}, u32[]{:S(2)}) %collective-permute-start.54) | collective-permute-done | bytes 32800 | tf_op jit(solution)/shard_map/ppermute | solution.py:207
  178.9 2.2 %collective-permute-done.56.refs_1_ = f32[32,512]{1,0:T(8,128)S(1)} collective-permute-done((f32[32,512]{1,0:T(8,128)S(1)}, f32[32,512]{1,0:T(8,128)S(1)}, u32[]{:S(2)}, u32[]{:S(2)}) %collective-permute-start.56) | collective-permute-done | bytes 65568 | tf_op jit(solution)/shard_map/ppermute | solution.py:207
  181.1 1.7 collective-permute-start.58
  184.6 3.0 %collective-permute-done.58.refs_1_ = f32[64,512]{1,0:T(8,128)S(1)} collective-permute-done((f32[64,512]{1,0:T(8,128)S(1)}, f32[64,512]{1,0:T(8,128)S(1)}, u32[]{:S(2)}, u32[]{:S(2)}) %collective-permute-start.58) | collective-permute-done | bytes 131104 | tf_op jit(solution)/shard_map/ppermute | solution.py:207
  187.6 2.0 %collective-permute-start.65 = (f32[128,512]{1,0:T(8,128)S(1)}, f32[128,512]{1,0:T(8,128)S(1)}, u32[]{:S(2)}, u32[]{:S(2)}) collective-permute-start(f32[128,512]{1,0:T(8,128)S(1)} %shard_map.259.refs_11_.refs_0_), channel_id=1, source_target_pairs={{0,2},{1,5},{2,0},{3,7},{4,6},{5,1},{6,4},{7,3},{8,10},{9,13},{10,... | collective-permute-start | bytes 786440 | tf_op jit(solution)/shard_map/ppermute | solution.py:207
  189.7 2.7 %shard_map.260 = (f32[16,64,512]{2,1,0:T(8,128)}, f32[2,512]{1,0:T(2,128)}, f32[2,512]{1,0:T(2,128)}, f32[2,256]{1,0:T(2,128)}, f32[2,256]{1,0:T(2,128)}, /*index=5*/f32[2,512]{1,0:T(2,128)}, f32[2,2,512]{2,1,0:T(2,128)}) custom-call(f32[32,512]{1,0:T(8,128)S(1)} %shard_map.252.refs_2_.refs_0_, s32[16,128]{1,0:T(8,128)S(1)} %copy-done.7, ...), custom_call_target="tpu_custom_call" | custom-call | flops 8589934592 | tf_op jit(solution)/shard_map/pallas_call | solution.py:40
  193.9 1.7 collective-permute-done.65.refs_1_
  198.1 2.3 %shard_map.265 = (f32[2,512,1024]{2,1,0:T(8,128)}, f32[2,512,512]{2,1,0:T(8,128)}, f32[2,512,512]{2,1,0:T(8,128)}) custom-call(f32[512,512]{1,0:T(8,128)S(1)} %shard_map.261.refs_2_.refs_0_, f32[512,512]{1,0:T(8,128)S(1)} %collective-permute-done.62.refs_1_, f32[512,512]{1,0:T(8,128)S(1)} %shard_map.262.refs_2_, ...), custom_call_target="tpu_custom_call", output_to_operand_aliasing={{0}: (6, {}), {1}: (7, {})} | custom-call | tf_op jit(solution)/shard_map/pallas_call | solution.py:419
  (213 shorter events, 86.8 us)
Async XLA Ops:
  73.4 7.7 %collective-permute-start.21 = (f32[768,512]{1,0:T(8,128)S(1)}, f32[768,512]{1,0:T(8,128)S(1)}, u32[]{:S(2)}, u32[]{:S(2)}) collective-permute-start(f32[768,512]{1,0:T(8,128)S(1)} %get-tuple-element.119), channel_id=1, source_target_pairs={{0,1},{1,0},{2,3},{3,2},{4,5},{5,4},{6,7},{7,6},{8,9},{9,8},{10,11... | collective-permute-start | bytes 4718600 | tf_op jit(solution)/shard_map/ppermute | solution.py:207
  81.3 12.1 %collective-permute-start.22 = (f32[384,512]{1,0:T(8,128)S(1)}, f32[384,512]{1,0:T(8,128)S(1)}, u32[]{:S(2)}, u32[]{:S(2)}) collective-permute-start(f32[384,512]{1,0:T(8,128)S(1)} %shard_map.215.refs_18_), channel_id=1, source_target_pairs={{0,2},{1,5},{2,0},{3,7},{4,6},{5,1},{6,4},{7,3},{8,10},{9,13},{10,... | collective-permute-start | bytes 2359304 | tf_op jit(solution)/shard_map/ppermute | solution.py:207
  93.4 12.0 %collective-permute-start.23 = (f32[192,512]{1,0:T(8,128)S(1)}, f32[192,512]{1,0:T(8,128)S(1)}, u32[]{:S(2)}, u32[]{:S(2)}) collective-permute-start(f32[192,512]{1,0:T(8,128)S(1)} %shard_map.218.refs_1_), channel_id=1, source_target_pairs={{0,4},{1,3},{2,6},{3,1},{4,0},{5,7},{6,2},{7,5},{8,12},{9,11},{10,... | collective-permute-start | bytes 1179656 | tf_op jit(solution)/shard_map/ppermute | solution.py:207
  105.4 10.0 %collective-permute-start.28 = (f32[96,512]{1,0:T(8,128)S(1)}, f32[96,512]{1,0:T(8,128)S(1)}, u32[]{:S(2)}, u32[]{:S(2)}) collective-permute-start(f32[96,512]{1,0:T(8,128)S(1)} %shard_map.220.refs_13_), channel_id=1, source_target_pairs={{0,8},{1,9},{2,10},{3,11},{4,12},{5,13},{6,14},{7,15},{8,0},{9,1},... | collective-permute-start | bytes 589832 | tf_op jit(solution)/shard_map/ppermute | solution.py:207
  110.5 6.0 %collective-permute-start.32 = (f32[512,512]{1,0:T(8,128)S(1)}, f32[512,512]{1,0:T(8,128)S(1)}, u32[]{:S(2)}, u32[]{:S(2)}) collective-permute-start(f32[512,512]{1,0:T(8,128)S(1)} %get-tuple-element.139), channel_id=1, source_target_pairs={{0,1},{1,0},{2,3},{3,2},{4,5},{5,4},{6,7},{7,6},{8,9},{9,8},{10,11... | collective-permute-start | bytes 3145736 | tf_op jit(solution)/shard_map/ppermute | solution.py:207
  116.6 11.6 %collective-permute-start.35 = (f32[256,512]{1,0:T(8,128)S(1)}, f32[256,512]{1,0:T(8,128)S(1)}, u32[]{:S(2)}, u32[]{:S(2)}) collective-permute-start(f32[256,512]{1,0:T(8,128)S(1)} %shard_map.227.refs_18_), channel_id=1, source_target_pairs={{0,2},{1,5},{2,0},{3,7},{4,6},{5,1},{6,4},{7,3},{8,10},{9,13},{10,... | collective-permute-start | bytes 1572872 | tf_op jit(solution)/shard_map/ppermute | solution.py:207
  117.8 10.4 %collective-permute-start.34 = (f32[512,512]{1,0:T(8,128)S(1)}, f32[512,512]{1,0:T(8,128)S(1)}, u32[]{:S(2)}, u32[]{:S(2)}) collective-permute-start(f32[512,512]{1,0:T(8,128)S(1)} %get-tuple-element.148), channel_id=1, source_target_pairs={{0,1},{1,0},{2,3},{3,2},{4,5},{5,4},{6,7},{7,6},{8,9},{9,8},{10,11... | collective-permute-start | bytes 3145736 | tf_op jit(solution)/shard_map/ppermute | solution.py:207
  117.8 6.1 %collective-permute-start.31 = (f32[16,512]{1,0:T(8,128)S(1)}, f32[16,512]{1,0:T(8,128)S(1)}, u32[]{:S(2)}, u32[]{:S(2)}) collective-permute-start(f32[16,512]{1,0:T(8,128)S(1)} %shard_map.226.refs_2_.refs_6_), channel_id=1, source_target_pairs={{0,24},{1,25},{2,26},{3,27},{4,28},{5,29},{6,30},{7,31},{8,16},{9,... | collective-permute-start | bytes 98312 | tf_op jit(solution)/shard_map/ppermute | solution.py:70
  123.8 6.0 %collective-permute-start.33 = (f32[48,512]{1,0:T(8,128)S(1)}, f32[48,512]{1,0:T(8,128)S(1)}, u32[]{:S(2)}, u32[]{:S(2)}) collective-permute-start(f32[48,512]{1,0:T(8,128)S(1)} %shard_map.224.refs_5_), channel_id=1, source_target_pairs={{0,16},{1,17},{2,18},{3,19},{4,20},{5,21},{6,22},{7,23},{8,24},{9,... | collective-permute-start | bytes 294920 | tf_op jit(solution)/shard_map/ppermute | solution.py:207
  129.9 6.6 %collective-permute-start.37 = (f32[48,512]{1,0:T(8,128)S(1)}, f32[48,512]{1,0:T(8,128)S(1)}, u32[]{:S(2)}, u32[]{:S(2)}) collective-permute-start(f32[48,512]{1,0:T(8,128)S(1)} %shard_map.233.refs_3_.refs_0_), channel_id=1, source_target_pairs={{0,16},{1,17},{2,18},{3,19},{4,20},{5,21},{6,22},{7,23},{8,24},{9,... | collective-permute-start | bytes 294920 | tf_op jit(solution)/shard_map/ppermute | solution.py:207
  130.1 11.4 %collective-permute-start.39 = (f32[128,512]{1,0:T(8,128)S(1)}, f32[128,512]{1,0:T(8,128)S(1)}, u32[]{:S(2)}, u32[]{:S(2)}) collective-permute-start(f32[128,512]{1,0:T(8,128)S(1)} %shard_map.231.refs_2_), channel_id=1, source_target_pairs={{0,4},{1,3},{2,6},{3,1},{4,0},{5,7},{6,2},{7,5},{8,12},{9,11},{10,... | collective-permute-start | bytes 786440 | tf_op jit(solution)/shard_map/ppermute | solution.py:207
  130.8 9.7 %collective-permute-start.40 = (f32[256,512]{1,0:T(8,128)S(1)}, f32[256,512]{1,0:T(8,128)S(1)}, u32[]{:S(2)}, u32[]{:S(2)}) collective-permute-start(f32[256,512]{1,0:T(8,128)S(1)} %shard_map.232.refs_6_), channel_id=1, source_target_pairs={{0,2},{1,5},{2,0},{3,7},{4,6},{5,1},{6,4},{7,3},{8,10},{9,13},{10,... | collective-permute-start | bytes 1572872 | tf_op jit(solution)/shard_map/ppermute | solution.py:207
  136.5 13.2 %collective-permute-start.42 = (f32[96,512]{1,0:T(8,128)S(1)}, f32[96,512]{1,0:T(8,128)S(1)}, u32[]{:S(2)}, u32[]{:S(2)}) collective-permute-start(f32[96,512]{1,0:T(8,128)S(1)} %shard_map.235.refs_3_.refs_0_), channel_id=1, source_target_pairs={{0,8},{1,9},{2,10},{3,11},{4,12},{5,13},{6,14},{7,15},{8,0},{9,1},... | collective-permute-start | bytes 589832 | tf_op jit(solution)/shard_map/ppermute | solution.py:207
  136.7 15.0 %collective-permute-start.38 = (f32[144,512]{1,0:T(8,128)S(1)}, f32[144,512]{1,0:T(8,128)S(1)}, u32[]{:S(2)}, u32[]{:S(2)}) collective-permute-start(f32[144,512]{1,0:T(8,128)S(1)} %shard_map.236.refs_3_), channel_id=1, source_target_pairs={{0,2},{1,5},{2,0},{3,7},{4,6},{5,1},{6,4},{7,3},{8,10},{9,13},{10,... | collective-permute-start | bytes 884744 | tf_op jit(solution)/shard_map/ppermute | solution.py:207
  140.6 6.6 %collective-permute-start.43 = (f32[128,512]{1,0:T(8,128)S(1)}, f32[128,512]{1,0:T(8,128)S(1)}, u32[]{:S(2)}, u32[]{:S(2)}) collective-permute-start(f32[128,512]{1,0:T(8,128)S(1)} %shard_map.237.refs_4_), channel_id=1, source_target_pairs={{0,4},{1,3},{2,6},{3,1},{4,0},{5,7},{6,2},{7,5},{8,12},{9,11},{10,... | collective-permute-start | bytes 786440 | tf_op jit(solution)/shard_map/ppermute | solution.py:207
  141.6 9.7 %collective-permute-start.41 = (f32[64,512]{1,0:T(8,128)S(1)}, f32[64,512]{1,0:T(8,128)S(1)}, u32[]{:S(2)}, u32[]{:S(2)}) collective-permute-start(f32[64,512]{1,0:T(8,128)S(1)} %shard_map.238.refs_4_), channel_id=1, source_target_pairs={{0,8},{1,9},{2,10},{3,11},{4,12},{5,13},{6,14},{7,15},{8,0},{9,1},... | collective-permute-start | bytes 393224 | tf_op jit(solution)/shard_map/ppermute | solution.py:207
  149.8 12.0 %collective-permute-start.49 = (f32[192,512]{1,0:T(8,128)S(1)}, f32[192,512]{1,0:T(8,128)S(1)}, u32[]{:S(2)}, u32[]{:S(2)}) collective-permute-start(f32[192,512]{1,0:T(8,128)S(1)} %shard_map.240.refs_5_.refs_0_), channel_id=1, source_target_pairs={{0,4},{1,3},{2,6},{3,1},{4,0},{5,7},{6,2},{7,5},{8,12},{9,11},{10,... | collective-permute-start | bytes 1179656 | tf_op jit(solution)/shard_map/ppermute | solution.py:207
  151.3 6.8 %collective-permute-start.45 = (f32[32,512]{1,0:T(8,128)S(1)}, f32[32,512]{1,0:T(8,128)S(1)}, u32[]{:S(2)}, u32[]{:S(2)}) collective-permute-start(f32[32,512]{1,0:T(8,128)S(1)} %shard_map.241.refs_4_), channel_id=1, source_target_pairs={{0,16},{1,17},{2,18},{3,19},{4,20},{5,21},{6,22},{7,23},{8,24},{9,... | collective-permute-start | bytes 196616 | tf_op jit(solution)/shard_map/ppermute | solution.py:207
  151.7 7.7 %collective-permute-start.44 = (f32[80,512]{1,0:T(8,128)S(1)}, f32[80,512]{1,0:T(8,128)S(1)}, u32[]{:S(2)}, u32[]{:S(2)}) collective-permute-start(f32[80,512]{1,0:T(8,128)S(1)} %shard_map.242.refs_5_.refs_4_), channel_id=1, source_target_pairs={{0,4},{1,3},{2,6},{3,1},{4,0},{5,7},{6,2},{7,5},{8,12},{9,11},{10,... | collective-permute-start | bytes 491528 | tf_op jit(solution)/shard_map/ppermute | solution.py:207
  153.2 7.8 %collective-permute-start.50 = (f32[32,512]{1,0:T(8,128)S(1)}, f32[32,512]{1,0:T(8,128)S(1)}, u32[]{:S(2)}, u32[]{:S(2)}) collective-permute-start(f32[32,512]{1,0:T(8,128)S(1)} %shard_map.243.refs_6_), channel_id=1, source_target_pairs={{0,16},{1,17},{2,18},{3,19},{4,20},{5,21},{6,22},{7,23},{8,24},{9,... | collective-permute-start | bytes 196616 | tf_op jit(solution)/shard_map/ppermute | solution.py:207
  158.1 6.6 %collective-permute-start.48 = (f32[32,512]{1,0:T(8,128)S(1)}, f32[32,512]{1,0:T(8,128)S(1)}, u32[]{:S(2)}, u32[]{:S(2)}) collective-permute-start(f32[32,512]{1,0:T(8,128)S(1)} %shard_map.244.refs_5_.refs_0_), channel_id=1, source_target_pairs={{0,16},{1,17},{2,18},{3,19},{4,20},{5,21},{6,22},{7,23},{8,24},{9,... | collective-permute-start | bytes 196616 | tf_op jit(solution)/shard_map/ppermute | solution.py:207
  159.4 6.1 %collective-permute-start.47 = (f32[48,512]{1,0:T(8,128)S(1)}, f32[48,512]{1,0:T(8,128)S(1)}, u32[]{:S(2)}, u32[]{:S(2)}) collective-permute-start(f32[48,512]{1,0:T(8,128)S(1)} %shard_map.245.refs_6_.refs_5_), channel_id=1, source_target_pairs={{0,8},{1,9},{2,10},{3,11},{4,12},{5,13},{6,14},{7,15},{8,0},{9,1},... | collective-permute-start | bytes 294920 | tf_op jit(solution)/shard_map/ppermute | solution.py:207
  161.0 7.4 %collective-permute-start.53 = (f32[32,512]{1,0:T(8,128)S(1)}, f32[32,512]{1,0:T(8,128)S(1)}, u32[]{:S(2)}, u32[]{:S(2)}) collective-permute-start(f32[32,512]{1,0:T(8,128)S(1)} %shard_map.246.refs_2_.refs_0_), channel_id=1, source_target_pairs={{0,16},{1,17},{2,18},{3,19},{4,20},{5,21},{6,22},{7,23},{8,24},{9,... | collective-permute-start | bytes 196616 | tf_op jit(solution)/shard_map/ppermute | solution.py:207
  161.9 22.5 %collective-permute-start.59 = (f32[384,512]{1,0:T(8,128)S(1)}, f32[384,512]{1,0:T(8,128)S(1)}, u32[]{:S(2)}, u32[]{:S(2)}) collective-permute-start(f32[384,512]{1,0:T(8,128)S(1)} %shard_map.247.refs_2_.refs_0_), channel_id=1, source_target_pairs={{0,2},{1,5},{2,0},{3,7},{4,6},{5,1},{6,4},{7,3},{8,10},{9,13},{10,... | collective-permute-start | bytes 2359304 | tf_op jit(solution)/shard_map/ppermute | solution.py:207
  164.8 6.7 %collective-permute-start.52 = (f32[64,512]{1,0:T(8,128)S(1)}, f32[64,512]{1,0:T(8,128)S(1)}, u32[]{:S(2)}, u32[]{:S(2)}) collective-permute-start(f32[64,512]{1,0:T(8,128)S(1)} %shard_map.248.refs_6_.refs_0_), channel_id=1, source_target_pairs={{0,8},{1,9},{2,10},{3,11},{4,12},{5,13},{6,14},{7,15},{8,0},{9,1},... | collective-permute-start | bytes 393224 | tf_op jit(solution)/shard_map/ppermute | solution.py:207
  171.5 6.4 %collective-permute-start.57 = (f32[128,512]{1,0:T(8,128)S(1)}, f32[128,512]{1,0:T(8,128)S(1)}, u32[]{:S(2)}, u32[]{:S(2)}) collective-permute-start(f32[128,512]{1,0:T(8,128)S(1)} %shard_map.251.refs_7_.refs_0_), channel_id=1, source_target_pairs={{0,4},{1,3},{2,6},{3,1},{4,0},{5,7},{6,2},{7,5},{8,12},{9,11},{10,... | collective-permute-start | bytes 786440 | tf_op jit(solution)/shard_map/ppermute | solution.py:207
  173.9 9.0 %collective-permute-start.60 = (f32[128,512]{1,0:T(8,128)S(1)}, f32[128,512]{1,0:T(8,128)S(1)}, u32[]{:S(2)}, u32[]{:S(2)}) collective-permute-start(f32[128,512]{1,0:T(8,128)S(1)} %shard_map.253.refs_2_.refs_0_), channel_id=1, source_target_pairs={{0,4},{1,3},{2,6},{3,1},{4,0},{5,7},{6,2},{7,5},{8,12},{9,11},{10,... | collective-permute-start | bytes 786440 | tf_op jit(solution)/shard_map/ppermute | solution.py:207
  177.9 14.4 %collective-permute-start.61 = (f32[256,512]{1,0:T(8,128)S(1)}, f32[256,512]{1,0:T(8,128)S(1)}, u32[]{:S(2)}, u32[]{:S(2)}) collective-permute-start(f32[256,512]{1,0:T(8,128)S(1)} %shard_map.255.refs_2_.refs_0_), channel_id=1, source_target_pairs={{0,2},{1,5},{2,0},{3,7},{4,6},{5,1},{6,4},{7,3},{8,10},{9,13},{10,... | collective-permute-start | bytes 1572872 | tf_op jit(solution)/shard_map/ppermute | solution.py:207
  181.1 6.5 %collective-permute-start.58 = (f32[64,512]{1,0:T(8,128)S(1)}, f32[64,512]{1,0:T(8,128)S(1)}, u32[]{:S(2)}, u32[]{:S(2)}) collective-permute-start(f32[64,512]{1,0:T(8,128)S(1)} %shard_map.256.refs_2_.refs_0_), channel_id=1, source_target_pairs={{0,4},{1,3},{2,6},{3,1},{4,0},{5,7},{6,2},{7,5},{8,12},{9,11},{10,... | collective-permute-start | bytes 393224 | tf_op jit(solution)/shard_map/ppermute | solution.py:207
  182.9 10.4 %collective-permute-start.63 = (f32[256,512]{1,0:T(8,128)S(1)}, f32[256,512]{1,0:T(8,128)S(1)}, u32[]{:S(2)}, u32[]{:S(2)}) collective-permute-start(f32[256,512]{1,0:T(8,128)S(1)} %shard_map.257.refs_2_.refs_0_), channel_id=1, source_target_pairs={{0,2},{1,5},{2,0},{3,7},{4,6},{5,1},{6,4},{7,3},{8,10},{9,13},{10,... | collective-permute-start | bytes 1572872 | tf_op jit(solution)/shard_map/ppermute | solution.py:207
  184.6 11.5 %collective-permute-start.67 = (f32[768,512]{1,0:T(8,128)S(1)}, f32[768,512]{1,0:T(8,128)S(1)}, u32[]{:S(2)}, u32[]{:S(2)}) collective-permute-start(f32[768,512]{1,0:T(8,128)S(1)} %shard_map.258.refs_2_.refs_0_), channel_id=1, source_target_pairs={{0,1},{1,0},{2,3},{3,2},{4,5},{5,4},{6,7},{7,6},{8,9},{9,8},{10,11... | collective-permute-start | bytes 4718600 | tf_op jit(solution)/shard_map/ppermute | solution.py:207
  187.6 8.0 %collective-permute-start.65 = (f32[128,512]{1,0:T(8,128)S(1)}, f32[128,512]{1,0:T(8,128)S(1)}, u32[]{:S(2)}, u32[]{:S(2)}) collective-permute-start(f32[128,512]{1,0:T(8,128)S(1)} %shard_map.259.refs_11_.refs_0_), channel_id=1, source_target_pairs={{0,2},{1,5},{2,0},{3,7},{4,6},{5,1},{6,4},{7,3},{8,10},{9,13},{10,... | collective-permute-start | bytes 786440 | tf_op jit(solution)/shard_map/ppermute | solution.py:207
  (57 other events, 616.4 us)

commit v5 on v4

--- a/solution.py
+++ b/solution.py
@@ -427,11 +427,16 @@
     )(*operands, *into)
 
 
-def steps(span, backward, body, start, unroll=8):
+def steps(span, backward, body, start, unroll=None):
     def one(k, carry):
         return body(span - 1 - k if backward else k, carry)
 
-    return lax.fori_loop(0, span, one, start, unroll=unroll)
+    return lax.fori_loop(0, span, one, start, unroll=unroll or span)
+
+
+def pieces(rows, step, backward=False):
+    starts = range(0, rows, step)
+    return reversed(starts) if backward else starts
 
 
 def at(t, seqs):
@@ -454,7 +459,7 @@
     return steps(span, backward, body, start)
 
 
-def adjoint_scan(g_ref, rel, lr, li, start, span, backward, use=None, extra=()):
+def adjoint_scan(g_ref, rel, lr, li, start, span, backward, use=None, extra=(), unroll=None):
     seqs, states = lr.shape
 
     def body(t, carry):
@@ -466,7 +471,7 @@
         next_re, next_im = mul(lr, -li, ar, ai)
         return (jnp.where(live, next_re, ar), jnp.where(live, next_im, ai)), kept
 
-    return steps(span, backward, body, (start, extra))
+    return steps(span, backward, body, (start, extra), unroll)
 
 
 def wide(ref, row, shape):
@@ -499,10 +504,9 @@
 PIECE = 8
 
 
-def prepare_body(plan, span, lengths_any, x_any, nu_any, phase_any, *outs):
+def prepare_body(span, lengths_any, x_any, nu_any, phase_any, *outs):
     lens_ref, sums_ref, tm_ref, mask_ref, decay_ref = outs[:5]
-    factor_refs = outs[5 : 5 + len(plan)]
-    lengths_ref, x_ref, nu_ref, phase_ref, sems = outs[5 + len(plan) :]
+    lengths_ref, x_ref, nu_ref, phase_ref, sems = outs[5:]
     seqs, _, width = x_ref.shape
     states = nu_ref.shape[-1]
     copies = [
@@ -535,6 +539,27 @@
     for row, value in enumerate((radius * cosine, radius * sine, gamma, rate, radius, cosine, sine)):
         for k in range(2):
             decay_ref[k, row : row + 1, :] = value[k : k + 1, :]
+    first = jnp.zeros((seqs, width), F32)
+    second = jnp.zeros((seqs, width), F32)
+    for t0 in range(0, span, PIECE):
+        copies[t0 // PIECE].wait()
+        piece = jnp.swapaxes(x_ref[:, t0 : t0 + PIECE, :], 0, 1)
+        for j in range(PIECE):
+            rows = piece[j]
+            mask = jnp.where(rel > t0 + j, 1.0, 0.0)
+            place = slice((t0 + j) * seqs, (t0 + j + 1) * seqs)
+            mask_ref[place, :] = mask
+            tm_ref[place, :] = rows
+            live = rows * lane_tiled(mask, width)
+            first += live
+            second += live * rows
+    spread(sums_ref, jnp.sum(first, 0, keepdims=True), jnp.sum(second, 0, keepdims=True))
+
+
+def factors_body(plan, span, lens_ref, decay_ref, *factor_refs):
+    seqs, states = lens_ref.shape[0], decay_ref.shape[-1]
+    here = lax.axis_index("tm")
+    lens = lens_ref[...]
     for k in range(2):
         for level, (radix, stride) in enumerate(plan):
             base = lax.div(here, radix * stride) * (radix * stride)
@@ -552,21 +577,6 @@
                     power = mul(*power, *power)
                 factor_refs[level][k, member, :, :states] = re
                 factor_refs[level][k, member, :, states:] = im
-    first = jnp.zeros((seqs, width), F32)
-    second = jnp.zeros((seqs, width), F32)
-    for t0 in range(0, span, PIECE):
-        copies[t0 // PIECE].wait()
-        piece = jnp.swapaxes(x_ref[:, t0 : t0 + PIECE, :], 0, 1)
-        for j in range(PIECE):
-            rows = piece[j]
-            mask = jnp.where(rel > t0 + j, 1.0, 0.0)
-            place = slice((t0 + j) * seqs, (t0 + j + 1) * seqs)
-            mask_ref[place, :] = mask
-            tm_ref[place, :] = rows
-            live = rows * lane_tiled(mask, width)
-            first += live
-            second += live * rows
-    spread(sums_ref, jnp.sum(first, 0, keepdims=True), jnp.sum(second, 0, keepdims=True))
 
 
 def one_less_exp(x):
@@ -602,8 +612,8 @@
     stats_ref[3:4, :] = rstd * gain_ref[k : k + 1, :]
     slope = rstd * gain_ref[k : k + 1, :]
     bias = bias_ref[k : k + 1, :]
-    step = CHUNK * seqs
-    for r in range(0, span * seqs, step):
+    step = 16 * seqs
+    for r in pieces(span * seqs, step, backward):
         u = ((x_ref[r : r + step, :] - mean) * slope + bias).astype(BF16)
         u_ref[r : r + step, :] = u
         v_ref[r : r + step, :] = dot(u, w_ref[k])
@@ -643,10 +653,10 @@
     rebuild_states(k, plan, span, False, exch, buffers, rel, v_ref, decay_ref, h_ref)
     mean, scale = stats_ref[0:1, :], stats_ref[3:4, :]
     bias, skip = bias_ref[k : k + 1, :], skip_ref[k : k + 1, :]
-    step = CHUNK * seqs
+    step = 64 * seqs
     first = jnp.zeros((8, width), F32)
     second = jnp.zeros((8, width), F32)
-    for r in range(0, span * seqs, step):
+    for r in pieces(span * seqs, step, False):
         x = x_ref[r : r + step, :]
         u = (x - mean) * scale + bias
         y = dot(h_ref[r + seqs : r + seqs + step, :], w_out_ref[k]) + skip * u
@@ -678,11 +688,11 @@
     g_ref[r : r + step, :] = dot_nt(dy, w_out_ref[k])
 
 
-def local_adjoint(k, span, backward, rel, g_ref, decay_ref, summary_ref):
+def local_adjoint(k, span, backward, rel, g_ref, decay_ref, summary_ref, unroll=None):
     seqs, states = rel.shape
     lr, li = wide(decay_ref.at[k], 0, rel.shape), wide(decay_ref.at[k], 1, rel.shape)
     zero = jnp.zeros(rel.shape, F32)
-    (re, im), _ = adjoint_scan(g_ref, rel, lr, li, (zero, zero), span, backward)
+    (re, im), _ = adjoint_scan(g_ref, rel, lr, li, (zero, zero), span, backward, unroll=unroll)
     summary_ref[:, :states] = re
     summary_ref[:, states:] = im
 
@@ -699,8 +709,8 @@
     rebuild_states(k, plan, span, True, exch, buffers, rel, v_ref, decay_ref, h_ref)
     mean, scale = stats_ref[0:1, :], stats_ref[3:4, :]
     bias, skip = bias_ref[k : k + 1, :], skip_ref[k : k + 1, :]
-    step = CHUNK * seqs
-    for r in range(0, span * seqs, step):
+    step = 64 * seqs
+    for r in pieces(span * seqs, step, True):
         t0 = r // seqs
         x = x_ref[r : r + step, :]
         u = (x - mean) * scale + bias
@@ -711,8 +721,8 @@
         z = dot(act, w_glu_ref[k])
         value, gate = z[:, :width], sigmoid(z[:, width:])
         gated = value * gate
-        out_ref[:, t0 : t0 + CHUNK, :] = from_time_major(x + gated, seqs)
-        d = to_time_major(cot_ref[:, t0 : t0 + CHUNK, :])
+        out_ref[:, t0 : t0 + 64, :] = from_time_major(x + gated, seqs)
+        d = to_time_major(cot_ref[:, t0 : t0 + 64, :])
         back_rows(
             k, r, step, d * gate, d * (gated * (1.0 - gate)), slope, width,
             w_glu_ref, w_out_ref, dz_ref, dy_ref, g_ref,
@@ -736,8 +746,8 @@
         k + 1, token_scale(lens_ref), bias_grad, gain_grad, stats_ref, gain_ref
     )
     mean = stats_ref[0:1, :]
-    step = CHUNK * seqs
-    for r in range(0, span * seqs, step):
+    step = 64 * seqs
+    for r in pieces(span * seqs, step, backward):
         live = lane_tiled(mask_ref[r : r + step, :], width)
         d = part_ref[r : r + step, :] + live * (shift + tilt * (x_ref[r : r + step, :] - mean))
         d_ref[r : r + step, :] = d
@@ -746,7 +756,7 @@
             d * value_ref[r : r + step, :].astype(F32), slope_ref[r : r + step, :].astype(F32), width,
             w_glu_ref, w_out_ref, dz_ref, dy_ref, g_ref,
         )
-    local_adjoint(k, span, backward, rel, g_ref, decay_ref, summary_ref)
+    local_adjoint(k, span, backward, rel, g_ref, decay_ref, summary_ref, 8)
 
 
 def input_terms(k, scale, bias_grad, gain_grad, stats_ref, gain_ref):
@@ -891,9 +901,8 @@
 
     in_hbm = pl.BlockSpec(memory_space=pltpu.HBM)
     outs = [((seqs, LANES), jnp.int32), tile, whole, ((rows, LANES), F32), ((2, 8, states), F32)]
-    outs += [((2, radix) + summary[0], F32) for radix, _ in plan]
     prepared = pl.pallas_call(
-        functools.partial(prepare_body, plan, span),
+        functools.partial(prepare_body, span),
         out_shape=[jax.ShapeDtypeStruct(shape, dtype) for shape, dtype in outs],
         in_specs=[in_hbm] * 4,
         out_specs=[pl.BlockSpec(memory_space=pltpu.VMEM)] * len(outs),
@@ -907,7 +916,6 @@
         compiler_params=pltpu.CompilerParams(vmem_limit_bytes=24 * MIB),
     )(*(pltpu.with_memory_space_constraint(a, pltpu.HBM) for a in (lengths, inputs, nu_log, phase)))
     lens, sums, x0, mask, decay = prepared[:5]
-    factors = prepared[5:]
 
     def project(k, sums, x):
         return run(
@@ -921,6 +929,12 @@
         return run(with_entry(body, plan), outs, operands, after, buffers, limit, weight)
 
     u0, v0, stats0, part = project(0, sums, x0)
+    factors = run(
+        functools.partial(factors_body, plan, span),
+        [((2, radix) + summary[0], F32) for radix, _ in plan],
+        [lens, decay],
+        [part],
+    )
     held = exchange(0, part, plan, factors, False, False)
     x1, h0, act0, slope0, gate0, value0, sums = entered(
         functools.partial(forward_body, 0, plan, span),
@@ -998,12 +1012,13 @@
     held = exchange(0, part, plan, factors, True, True, beside_middle)
     middle = flows["middle"]
     other = flows["other"]
+    sent = other.send([held[-1][1]])
     dv0, small0 = entered(
         functools.partial(adjoint_body, 0, plan, span, True),
         [pair_low, eight],
         held,
         [lens, g0, h0, v0, decay],
-        [flows["step"]],
+        [flows["step"], sent],
         weight=1 << 20,
     )
     part0, skip0, sums = run(
@@ -1015,15 +1030,14 @@
 
     (small,) = run(small_body, [((16, width), F32)], [small0, skip0, sums, small1, skip1], limit=4)
     step = middle.send([part0])
-    step = other.send([step])
     step = top.settle([step])
     top.fetch()
     last = Bulk(count, [u0], [dv0], [(0, 0, 0, 0)], [step], [small], weight=1 << 20)
     last.send()
     step = last.parts[-1]
     step = top.fetch([step])
+    step = other.send([step])
     step = last.send([step])
-    step = other.send([step])
     step = middle.send([step])
     step = other.send([step])
     step = top.fetch([step])
@@ -1049,6 +1063,7 @@
     step = other.fetch([step])
     step = top.fetch([step])
     step = last.fetch([step])
+    step = middle.fetch([step])
     grad_x, g_gain, g_bias, g_nu, g_phase, g_skip, running_out = run(
         functools.partial(finish_body, span),
         [seq_major] + [((2, width), F32)] * 2 + [((2, states), F32)] * 2
@@ -1056,8 +1071,7 @@
         [last.total, lens, part0, x0, mask, bn_gain, decay, running, stats0, stats1, grads1],
         [step],
     )
-    step = middle.fetch([g_gain])
-    step = other.fetch([step])
+    step = other.fetch([g_gain])
     step = last.fetch([step])
     g_glu, g_out = unpack(
         count,

time: 201 us -> 197 us (0.980)
  starting transfers between devices: 65.8 us -> 63.3 us
    ppermute x40, starting transfers between devices: 33.3 us -> 30.7 us  [with_partner(): lax.ppermute(value, 'tm', [(i, i ^ (odd if i & 1 else even)) for i in ran...]
    pallas_call x60 -> x61, Pallas kernels: 31.5 us -> 30.2 us  [run(): pl.pallas_call(kernel, out_shape=[jax.ShapeDtypeStruct(shape, dtype) for...]
  transfers between devices with their start and end apart: 68 -> 68, of which waited for: 43 -> 46; matrix products, arithmetic and copies ran while one was open for 0% -> 0% of each run, Pallas kernels for 10% -> 10%
where the time goes in v5:
time: 197 us
  starting transfers between devices  63.3 us (32%)
  waiting for transfers between devices  56.2 us (29%)
  blocking collectives  38.1 us (19%)
  Pallas kernels  36.1 us (18%)
    all_to_all x3, blocking collectives, everywhere(): return lax.all_to_all(tiles, 'tm', 0, 0)  38.1 us
    ppermute x40, waiting for transfers between devices, with_partner(): lax.ppermute(value, 'tm', [(i, i ^ (odd if i & 1 else even)) for i in ran...  36.6 us
    ppermute x28, starting transfers between devices, swap(): lax.ppermute(value, 'tm', [(i, i ^ stride * mask) for i in range(count)])  32.5 us
    ppermute x40, starting transfers between devices, with_partner(): lax.ppermute(value, 'tm', [(i, i ^ (odd if i & 1 else even)) for i in ran...  30.7 us
    pallas_call x61, Pallas kernels, run(): pl.pallas_call(kernel, out_shape=[jax.ShapeDtypeStruct(shape, dtype) for...  30.2 us
    ppermute x28, waiting for transfers between devices, swap(): lax.ppermute(value, 'tm', [(i, i ^ stride * mask) for i in range(count)])  19.6 us
  transfers between devices with their start and end apart: 68, of which 46 were waited for; matrix products, arithmetic and copies ran while one was open for 0% of the time, Pallas kernels for 10%

profile of v5, /device:TPU:0, one launch (start us, length us, event | category | flops | bytes accessed | tf_op | source)
XLA Modules:
  0.0 196.8 jit_solution(6520525210277581769)
XLA Ops:
  0.7 1.9 shard_map.203
  2.6 15.3 %all_to_all.15.refs_1_ = f32[32,8,128]{2,1,0:T(8,128)S(1)} all-to-all(f32[32,8,128]{2,1,0:T(8,128)S(1)} %get-tuple-element.94), channel_id=1, replica_groups=mesh['tm'=32] {'tm'}, dimensions={0} | all-to-all | bytes 262144 | tf_op jit(solution)/shard_map/all_to_all | solution.py:105
  28.2 2.4 %collective-permute-start.4 = (f32[16,512]{1,0:T(8,128)S(1)}, f32[16,512]{1,0:T(8,128)S(1)}, u32[]{:S(2)}, u32[]{:S(2)}) collective-permute-start(f32[16,512]{1,0:T(8,128)S(1)} %shard_map.207.refs_6_), channel_id=1, source_target_pairs={{0,8},{1,9},{2,10},{3,11},{4,12},{5,13},{6,14},{7,15},{8,0},{9,1},... | collective-permute-start | bytes 98312 | tf_op jit(solution)/shard_map/ppermute | solution.py:70
  32.9 3.3 %shard_map.208 = (f32[1024,512]{1,0:T(8,128)S(1)}, bf16[1040,512]{1,0:T(8,128)(2,1)S(1)}, bf16[1024,512]{1,0:T(8,128)(2,1)S(1)}, bf16[1024,512]{1,0:T(8,128)(2,1...) custom-call(f32[16,512]{1,0:T(8,128)S(1)} %get-tuple-element.97.refs_2_.refs_0_, ...), custom_call_target="tpu_custom_call" | custom-call | flops 8589934592 | tf_op jit(solution)/shard_map/pallas_call | solution.py:40
  36.2 11.6 %all_to_all.16.refs_1_ = f32[32,8,128]{2,1,0:T(8,128)S(1)} all-to-all(f32[32,8,128]{2,1,0:T(8,128)S(1)} %get-tuple-element.104), channel_id=1, replica_groups=mesh['tm'=32] {'tm'}, dimensions={0} | all-to-all | bytes 262144 | tf_op jit(solution)/shard_map/all_to_all | solution.py:105
  58.0 2.5 %collective-permute-start.11 = (f32[16,512]{1,0:T(8,128)S(1)}, f32[16,512]{1,0:T(8,128)S(1)}, u32[]{:S(2)}, u32[]{:S(2)}) collective-permute-start(f32[16,512]{1,0:T(8,128)S(1)} %shard_map.211.refs_6_), channel_id=1, source_target_pairs={{0,8},{1,9},{2,10},{3,11},{4,12},{5,13},{6,14},{7,15},{8,0},{9,1},... | collective-permute-start | bytes 98312 | tf_op jit(solution)/shard_map/ppermute | solution.py:70
  62.8 6.3 %shard_map.212 = (f32[16,64,512]{2,1,0:T(8,128)}, bf16[1040,512]{1,0:T(8,128)(2,1)S(1)}, bf16[1024,512]{1,0:T(8,128)(2,1)S(1)}, bf16[1024,1024]{1,0:T(8,128)(2,1...) custom-call(f32[16,512]{1,0:T(8,128)S(1)} %get-tuple-element.106.refs_0_, ...), custom_call_target="tpu_custom_call" | custom-call | flops 8589934592 | tf_op jit(solution)/shard_map/pallas_call | solution.py:40
  69.0 1.9 shard_map.213
  71.6 1.7 collective-permute-start.17
  79.3 2.0 %collective-permute-start.20 = (f32[16,512]{1,0:T(8,128)S(1)}, f32[16,512]{1,0:T(8,128)S(1)}, u32[]{:S(2)}, u32[]{:S(2)}) collective-permute-start(f32[16,512]{1,0:T(8,128)S(1)} %shard_map.215.refs_2_.refs_6_), channel_id=1, source_target_pairs={{0,24},{1,25},{2,26},{3,27},{4,28},{5,29},{6,30},{7,31},{8,16},{9,... | collective-permute-start | bytes 98312 | tf_op jit(solution)/shard_map/ppermute | solution.py:70
  87.6 2.0 shard_map.218
  91.6 11.2 %all_to_all.17.refs_4_.refs_1_ = f32[32,8,128]{2,1,0:T(8,128)S(1)} all-to-all(f32[32,8,128]{2,1,0:T(8,128)S(1)} %shard_map.220), channel_id=1, replica_groups=mesh['tm'=32] {'tm'}, dimensions={0} | all-to-all | bytes 262144 | tf_op jit(solution)/shard_map/all_to_all | solution.py:105
  103.6 2.4 %shard_map.222 = (f32[1024,512]{1,0:T(8,128)S(1)}, bf16[1024,1024]{1,0:T(8,128)(2,1)S(1)}, bf16[1024,512]{1,0:T(8,128)(2,1)S(1)}, f32[1024,512]{1,0:T(8,128)S(1)...) custom-call(s32[16,128]{1,0:T(8,128)S(1)} %get-tuple-element.93.refs_0_.refs_13_.refs_1_, ...), custom_call_target="tpu_custom_call" | custom-call | flops 8589934592 | tf_op jit(solution)/shard_map/pallas_call | solution.py:40
  108.2 1.8 collective-permute-start.27
  118.8 2.1 %collective-permute-done.29.refs_2_.refs_7_ = f32[16,512]{1,0:T(8,128)S(1)} collective-permute-done((f32[16,512]{1,0:T(8,128)S(1)}, f32[16,512]{1,0:T(8,128)S(1)}, u32[]{:S(2)}, u32[]{:S(2)}) %collective-permute-start.29) | collective-permute-done | bytes 32800 | tf_op jit(solution)/shard_map/ppermute | solution.py:70
  126.6 3.5 %collective-permute-done.35.refs_2_ = f32[256,512]{1,0:T(8,128)S(1)} collective-permute-done((f32[256,512]{1,0:T(8,128)S(1)}, f32[256,512]{1,0:T(8,128)S(1)}, u32[]{:S(2)}, u32[]{:S(2)}) %collective-permute-start.35) | collective-permute-done | bytes 524320 | tf_op jit(solution)/shard_map/ppermute | solution.py:207
  130.2 1.8 collective-permute-start.38
  134.1 2.7 %collective-permute-done.38.refs_1_ = f32[48,512]{1,0:T(8,128)S(1)} collective-permute-done((f32[48,512]{1,0:T(8,128)S(1)}, f32[48,512]{1,0:T(8,128)S(1)}, u32[]{:S(2)}, u32[]{:S(2)}) %collective-permute-start.38) | collective-permute-done | bytes 98336 | tf_op jit(solution)/shard_map/ppermute | solution.py:207
  137.4 2.1 %collective-permute-done.37.refs_2_ = f32[256,512]{1,0:T(8,128)S(1)} collective-permute-done((f32[256,512]{1,0:T(8,128)S(1)}, f32[256,512]{1,0:T(8,128)S(1)}, u32[]{:S(2)}, u32[]{:S(2)}) %collective-permute-start.37) | collective-permute-done | bytes 524320 | tf_op jit(solution)/shard_map/ppermute | solution.py:207
  139.5 1.7 collective-permute-start.43
  143.0 3.0 %collective-permute-done.43.refs_3_ = f32[128,512]{1,0:T(8,128)S(1)} collective-permute-done((f32[128,512]{1,0:T(8,128)S(1)}, f32[128,512]{1,0:T(8,128)S(1)}, u32[]{:S(2)}, u32[]{:S(2)}) %collective-permute-start.43) | collective-permute-done | bytes 262176 | tf_op jit(solution)/shard_map/ppermute | solution.py:207
  147.2 2.0 collective-permute-start.49
  152.5 2.6 %collective-permute-done.45.refs_5_ = f32[32,512]{1,0:T(8,128)S(1)} collective-permute-done((f32[32,512]{1,0:T(8,128)S(1)}, f32[32,512]{1,0:T(8,128)S(1)}, u32[]{:S(2)}, u32[]{:S(2)}) %collective-permute-start.45) | collective-permute-done | bytes 65568 | tf_op jit(solution)/shard_map/ppermute | solution.py:207
  161.7 1.9 collective-permute-done.47.refs_4_
  164.6 1.8 collective-permute-start.56
  170.5 1.9 collective-permute-start.61
  172.4 2.0 %collective-permute-done.55.refs_1_ = f32[16,512]{1,0:T(8,128)S(1)} collective-permute-done((f32[16,512]{1,0:T(8,128)S(1)}, f32[16,512]{1,0:T(8,128)S(1)}, u32[]{:S(2)}, u32[]{:S(2)}) %collective-permute-start.55) | collective-permute-done | bytes 32800 | tf_op jit(solution)/shard_map/ppermute | solution.py:207
  176.0 2.7 %collective-permute-done.58.refs_1_ = f32[32,512]{1,0:T(8,128)S(1)} collective-permute-done((f32[32,512]{1,0:T(8,128)S(1)}, f32[32,512]{1,0:T(8,128)S(1)}, u32[]{:S(2)}, u32[]{:S(2)}) %collective-permute-start.58) | collective-permute-done | bytes 65568 | tf_op jit(solution)/shard_map/ppermute | solution.py:207
  181.8 3.4 %collective-permute-done.59.refs_1_ = f32[64,512]{1,0:T(8,128)S(1)} collective-permute-done((f32[64,512]{1,0:T(8,128)S(1)}, f32[64,512]{1,0:T(8,128)S(1)}, u32[]{:S(2)}, u32[]{:S(2)}) %collective-permute-start.59) | collective-permute-done | bytes 131104 | tf_op jit(solution)/shard_map/ppermute | solution.py:207
  186.4 2.7 %shard_map.262 = (f32[16,64,512]{2,1,0:T(8,128)}, f32[2,512]{1,0:T(2,128)}, f32[2,512]{1,0:T(2,128)}, f32[2,256]{1,0:T(2,128)}, f32[2,256]{1,0:T(2,128)}, /*index=5*/f32[2,512]{1,0:T(2,128)}, f32[2,2,512]{2,1,0:T(2,128)}) custom-call(f32[32,512]{1,0:T(8,128)S(1)} %shard_map.253.refs_2_.refs_0_, s32[16,128]{1,0:T(8,128)S(1)} %get-tuple-element.93.refs_0_.refs_13_.refs_1_, ...), custom_call_target="tpu_custom_call" | custom-call | flops 8589934592 | tf_op jit(solution)/shard_map/pallas_call | solution.py:40
  190.4 2.0 collective-permute-done.65.refs_1_
  194.4 2.3 %shard_map.266 = (f32[2,512,1024]{2,1,0:T(8,128)}, f32[2,512,512]{2,1,0:T(8,128)}, f32[2,512,512]{2,1,0:T(8,128)}) custom-call(f32[512,512]{1,0:T(8,128)S(1)} %shard_map.261.refs_11_.refs_0_, f32[512,512]{1,0:T(8,128)S(1)} %collective-permute-done.62.refs_1_, f32[512,512]{1,0:T(8,128)S(1)} %shard_map.263.refs_2_, ...), custom_call_target="tpu_custom_call", output_to_operand_aliasing={{0}: (6, {}), {1}: (7, {})} | custom-call | tf_op jit(solution)/shard_map/pallas_call | solution.py:419
  (212 shorter events, 86.7 us)
Async XLA Ops:
  71.0 7.7 %collective-permute-start.21 = (f32[768,512]{1,0:T(8,128)S(1)}, f32[768,512]{1,0:T(8,128)S(1)}, u32[]{:S(2)}, u32[]{:S(2)}) collective-permute-start(f32[768,512]{1,0:T(8,128)S(1)} %get-tuple-element.119), channel_id=1, source_target_pairs={{0,1},{1,0},{2,3},{3,2},{4,5},{5,4},{6,7},{7,6},{8,9},{9,8},{10,11... | collective-permute-start | bytes 4718600 | tf_op jit(solution)/shard_map/ppermute | solution.py:207
  78.7 12.1 %collective-permute-start.22 = (f32[384,512]{1,0:T(8,128)S(1)}, f32[384,512]{1,0:T(8,128)S(1)}, u32[]{:S(2)}, u32[]{:S(2)}) collective-permute-start(f32[384,512]{1,0:T(8,128)S(1)} %shard_map.216.refs_18_), channel_id=1, source_target_pairs={{0,2},{1,5},{2,0},{3,7},{4,6},{5,1},{6,4},{7,3},{8,10},{9,13},{10,... | collective-permute-start | bytes 2359304 | tf_op jit(solution)/shard_map/ppermute | solution.py:207
  90.9 12.0 %collective-permute-start.23 = (f32[192,512]{1,0:T(8,128)S(1)}, f32[192,512]{1,0:T(8,128)S(1)}, u32[]{:S(2)}, u32[]{:S(2)}) collective-permute-start(f32[192,512]{1,0:T(8,128)S(1)} %shard_map.219.refs_1_), channel_id=1, source_target_pairs={{0,4},{1,3},{2,6},{3,1},{4,0},{5,7},{6,2},{7,5},{8,12},{9,11},{10,... | collective-permute-start | bytes 1179656 | tf_op jit(solution)/shard_map/ppermute | solution.py:207
  102.9 10.1 %collective-permute-start.28 = (f32[96,512]{1,0:T(8,128)S(1)}, f32[96,512]{1,0:T(8,128)S(1)}, u32[]{:S(2)}, u32[]{:S(2)}) collective-permute-start(f32[96,512]{1,0:T(8,128)S(1)} %shard_map.221.refs_13_), channel_id=1, source_target_pairs={{0,8},{1,9},{2,10},{3,11},{4,12},{5,13},{6,14},{7,15},{8,0},{9,1},... | collective-permute-start | bytes 589832 | tf_op jit(solution)/shard_map/ppermute | solution.py:207
  107.9 10.5 %collective-permute-start.32 = (f32[512,512]{1,0:T(8,128)S(1)}, f32[512,512]{1,0:T(8,128)S(1)}, u32[]{:S(2)}, u32[]{:S(2)}) collective-permute-start(f32[512,512]{1,0:T(8,128)S(1)} %get-tuple-element.139), channel_id=1, source_target_pairs={{0,1},{1,0},{2,3},{3,2},{4,5},{5,4},{6,7},{7,6},{8,9},{9,8},{10,11... | collective-permute-start | bytes 3145736 | tf_op jit(solution)/shard_map/ppermute | solution.py:207
  112.9 9.0 %collective-permute-start.33 = (f32[512,512]{1,0:T(8,128)S(1)}, f32[512,512]{1,0:T(8,128)S(1)}, u32[]{:S(2)}, u32[]{:S(2)}) collective-permute-start(f32[512,512]{1,0:T(8,128)S(1)} %get-tuple-element.141), channel_id=1, source_target_pairs={{0,1},{1,0},{2,3},{3,2},{4,5},{5,4},{6,7},{7,6},{8,9},{9,8},{10,11... | collective-permute-start | bytes 3145736 | tf_op jit(solution)/shard_map/ppermute | solution.py:207
  113.9 9.1 %collective-permute-start.31 = (f32[16,512]{1,0:T(8,128)S(1)}, f32[16,512]{1,0:T(8,128)S(1)}, u32[]{:S(2)}, u32[]{:S(2)}) collective-permute-start(f32[16,512]{1,0:T(8,128)S(1)} %shard_map.227.refs_2_.refs_6_), channel_id=1, source_target_pairs={{0,24},{1,25},{2,26},{3,27},{4,28},{5,29},{6,30},{7,31},{8,16},{9,... | collective-permute-start | bytes 98312 | tf_op jit(solution)/shard_map/ppermute | solution.py:70
  115.6 7.5 %collective-permute-start.30 = (f32[16,512]{1,0:T(8,128)S(1)}, f32[16,512]{1,0:T(8,128)S(1)}, u32[]{:S(2)}, u32[]{:S(2)}) collective-permute-start(f32[16,512]{1,0:T(8,128)S(1)} %shard_map.227.refs_2_.refs_6_), channel_id=1, source_target_pairs={{0,16},{1,17},{2,18},{3,19},{4,20},{5,21},{6,22},{7,23},{8,24},{9,... | collective-permute-start | bytes 98312 | tf_op jit(solution)/shard_map/ppermute | solution.py:70
  118.4 11.7 %collective-permute-start.34 = (f32[48,512]{1,0:T(8,128)S(1)}, f32[48,512]{1,0:T(8,128)S(1)}, u32[]{:S(2)}, u32[]{:S(2)}) collective-permute-start(f32[48,512]{1,0:T(8,128)S(1)} %shard_map.225.refs_5_), channel_id=1, source_target_pairs={{0,16},{1,17},{2,18},{3,19},{4,20},{5,21},{6,22},{7,23},{8,24},{9,... | collective-permute-start | bytes 294920 | tf_op jit(solution)/shard_map/ppermute | solution.py:207
  120.9 9.2 %collective-permute-start.35 = (f32[256,512]{1,0:T(8,128)S(1)}, f32[256,512]{1,0:T(8,128)S(1)}, u32[]{:S(2)}, u32[]{:S(2)}) collective-permute-start(f32[256,512]{1,0:T(8,128)S(1)} %shard_map.228.refs_18_), channel_id=1, source_target_pairs={{0,2},{1,5},{2,0},{3,7},{4,6},{5,1},{6,4},{7,3},{8,10},{9,13},{10,... | collective-permute-start | bytes 1572872 | tf_op jit(solution)/shard_map/ppermute | solution.py:207
  122.0 17.5 %collective-permute-start.37 = (f32[256,512]{1,0:T(8,128)S(1)}, f32[256,512]{1,0:T(8,128)S(1)}, u32[]{:S(2)}, u32[]{:S(2)}) collective-permute-start(f32[256,512]{1,0:T(8,128)S(1)} %shard_map.229.refs_19_), channel_id=1, source_target_pairs={{0,2},{1,5},{2,0},{3,7},{4,6},{5,1},{6,4},{7,3},{8,10},{9,13},{10,... | collective-permute-start | bytes 1572872 | tf_op jit(solution)/shard_map/ppermute | solution.py:207
  130.2 6.6 %collective-permute-start.38 = (f32[48,512]{1,0:T(8,128)S(1)}, f32[48,512]{1,0:T(8,128)S(1)}, u32[]{:S(2)}, u32[]{:S(2)}) collective-permute-start(f32[48,512]{1,0:T(8,128)S(1)} %shard_map.234.refs_3_.refs_0_), channel_id=1, source_target_pairs={{0,16},{1,17},{2,18},{3,19},{4,20},{5,21},{6,22},{7,23},{8,24},{9,... | collective-permute-start | bytes 294920 | tf_op jit(solution)/shard_map/ppermute | solution.py:207
  132.0 9.8 %collective-permute-start.40 = (f32[128,512]{1,0:T(8,128)S(1)}, f32[128,512]{1,0:T(8,128)S(1)}, u32[]{:S(2)}, u32[]{:S(2)}) collective-permute-start(f32[128,512]{1,0:T(8,128)S(1)} %shard_map.233.refs_6_), channel_id=1, source_target_pairs={{0,4},{1,3},{2,6},{3,1},{4,0},{5,7},{6,2},{7,5},{8,12},{9,11},{10,... | collective-permute-start | bytes 786440 | tf_op jit(solution)/shard_map/ppermute | solution.py:207
  134.1 7.2 %collective-permute-start.36 = (f32[272,512]{1,0:T(8,128)S(1)}, f32[272,512]{1,0:T(8,128)S(1)}, u32[]{:S(2)}, u32[]{:S(2)}) collective-permute-start(f32[272,512]{1,0:T(8,128)S(1)} %get-tuple-element.152.refs_2_), channel_id=1, source_target_pairs={{0,1},{1,0},{2,3},{3,2},{4,5},{5,4},{6,7},{7,6},{8,9},{9,8},{10,11... | collective-permute-start | bytes 1671176 | tf_op jit(solution)/shard_map/ppermute | solution.py:207
  136.8 10.3 %collective-permute-start.42 = (f32[96,512]{1,0:T(8,128)S(1)}, f32[96,512]{1,0:T(8,128)S(1)}, u32[]{:S(2)}, u32[]{:S(2)}) collective-permute-start(f32[96,512]{1,0:T(8,128)S(1)} %shard_map.236.refs_3_.refs_0_), channel_id=1, source_target_pairs={{0,8},{1,9},{2,10},{3,11},{4,12},{5,13},{6,14},{7,15},{8,0},{9,1},... | collective-permute-start | bytes 589832 | tf_op jit(solution)/shard_map/ppermute | solution.py:207
  139.5 6.4 %collective-permute-start.43 = (f32[128,512]{1,0:T(8,128)S(1)}, f32[128,512]{1,0:T(8,128)S(1)}, u32[]{:S(2)}, u32[]{:S(2)}) collective-permute-start(f32[128,512]{1,0:T(8,128)S(1)} %shard_map.237.refs_3_), channel_id=1, source_target_pairs={{0,4},{1,3},{2,6},{3,1},{4,0},{5,7},{6,2},{7,5},{8,12},{9,11},{10,... | collective-permute-start | bytes 786440 | tf_op jit(solution)/shard_map/ppermute | solution.py:207
  141.3 9.6 %collective-permute-start.39 = (f32[144,512]{1,0:T(8,128)S(1)}, f32[144,512]{1,0:T(8,128)S(1)}, u32[]{:S(2)}, u32[]{:S(2)}) collective-permute-start(f32[144,512]{1,0:T(8,128)S(1)} %shard_map.238.refs_4_.refs_3_), channel_id=1, source_target_pairs={{0,2},{1,5},{2,0},{3,7},{4,6},{5,1},{6,4},{7,3},{8,10},{9,13},{10,... | collective-permute-start | bytes 884744 | tf_op jit(solution)/shard_map/ppermute | solution.py:207
  141.8 7.4 %collective-permute-start.41 = (f32[64,512]{1,0:T(8,128)S(1)}, f32[64,512]{1,0:T(8,128)S(1)}, u32[]{:S(2)}, u32[]{:S(2)}) collective-permute-start(f32[64,512]{1,0:T(8,128)S(1)} %shard_map.239.refs_4_), channel_id=1, source_target_pairs={{0,8},{1,9},{2,10},{3,11},{4,12},{5,13},{6,14},{7,15},{8,0},{9,1},... | collective-permute-start | bytes 393224 | tf_op jit(solution)/shard_map/ppermute | solution.py:207
  147.2 11.4 %collective-permute-start.49 = (f32[192,512]{1,0:T(8,128)S(1)}, f32[192,512]{1,0:T(8,128)S(1)}, u32[]{:S(2)}, u32[]{:S(2)}) collective-permute-start(f32[192,512]{1,0:T(8,128)S(1)} %shard_map.241.refs_5_.refs_0_), channel_id=1, source_target_pairs={{0,4},{1,3},{2,6},{3,1},{4,0},{5,7},{6,2},{7,5},{8,12},{9,11},{10,... | collective-permute-start | bytes 1179656 | tf_op jit(solution)/shard_map/ppermute | solution.py:207
  151.6 6.4 %collective-permute-start.50 = (f32[32,512]{1,0:T(8,128)S(1)}, f32[32,512]{1,0:T(8,128)S(1)}, u32[]{:S(2)}, u32[]{:S(2)}) collective-permute-start(f32[32,512]{1,0:T(8,128)S(1)} %shard_map.244.refs_6_), channel_id=1, source_target_pairs={{0,16},{1,17},{2,18},{3,19},{4,20},{5,21},{6,22},{7,23},{8,24},{9,... | collective-permute-start | bytes 196616 | tf_op jit(solution)/shard_map/ppermute | solution.py:207
  155.2 6.4 %collective-permute-start.48 = (f32[32,512]{1,0:T(8,128)S(1)}, f32[32,512]{1,0:T(8,128)S(1)}, u32[]{:S(2)}, u32[]{:S(2)}) collective-permute-start(f32[32,512]{1,0:T(8,128)S(1)} %shard_map.245.refs_5_.refs_0_), channel_id=1, source_target_pairs={{0,16},{1,17},{2,18},{3,19},{4,20},{5,21},{6,22},{7,23},{8,24},{9,... | collective-permute-start | bytes 196616 | tf_op jit(solution)/shard_map/ppermute | solution.py:207
  156.8 6.7 %collective-permute-start.47 = (f32[48,512]{1,0:T(8,128)S(1)}, f32[48,512]{1,0:T(8,128)S(1)}, u32[]{:S(2)}, u32[]{:S(2)}) collective-permute-start(f32[48,512]{1,0:T(8,128)S(1)} %shard_map.246.refs_6_.refs_5_), channel_id=1, source_target_pairs={{0,8},{1,9},{2,10},{3,11},{4,12},{5,13},{6,14},{7,15},{8,0},{9,1},... | collective-permute-start | bytes 294920 | tf_op jit(solution)/shard_map/ppermute | solution.py:207
  158.1 6.4 %collective-permute-start.53 = (f32[32,512]{1,0:T(8,128)S(1)}, f32[32,512]{1,0:T(8,128)S(1)}, u32[]{:S(2)}, u32[]{:S(2)}) collective-permute-start(f32[32,512]{1,0:T(8,128)S(1)} %shard_map.247.refs_2_.refs_0_), channel_id=1, source_target_pairs={{0,16},{1,17},{2,18},{3,19},{4,20},{5,21},{6,22},{7,23},{8,24},{9,... | collective-permute-start | bytes 196616 | tf_op jit(solution)/shard_map/ppermute | solution.py:207
  158.7 22.9 %collective-permute-start.60 = (f32[384,512]{1,0:T(8,128)S(1)}, f32[384,512]{1,0:T(8,128)S(1)}, u32[]{:S(2)}, u32[]{:S(2)}) collective-permute-start(f32[384,512]{1,0:T(8,128)S(1)} %shard_map.248.refs_2_.refs_0_), channel_id=1, source_target_pairs={{0,2},{1,5},{2,0},{3,7},{4,6},{5,1},{6,4},{7,3},{8,10},{9,13},{10,... | collective-permute-start | bytes 2359304 | tf_op jit(solution)/shard_map/ppermute | solution.py:207
  167.1 7.6 %collective-permute-start.54 = (f32[128,512]{1,0:T(8,128)S(1)}, f32[128,512]{1,0:T(8,128)S(1)}, u32[]{:S(2)}, u32[]{:S(2)}) collective-permute-start(f32[128,512]{1,0:T(8,128)S(1)} %shard_map.252.refs_7_.refs_0_), channel_id=1, source_target_pairs={{0,4},{1,3},{2,6},{3,1},{4,0},{5,7},{6,2},{7,5},{8,12},{9,11},{10,... | collective-permute-start | bytes 786440 | tf_op jit(solution)/shard_map/ppermute | solution.py:207
  170.5 9.8 %collective-permute-start.61 = (f32[128,512]{1,0:T(8,128)S(1)}, f32[128,512]{1,0:T(8,128)S(1)}, u32[]{:S(2)}, u32[]{:S(2)}) collective-permute-start(f32[128,512]{1,0:T(8,128)S(1)} %shard_map.254.refs_2_.refs_0_), channel_id=1, source_target_pairs={{0,4},{1,3},{2,6},{3,1},{4,0},{5,7},{6,2},{7,5},{8,12},{9,11},{10,... | collective-permute-start | bytes 786440 | tf_op jit(solution)/shard_map/ppermute | solution.py:207
  174.7 11.5 %collective-permute-start.57 = (f32[256,512]{1,0:T(8,128)S(1)}, f32[256,512]{1,0:T(8,128)S(1)}, u32[]{:S(2)}, u32[]{:S(2)}) collective-permute-start(f32[256,512]{1,0:T(8,128)S(1)} %shard_map.256.refs_2_.refs_0_), channel_id=1, source_target_pairs={{0,2},{1,5},{2,0},{3,7},{4,6},{5,1},{6,4},{7,3},{8,10},{9,13},{10,... | collective-permute-start | bytes 1572872 | tf_op jit(solution)/shard_map/ppermute | solution.py:207
  178.7 6.5 %collective-permute-start.59 = (f32[64,512]{1,0:T(8,128)S(1)}, f32[64,512]{1,0:T(8,128)S(1)}, u32[]{:S(2)}, u32[]{:S(2)}) collective-permute-start(f32[64,512]{1,0:T(8,128)S(1)} %shard_map.257.refs_2_.refs_0_), channel_id=1, source_target_pairs={{0,4},{1,3},{2,6},{3,1},{4,0},{5,7},{6,2},{7,5},{8,12},{9,11},{10,... | collective-permute-start | bytes 393224 | tf_op jit(solution)/shard_map/ppermute | solution.py:207
  180.3 9.2 %collective-permute-start.63 = (f32[256,512]{1,0:T(8,128)S(1)}, f32[256,512]{1,0:T(8,128)S(1)}, u32[]{:S(2)}, u32[]{:S(2)}) collective-permute-start(f32[256,512]{1,0:T(8,128)S(1)} %shard_map.258.refs_2_.refs_0_), channel_id=1, source_target_pairs={{0,2},{1,5},{2,0},{3,7},{4,6},{5,1},{6,4},{7,3},{8,10},{9,13},{10,... | collective-permute-start | bytes 1572872 | tf_op jit(solution)/shard_map/ppermute | solution.py:207
  181.7 10.8 %collective-permute-start.67 = (f32[768,512]{1,0:T(8,128)S(1)}, f32[768,512]{1,0:T(8,128)S(1)}, u32[]{:S(2)}, u32[]{:S(2)}) collective-permute-start(f32[768,512]{1,0:T(8,128)S(1)} %shard_map.259.refs_2_.refs_0_), channel_id=1, source_target_pairs={{0,1},{1,0},{2,3},{3,2},{4,5},{5,4},{6,7},{7,6},{8,9},{9,8},{10,11... | collective-permute-start | bytes 4718600 | tf_op jit(solution)/shard_map/ppermute | solution.py:207
  185.3 7.1 %collective-permute-start.65 = (f32[128,512]{1,0:T(8,128)S(1)}, f32[128,512]{1,0:T(8,128)S(1)}, u32[]{:S(2)}, u32[]{:S(2)}) collective-permute-start(f32[128,512]{1,0:T(8,128)S(1)} %shard_map.260.refs_2_.refs_0_), channel_id=1, source_target_pairs={{0,2},{1,5},{2,0},{3,7},{4,6},{5,1},{6,4},{7,3},{8,10},{9,13},{10,... | collective-permute-start | bytes 786440 | tf_op jit(solution)/shard_map/ppermute | solution.py:207
  186.3 8.1 %collective-permute-start.62 = (f32[512,512]{1,0:T(8,128)S(1)}, f32[512,512]{1,0:T(8,128)S(1)}, u32[]{:S(2)}, u32[]{:S(2)}) collective-permute-start(f32[512,512]{1,0:T(8,128)S(1)} %shard_map.261.refs_11_.refs_0_), channel_id=1, source_target_pairs={{0,1},{1,0},{2,3},{3,2},{4,5},{5,4},{6,7},{7,6},{8,9},{9,8},{10,11... | collective-permute-start | bytes 3145736 | tf_op jit(solution)/shard_map/ppermute | solution.py:207
  (56 other events, 467.4 us)

commit v6 on v5

--- a/solution.py
+++ b/solution.py
@@ -980,8 +980,7 @@
         [dv1, dy1, x1, cotangent, stats1, bn_gain, bn_bias, w_in, skip],
         weight=1 << 20,
     )
-    step = top.send([sums])
-    (sums,) = run(join_body, [tile], [sums], [step], limit=4)
+    top.send([sums])
     sums = everywhere(sums)
     step = top.send([sums])
     d0, dz0, dy0, g0, grads1, part = run(

time: 197 us -> 197 us (level)
    pallas_call x61 -> x60, Pallas kernels: 30.2 us -> 30.2 us  [run(): pl.pallas_call(kernel, out_shape=[jax.ShapeDtypeStruct(shape, dtype) for...]
where the time goes in v6:
time: 197 us
  starting transfers between devices  63.4 us (32%)
  waiting for transfers between devices  56.1 us (28%)
  blocking collectives  38.1 us (19%)
  Pallas kernels  36.1 us (18%)
    all_to_all x3, blocking collectives, everywhere(): return lax.all_to_all(tiles, 'tm', 0, 0)  38.1 us
    ppermute x40, waiting for transfers between devices, with_partner(): lax.ppermute(value, 'tm', [(i, i ^ (odd if i & 1 else even)) for i in ran...  36.5 us
    ppermute x28, starting transfers between devices, swap(): lax.ppermute(value, 'tm', [(i, i ^ stride * mask) for i in range(count)])  32.5 us
    ppermute x40, starting transfers between devices, with_partner(): lax.ppermute(value, 'tm', [(i, i ^ (odd if i & 1 else even)) for i in ran...  30.8 us
    pallas_call x60, Pallas kernels, run(): pl.pallas_call(kernel, out_shape=[jax.ShapeDtypeStruct(shape, dtype) for...  30.2 us
    ppermute x28, waiting for transfers between devices, swap(): lax.ppermute(value, 'tm', [(i, i ^ stride * mask) for i in range(count)])  19.6 us
  transfers between devices with their start and end apart: 68, of which 46 were waited for; matrix products, arithmetic and copies ran while one was open for 0% of the time, Pallas kernels for 10%

profile of v6, /device:TPU:0, one launch (start us, length us, event | category | flops | bytes accessed | tf_op | source)
XLA Modules:
  0.0 196.8 jit_solution(17935320709855422740)
XLA Ops:
  0.7 1.9 shard_map.203
  2.6 15.3 %all_to_all.15.refs_1_ = f32[32,8,128]{2,1,0:T(8,128)S(1)} all-to-all(f32[32,8,128]{2,1,0:T(8,128)S(1)} %get-tuple-element.94), channel_id=1, replica_groups=mesh['tm'=32] {'tm'}, dimensions={0} | all-to-all | bytes 262144 | tf_op jit(solution)/shard_map/all_to_all | solution.py:105
  28.2 2.4 %collective-permute-start.4 = (f32[16,512]{1,0:T(8,128)S(1)}, f32[16,512]{1,0:T(8,128)S(1)}, u32[]{:S(2)}, u32[]{:S(2)}) collective-permute-start(f32[16,512]{1,0:T(8,128)S(1)} %shard_map.207.refs_6_), channel_id=1, source_target_pairs={{0,8},{1,9},{2,10},{3,11},{4,12},{5,13},{6,14},{7,15},{8,0},{9,1},... | collective-permute-start | bytes 98312 | tf_op jit(solution)/shard_map/ppermute | solution.py:70
  32.9 3.3 %shard_map.208 = (f32[1024,512]{1,0:T(8,128)S(1)}, bf16[1040,512]{1,0:T(8,128)(2,1)S(1)}, bf16[1024,512]{1,0:T(8,128)(2,1)S(1)}, bf16[1024,512]{1,0:T(8,128)(2,1...) custom-call(f32[16,512]{1,0:T(8,128)S(1)} %get-tuple-element.97.refs_2_.refs_0_, ...), custom_call_target="tpu_custom_call" | custom-call | flops 8589934592 | tf_op jit(solution)/shard_map/pallas_call | solution.py:40
  36.2 11.6 %all_to_all.16.refs_1_ = f32[32,8,128]{2,1,0:T(8,128)S(1)} all-to-all(f32[32,8,128]{2,1,0:T(8,128)S(1)} %get-tuple-element.104), channel_id=1, replica_groups=mesh['tm'=32] {'tm'}, dimensions={0} | all-to-all | bytes 262144 | tf_op jit(solution)/shard_map/all_to_all | solution.py:105
  58.0 2.5 %collective-permute-start.11 = (f32[16,512]{1,0:T(8,128)S(1)}, f32[16,512]{1,0:T(8,128)S(1)}, u32[]{:S(2)}, u32[]{:S(2)}) collective-permute-start(f32[16,512]{1,0:T(8,128)S(1)} %shard_map.211.refs_6_), channel_id=1, source_target_pairs={{0,8},{1,9},{2,10},{3,11},{4,12},{5,13},{6,14},{7,15},{8,0},{9,1},... | collective-permute-start | bytes 98312 | tf_op jit(solution)/shard_map/ppermute | solution.py:70
  62.8 6.3 %shard_map.212 = (f32[16,64,512]{2,1,0:T(8,128)}, bf16[1040,512]{1,0:T(8,128)(2,1)S(1)}, bf16[1024,512]{1,0:T(8,128)(2,1)S(1)}, bf16[1024,1024]{1,0:T(8,128)(2,1...) custom-call(f32[16,512]{1,0:T(8,128)S(1)} %get-tuple-element.106.refs_0_, ...), custom_call_target="tpu_custom_call" | custom-call | flops 8589934592 | tf_op jit(solution)/shard_map/pallas_call | solution.py:40
  69.0 1.9 shard_map.213
  71.6 1.7 collective-permute-start.17
  79.3 2.0 %collective-permute-start.20 = (f32[16,512]{1,0:T(8,128)S(1)}, f32[16,512]{1,0:T(8,128)S(1)}, u32[]{:S(2)}, u32[]{:S(2)}) collective-permute-start(f32[16,512]{1,0:T(8,128)S(1)} %shard_map.215.refs_2_.refs_6_), channel_id=1, source_target_pairs={{0,24},{1,25},{2,26},{3,27},{4,28},{5,29},{6,30},{7,31},{8,16},{9,... | collective-permute-start | bytes 98312 | tf_op jit(solution)/shard_map/ppermute | solution.py:70
  87.6 2.0 shard_map.218
  91.6 11.2 %all_to_all.17.refs_4_.refs_1_ = f32[32,8,128]{2,1,0:T(8,128)S(1)} all-to-all(f32[32,8,128]{2,1,0:T(8,128)S(1)} %get-tuple-element.121.refs_3_), channel_id=1, replica_groups=mesh['tm'=32] {'tm'}, dimensions={0} | all-to-all | bytes 262144 | tf_op jit(solution)/shard_map/all_to_all | solution.py:105
  103.6 2.4 %shard_map.221 = (f32[1024,512]{1,0:T(8,128)S(1)}, bf16[1024,1024]{1,0:T(8,128)(2,1)S(1)}, bf16[1024,512]{1,0:T(8,128)(2,1)S(1)}, f32[1024,512]{1,0:T(8,128)S(1)...) custom-call(s32[16,128]{1,0:T(8,128)S(1)} %get-tuple-element.93.refs_0_.refs_13_.refs_1_, ...), custom_call_target="tpu_custom_call" | custom-call | flops 8589934592 | tf_op jit(solution)/shard_map/pallas_call | solution.py:40
  108.2 1.8 collective-permute-start.27
  118.8 2.1 %collective-permute-done.29.refs_2_.refs_7_ = f32[16,512]{1,0:T(8,128)S(1)} collective-permute-done((f32[16,512]{1,0:T(8,128)S(1)}, f32[16,512]{1,0:T(8,128)S(1)}, u32[]{:S(2)}, u32[]{:S(2)}) %collective-permute-start.29) | collective-permute-done | bytes 32800 | tf_op jit(solution)/shard_map/ppermute | solution.py:70
  126.5 3.5 %collective-permute-done.35.refs_2_ = f32[256,512]{1,0:T(8,128)S(1)} collective-permute-done((f32[256,512]{1,0:T(8,128)S(1)}, f32[256,512]{1,0:T(8,128)S(1)}, u32[]{:S(2)}, u32[]{:S(2)}) %collective-permute-start.35) | collective-permute-done | bytes 524320 | tf_op jit(solution)/shard_map/ppermute | solution.py:207
  130.2 1.8 collective-permute-start.38
  134.1 2.7 %collective-permute-done.38.refs_1_ = f32[48,512]{1,0:T(8,128)S(1)} collective-permute-done((f32[48,512]{1,0:T(8,128)S(1)}, f32[48,512]{1,0:T(8,128)S(1)}, u32[]{:S(2)}, u32[]{:S(2)}) %collective-permute-start.38) | collective-permute-done | bytes 98336 | tf_op jit(solution)/shard_map/ppermute | solution.py:207
  137.3 2.1 %collective-permute-done.37.refs_2_ = f32[256,512]{1,0:T(8,128)S(1)} collective-permute-done((f32[256,512]{1,0:T(8,128)S(1)}, f32[256,512]{1,0:T(8,128)S(1)}, u32[]{:S(2)}, u32[]{:S(2)}) %collective-permute-start.37) | collective-permute-done | bytes 524320 | tf_op jit(solution)/shard_map/ppermute | solution.py:207
  139.5 1.8 collective-permute-start.43
  142.9 3.0 %collective-permute-done.43.refs_3_ = f32[128,512]{1,0:T(8,128)S(1)} collective-permute-done((f32[128,512]{1,0:T(8,128)S(1)}, f32[128,512]{1,0:T(8,128)S(1)}, u32[]{:S(2)}, u32[]{:S(2)}) %collective-permute-start.43) | collective-permute-done | bytes 262176 | tf_op jit(solution)/shard_map/ppermute | solution.py:207
  147.2 2.0 %collective-permute-start.49 = (f32[192,512]{1,0:T(8,128)S(1)}, f32[192,512]{1,0:T(8,128)S(1)}, u32[]{:S(2)}, u32[]{:S(2)}) collective-permute-start(f32[192,512]{1,0:T(8,128)S(1)} %shard_map.240.refs_5_.refs_0_), channel_id=1, source_target_pairs={{0,4},{1,3},{2,6},{3,1},{4,0},{5,7},{6,2},{7,5},{8,12},{9,11},{10,... | collective-permute-start | bytes 1179656 | tf_op jit(solution)/shard_map/ppermute | solution.py:207
  152.5 2.6 %collective-permute-done.45.refs_5_ = f32[32,512]{1,0:T(8,128)S(1)} collective-permute-done((f32[32,512]{1,0:T(8,128)S(1)}, f32[32,512]{1,0:T(8,128)S(1)}, u32[]{:S(2)}, u32[]{:S(2)}) %collective-permute-start.45) | collective-permute-done | bytes 65568 | tf_op jit(solution)/shard_map/ppermute | solution.py:207
  161.6 1.9 collective-permute-done.47.refs_4_
  164.5 1.8 collective-permute-start.56
  170.4 1.9 collective-permute-start.61
  172.4 2.0 %collective-permute-done.55.refs_1_ = f32[16,512]{1,0:T(8,128)S(1)} collective-permute-done((f32[16,512]{1,0:T(8,128)S(1)}, f32[16,512]{1,0:T(8,128)S(1)}, u32[]{:S(2)}, u32[]{:S(2)}) %collective-permute-start.55) | collective-permute-done | bytes 32800 | tf_op jit(solution)/shard_map/ppermute | solution.py:207
  176.0 2.7 %collective-permute-done.58.refs_1_ = f32[32,512]{1,0:T(8,128)S(1)} collective-permute-done((f32[32,512]{1,0:T(8,128)S(1)}, f32[32,512]{1,0:T(8,128)S(1)}, u32[]{:S(2)}, u32[]{:S(2)}) %collective-permute-start.58) | collective-permute-done | bytes 65568 | tf_op jit(solution)/shard_map/ppermute | solution.py:207
  181.8 3.4 %collective-permute-done.59.refs_1_ = f32[64,512]{1,0:T(8,128)S(1)} collective-permute-done((f32[64,512]{1,0:T(8,128)S(1)}, f32[64,512]{1,0:T(8,128)S(1)}, u32[]{:S(2)}, u32[]{:S(2)}) %collective-permute-start.59) | collective-permute-done | bytes 131104 | tf_op jit(solution)/shard_map/ppermute | solution.py:207
  186.4 2.7 %shard_map.261 = (f32[16,64,512]{2,1,0:T(8,128)}, f32[2,512]{1,0:T(2,128)}, f32[2,512]{1,0:T(2,128)}, f32[2,256]{1,0:T(2,128)}, f32[2,256]{1,0:T(2,128)}, /*index=5*/f32[2,512]{1,0:T(2,128)}, f32[2,2,512]{2,1,0:T(2,128)}) custom-call(f32[32,512]{1,0:T(8,128)S(1)} %shard_map.252.refs_2_.refs_0_, s32[16,128]{1,0:T(8,128)S(1)} %get-tuple-element.93.refs_0_.refs_13_.refs_1_, ...), custom_call_target="tpu_custom_call" | custom-call | flops 8589934592 | tf_op jit(solution)/shard_map/pallas_call | solution.py:40
  190.4 2.0 %collective-permute-done.65.refs_1_ = f32[128,512]{1,0:T(8,128)S(1)} collective-permute-done((f32[128,512]{1,0:T(8,128)S(1)}, f32[128,512]{1,0:T(8,128)S(1)}, u32[]{:S(2)}, u32[]{:S(2)}) %collective-permute-start.65) | collective-permute-done | bytes 262176 | tf_op jit(solution)/shard_map/ppermute | solution.py:207
  194.4 2.3 %shard_map.265 = (f32[2,512,1024]{2,1,0:T(8,128)}, f32[2,512,512]{2,1,0:T(8,128)}, f32[2,512,512]{2,1,0:T(8,128)}) custom-call(f32[512,512]{1,0:T(8,128)S(1)} %shard_map.260.refs_11_.refs_0_, f32[512,512]{1,0:T(8,128)S(1)} %collective-permute-done.62.refs_1_, f32[512,512]{1,0:T(8,128)S(1)} %shard_map.262.refs_2_, ...), custom_call_target="tpu_custom_call", output_to_operand_aliasing={{0}: (6, {}), {1}: (7, {})} | custom-call | tf_op jit(solution)/shard_map/pallas_call | solution.py:419
  (211 shorter events, 86.8 us)
Async XLA Ops:
  71.0 7.7 %collective-permute-start.21 = (f32[768,512]{1,0:T(8,128)S(1)}, f32[768,512]{1,0:T(8,128)S(1)}, u32[]{:S(2)}, u32[]{:S(2)}) collective-permute-start(f32[768,512]{1,0:T(8,128)S(1)} %get-tuple-element.119), channel_id=1, source_target_pairs={{0,1},{1,0},{2,3},{3,2},{4,5},{5,4},{6,7},{7,6},{8,9},{9,8},{10,11... | collective-permute-start | bytes 4718600 | tf_op jit(solution)/shard_map/ppermute | solution.py:207
  78.7 12.1 %collective-permute-start.22 = (f32[384,512]{1,0:T(8,128)S(1)}, f32[384,512]{1,0:T(8,128)S(1)}, u32[]{:S(2)}, u32[]{:S(2)}) collective-permute-start(f32[384,512]{1,0:T(8,128)S(1)} %shard_map.216.refs_18_), channel_id=1, source_target_pairs={{0,2},{1,5},{2,0},{3,7},{4,6},{5,1},{6,4},{7,3},{8,10},{9,13},{10,... | collective-permute-start | bytes 2359304 | tf_op jit(solution)/shard_map/ppermute | solution.py:207
  90.9 11.9 %collective-permute-start.23 = (f32[192,512]{1,0:T(8,128)S(1)}, f32[192,512]{1,0:T(8,128)S(1)}, u32[]{:S(2)}, u32[]{:S(2)}) collective-permute-start(f32[192,512]{1,0:T(8,128)S(1)} %shard_map.219), channel_id=1, source_target_pairs={{0,4},{1,3},{2,6},{3,1},{4,0},{5,7},{6,2},{7,5},{8,12},{9,11},{10,... | collective-permute-start | bytes 1179656 | tf_op jit(solution)/shard_map/ppermute | solution.py:207
  102.9 10.1 %collective-permute-start.28 = (f32[96,512]{1,0:T(8,128)S(1)}, f32[96,512]{1,0:T(8,128)S(1)}, u32[]{:S(2)}, u32[]{:S(2)}) collective-permute-start(f32[96,512]{1,0:T(8,128)S(1)} %shard_map.220.refs_13_), channel_id=1, source_target_pairs={{0,8},{1,9},{2,10},{3,11},{4,12},{5,13},{6,14},{7,15},{8,0},{9,1},... | collective-permute-start | bytes 589832 | tf_op jit(solution)/shard_map/ppermute | solution.py:207
  107.9 10.5 %collective-permute-start.32 = (f32[512,512]{1,0:T(8,128)S(1)}, f32[512,512]{1,0:T(8,128)S(1)}, u32[]{:S(2)}, u32[]{:S(2)}) collective-permute-start(f32[512,512]{1,0:T(8,128)S(1)} %get-tuple-element.139), channel_id=1, source_target_pairs={{0,1},{1,0},{2,3},{3,2},{4,5},{5,4},{6,7},{7,6},{8,9},{9,8},{10,11... | collective-permute-start | bytes 3145736 | tf_op jit(solution)/shard_map/ppermute | solution.py:207
  112.9 9.0 %collective-permute-start.33 = (f32[512,512]{1,0:T(8,128)S(1)}, f32[512,512]{1,0:T(8,128)S(1)}, u32[]{:S(2)}, u32[]{:S(2)}) collective-permute-start(f32[512,512]{1,0:T(8,128)S(1)} %get-tuple-element.141), channel_id=1, source_target_pairs={{0,1},{1,0},{2,3},{3,2},{4,5},{5,4},{6,7},{7,6},{8,9},{9,8},{10,11... | collective-permute-start | bytes 3145736 | tf_op jit(solution)/shard_map/ppermute | solution.py:207
  113.9 9.1 %collective-permute-start.31 = (f32[16,512]{1,0:T(8,128)S(1)}, f32[16,512]{1,0:T(8,128)S(1)}, u32[]{:S(2)}, u32[]{:S(2)}) collective-permute-start(f32[16,512]{1,0:T(8,128)S(1)} %shard_map.226.refs_2_.refs_6_), channel_id=1, source_target_pairs={{0,24},{1,25},{2,26},{3,27},{4,28},{5,29},{6,30},{7,31},{8,16},{9,... | collective-permute-start | bytes 98312 | tf_op jit(solution)/shard_map/ppermute | solution.py:70
  115.5 7.5 %collective-permute-start.30 = (f32[16,512]{1,0:T(8,128)S(1)}, f32[16,512]{1,0:T(8,128)S(1)}, u32[]{:S(2)}, u32[]{:S(2)}) collective-permute-start(f32[16,512]{1,0:T(8,128)S(1)} %shard_map.226.refs_2_.refs_6_), channel_id=1, source_target_pairs={{0,16},{1,17},{2,18},{3,19},{4,20},{5,21},{6,22},{7,23},{8,24},{9,... | collective-permute-start | bytes 98312 | tf_op jit(solution)/shard_map/ppermute | solution.py:70
  118.4 11.7 %collective-permute-start.34 = (f32[48,512]{1,0:T(8,128)S(1)}, f32[48,512]{1,0:T(8,128)S(1)}, u32[]{:S(2)}, u32[]{:S(2)}) collective-permute-start(f32[48,512]{1,0:T(8,128)S(1)} %shard_map.224.refs_5_), channel_id=1, source_target_pairs={{0,16},{1,17},{2,18},{3,19},{4,20},{5,21},{6,22},{7,23},{8,24},{9,... | collective-permute-start | bytes 294920 | tf_op jit(solution)/shard_map/ppermute | solution.py:207
  120.9 9.2 %collective-permute-start.35 = (f32[256,512]{1,0:T(8,128)S(1)}, f32[256,512]{1,0:T(8,128)S(1)}, u32[]{:S(2)}, u32[]{:S(2)}) collective-permute-start(f32[256,512]{1,0:T(8,128)S(1)} %shard_map.227.refs_18_), channel_id=1, source_target_pairs={{0,2},{1,5},{2,0},{3,7},{4,6},{5,1},{6,4},{7,3},{8,10},{9,13},{10,... | collective-permute-start | bytes 1572872 | tf_op jit(solution)/shard_map/ppermute | solution.py:207
  122.0 17.5 %collective-permute-start.37 = (f32[256,512]{1,0:T(8,128)S(1)}, f32[256,512]{1,0:T(8,128)S(1)}, u32[]{:S(2)}, u32[]{:S(2)}) collective-permute-start(f32[256,512]{1,0:T(8,128)S(1)} %shard_map.228.refs_19_), channel_id=1, source_target_pairs={{0,2},{1,5},{2,0},{3,7},{4,6},{5,1},{6,4},{7,3},{8,10},{9,13},{10,... | collective-permute-start | bytes 1572872 | tf_op jit(solution)/shard_map/ppermute | solution.py:207
  130.2 6.6 %collective-permute-start.38 = (f32[48,512]{1,0:T(8,128)S(1)}, f32[48,512]{1,0:T(8,128)S(1)}, u32[]{:S(2)}, u32[]{:S(2)}) collective-permute-start(f32[48,512]{1,0:T(8,128)S(1)} %shard_map.233.refs_3_.refs_0_), channel_id=1, source_target_pairs={{0,16},{1,17},{2,18},{3,19},{4,20},{5,21},{6,22},{7,23},{8,24},{9,... | collective-permute-start | bytes 294920 | tf_op jit(solution)/shard_map/ppermute | solution.py:207
  132.0 9.8 %collective-permute-start.40 = (f32[128,512]{1,0:T(8,128)S(1)}, f32[128,512]{1,0:T(8,128)S(1)}, u32[]{:S(2)}, u32[]{:S(2)}) collective-permute-start(f32[128,512]{1,0:T(8,128)S(1)} %shard_map.232.refs_6_), channel_id=1, source_target_pairs={{0,4},{1,3},{2,6},{3,1},{4,0},{5,7},{6,2},{7,5},{8,12},{9,11},{10,... | collective-permute-start | bytes 786440 | tf_op jit(solution)/shard_map/ppermute | solution.py:207
  134.0 7.2 %collective-permute-start.36 = (f32[272,512]{1,0:T(8,128)S(1)}, f32[272,512]{1,0:T(8,128)S(1)}, u32[]{:S(2)}, u32[]{:S(2)}) collective-permute-start(f32[272,512]{1,0:T(8,128)S(1)} %get-tuple-element.152.refs_2_), channel_id=1, source_target_pairs={{0,1},{1,0},{2,3},{3,2},{4,5},{5,4},{6,7},{7,6},{8,9},{9,8},{10,11... | collective-permute-start | bytes 1671176 | tf_op jit(solution)/shard_map/ppermute | solution.py:207
  136.8 10.3 %collective-permute-start.42 = (f32[96,512]{1,0:T(8,128)S(1)}, f32[96,512]{1,0:T(8,128)S(1)}, u32[]{:S(2)}, u32[]{:S(2)}) collective-permute-start(f32[96,512]{1,0:T(8,128)S(1)} %shard_map.235.refs_3_.refs_0_), channel_id=1, source_target_pairs={{0,8},{1,9},{2,10},{3,11},{4,12},{5,13},{6,14},{7,15},{8,0},{9,1},... | collective-permute-start | bytes 589832 | tf_op jit(solution)/shard_map/ppermute | solution.py:207
  139.5 6.4 %collective-permute-start.43 = (f32[128,512]{1,0:T(8,128)S(1)}, f32[128,512]{1,0:T(8,128)S(1)}, u32[]{:S(2)}, u32[]{:S(2)}) collective-permute-start(f32[128,512]{1,0:T(8,128)S(1)} %shard_map.236.refs_3_), channel_id=1, source_target_pairs={{0,4},{1,3},{2,6},{3,1},{4,0},{5,7},{6,2},{7,5},{8,12},{9,11},{10,... | collective-permute-start | bytes 786440 | tf_op jit(solution)/shard_map/ppermute | solution.py:207
  141.3 9.6 %collective-permute-start.39 = (f32[144,512]{1,0:T(8,128)S(1)}, f32[144,512]{1,0:T(8,128)S(1)}, u32[]{:S(2)}, u32[]{:S(2)}) collective-permute-start(f32[144,512]{1,0:T(8,128)S(1)} %shard_map.237.refs_4_.refs_3_), channel_id=1, source_target_pairs={{0,2},{1,5},{2,0},{3,7},{4,6},{5,1},{6,4},{7,3},{8,10},{9,13},{10,... | collective-permute-start | bytes 884744 | tf_op jit(solution)/shard_map/ppermute | solution.py:207
  141.8 7.4 %collective-permute-start.41 = (f32[64,512]{1,0:T(8,128)S(1)}, f32[64,512]{1,0:T(8,128)S(1)}, u32[]{:S(2)}, u32[]{:S(2)}) collective-permute-start(f32[64,512]{1,0:T(8,128)S(1)} %shard_map.238.refs_4_), channel_id=1, source_target_pairs={{0,8},{1,9},{2,10},{3,11},{4,12},{5,13},{6,14},{7,15},{8,0},{9,1},... | collective-permute-start | bytes 393224 | tf_op jit(solution)/shard_map/ppermute | solution.py:207
  147.2 11.4 %collective-permute-start.49 = (f32[192,512]{1,0:T(8,128)S(1)}, f32[192,512]{1,0:T(8,128)S(1)}, u32[]{:S(2)}, u32[]{:S(2)}) collective-permute-start(f32[192,512]{1,0:T(8,128)S(1)} %shard_map.240.refs_5_.refs_0_), channel_id=1, source_target_pairs={{0,4},{1,3},{2,6},{3,1},{4,0},{5,7},{6,2},{7,5},{8,12},{9,11},{10,... | collective-permute-start | bytes 1179656 | tf_op jit(solution)/shard_map/ppermute | solution.py:207
  151.6 6.5 %collective-permute-start.50 = (f32[32,512]{1,0:T(8,128)S(1)}, f32[32,512]{1,0:T(8,128)S(1)}, u32[]{:S(2)}, u32[]{:S(2)}) collective-permute-start(f32[32,512]{1,0:T(8,128)S(1)} %shard_map.243.refs_6_), channel_id=1, source_target_pairs={{0,16},{1,17},{2,18},{3,19},{4,20},{5,21},{6,22},{7,23},{8,24},{9,... | collective-permute-start | bytes 196616 | tf_op jit(solution)/shard_map/ppermute | solution.py:207
  155.1 6.4 %collective-permute-start.48 = (f32[32,512]{1,0:T(8,128)S(1)}, f32[32,512]{1,0:T(8,128)S(1)}, u32[]{:S(2)}, u32[]{:S(2)}) collective-permute-start(f32[32,512]{1,0:T(8,128)S(1)} %shard_map.244.refs_5_.refs_0_), channel_id=1, source_target_pairs={{0,16},{1,17},{2,18},{3,19},{4,20},{5,21},{6,22},{7,23},{8,24},{9,... | collective-permute-start | bytes 196616 | tf_op jit(solution)/shard_map/ppermute | solution.py:207
  156.8 6.7 %collective-permute-start.47 = (f32[48,512]{1,0:T(8,128)S(1)}, f32[48,512]{1,0:T(8,128)S(1)}, u32[]{:S(2)}, u32[]{:S(2)}) collective-permute-start(f32[48,512]{1,0:T(8,128)S(1)} %shard_map.245.refs_6_.refs_5_), channel_id=1, source_target_pairs={{0,8},{1,9},{2,10},{3,11},{4,12},{5,13},{6,14},{7,15},{8,0},{9,1},... | collective-permute-start | bytes 294920 | tf_op jit(solution)/shard_map/ppermute | solution.py:207
  158.1 6.4 %collective-permute-start.53 = (f32[32,512]{1,0:T(8,128)S(1)}, f32[32,512]{1,0:T(8,128)S(1)}, u32[]{:S(2)}, u32[]{:S(2)}) collective-permute-start(f32[32,512]{1,0:T(8,128)S(1)} %shard_map.246.refs_2_.refs_0_), channel_id=1, source_target_pairs={{0,16},{1,17},{2,18},{3,19},{4,20},{5,21},{6,22},{7,23},{8,24},{9,... | collective-permute-start | bytes 196616 | tf_op jit(solution)/shard_map/ppermute | solution.py:207
  158.7 22.9 %collective-permute-start.60 = (f32[384,512]{1,0:T(8,128)S(1)}, f32[384,512]{1,0:T(8,128)S(1)}, u32[]{:S(2)}, u32[]{:S(2)}) collective-permute-start(f32[384,512]{1,0:T(8,128)S(1)} %shard_map.247.refs_2_.refs_0_), channel_id=1, source_target_pairs={{0,2},{1,5},{2,0},{3,7},{4,6},{5,1},{6,4},{7,3},{8,10},{9,13},{10,... | collective-permute-start | bytes 2359304 | tf_op jit(solution)/shard_map/ppermute | solution.py:207
  167.0 7.6 %collective-permute-start.54 = (f32[128,512]{1,0:T(8,128)S(1)}, f32[128,512]{1,0:T(8,128)S(1)}, u32[]{:S(2)}, u32[]{:S(2)}) collective-permute-start(f32[128,512]{1,0:T(8,128)S(1)} %shard_map.251.refs_7_.refs_0_), channel_id=1, source_target_pairs={{0,4},{1,3},{2,6},{3,1},{4,0},{5,7},{6,2},{7,5},{8,12},{9,11},{10,... | collective-permute-start | bytes 786440 | tf_op jit(solution)/shard_map/ppermute | solution.py:207
  170.4 9.8 %collective-permute-start.61 = (f32[128,512]{1,0:T(8,128)S(1)}, f32[128,512]{1,0:T(8,128)S(1)}, u32[]{:S(2)}, u32[]{:S(2)}) collective-permute-start(f32[128,512]{1,0:T(8,128)S(1)} %shard_map.253.refs_2_.refs_0_), channel_id=1, source_target_pairs={{0,4},{1,3},{2,6},{3,1},{4,0},{5,7},{6,2},{7,5},{8,12},{9,11},{10,... | collective-permute-start | bytes 786440 | tf_op jit(solution)/shard_map/ppermute | solution.py:207
  174.7 11.5 %collective-permute-start.57 = (f32[256,512]{1,0:T(8,128)S(1)}, f32[256,512]{1,0:T(8,128)S(1)}, u32[]{:S(2)}, u32[]{:S(2)}) collective-permute-start(f32[256,512]{1,0:T(8,128)S(1)} %shard_map.255.refs_2_.refs_0_), channel_id=1, source_target_pairs={{0,2},{1,5},{2,0},{3,7},{4,6},{5,1},{6,4},{7,3},{8,10},{9,13},{10,... | collective-permute-start | bytes 1572872 | tf_op jit(solution)/shard_map/ppermute | solution.py:207
  178.7 6.5 %collective-permute-start.59 = (f32[64,512]{1,0:T(8,128)S(1)}, f32[64,512]{1,0:T(8,128)S(1)}, u32[]{:S(2)}, u32[]{:S(2)}) collective-permute-start(f32[64,512]{1,0:T(8,128)S(1)} %shard_map.256.refs_2_.refs_0_), channel_id=1, source_target_pairs={{0,4},{1,3},{2,6},{3,1},{4,0},{5,7},{6,2},{7,5},{8,12},{9,11},{10,... | collective-permute-start | bytes 393224 | tf_op jit(solution)/shard_map/ppermute | solution.py:207
  180.3 9.2 %collective-permute-start.63 = (f32[256,512]{1,0:T(8,128)S(1)}, f32[256,512]{1,0:T(8,128)S(1)}, u32[]{:S(2)}, u32[]{:S(2)}) collective-permute-start(f32[256,512]{1,0:T(8,128)S(1)} %shard_map.257.refs_2_.refs_0_), channel_id=1, source_target_pairs={{0,2},{1,5},{2,0},{3,7},{4,6},{5,1},{6,4},{7,3},{8,10},{9,13},{10,... | collective-permute-start | bytes 1572872 | tf_op jit(solution)/shard_map/ppermute | solution.py:207
  181.7 10.7 %collective-permute-start.67 = (f32[768,512]{1,0:T(8,128)S(1)}, f32[768,512]{1,0:T(8,128)S(1)}, u32[]{:S(2)}, u32[]{:S(2)}) collective-permute-start(f32[768,512]{1,0:T(8,128)S(1)} %shard_map.258.refs_2_.refs_0_), channel_id=1, source_target_pairs={{0,1},{1,0},{2,3},{3,2},{4,5},{5,4},{6,7},{7,6},{8,9},{9,8},{10,11... | collective-permute-start | bytes 4718600 | tf_op jit(solution)/shard_map/ppermute | solution.py:207
  185.3 7.1 %collective-permute-start.65 = (f32[128,512]{1,0:T(8,128)S(1)}, f32[128,512]{1,0:T(8,128)S(1)}, u32[]{:S(2)}, u32[]{:S(2)}) collective-permute-start(f32[128,512]{1,0:T(8,128)S(1)} %shard_map.259.refs_2_.refs_0_), channel_id=1, source_target_pairs={{0,2},{1,5},{2,0},{3,7},{4,6},{5,1},{6,4},{7,3},{8,10},{9,13},{10,... | collective-permute-start | bytes 786440 | tf_op jit(solution)/shard_map/ppermute | solution.py:207
  186.2 8.1 %collective-permute-start.62 = (f32[512,512]{1,0:T(8,128)S(1)}, f32[512,512]{1,0:T(8,128)S(1)}, u32[]{:S(2)}, u32[]{:S(2)}) collective-permute-start(f32[512,512]{1,0:T(8,128)S(1)} %shard_map.260.refs_11_.refs_0_), channel_id=1, source_target_pairs={{0,1},{1,0},{2,3},{3,2},{4,5},{5,4},{6,7},{7,6},{8,9},{9,8},{10,11... | collective-permute-start | bytes 3145736 | tf_op jit(solution)/shard_map/ppermute | solution.py:207
  (56 other events, 467.2 us)
